TPU v7x, 512 devices: a whole 4x8x8 slice. The times are simulated.
512 devices in a mesh: space: 128 (over z, y, core), snap: 4 (over x).
Axes of the slice: x: 4, y: 8, z: 8, core: 2. Of those that a mesh axis runs over, the one named last changes fastest.
Arguments:
- direct_snaps: bfloat16 [256, 3, 512, 8, 128], P('snap', None, 'space'), may hold values from -24 to 24
- adjoint_snaps: bfloat16 [256, 3, 512, 8, 128], P('snap', None, 'space'), may hold values from -6 to 6
- left_factor: float32 [256, 64], replicated, may hold values from -0.375 to 0.375
- right_factor: float32 [256, 64], replicated, may hold values from -0.375 to 0.375
- singular: float32 [64], replicated, may hold values from 1 to 100
- term_coeff: float32 [16, 512, 8, 128], P(None, 'space'), may hold values from -6 to 6
- term_slot: int32 [16], replicated, may hold values from 0 to 15, each once
Outputs:
- cross_gram: float32 [256, 256], P('snap', 'space')
- reduced_ops: float32 [1024, 64], P('space', 'snap')
Inputs may be any that keep to these rules, and one draw needn't show every extreme that they name: term_slot is a permutation: each of the 16 slots holds the operator of exactly one term.
All inputs are finite; a program needn't handle non-finite values.
Results may differ from a plain program's by a relative error of at most 0.00105.
The roundings to bfloat16 on the way count: a program that leaves them out, or rounds other values in their place, can miss the bound.
Values may be sent and summed in bfloat16 or wider, within the bound.
No kernel may reach another device: no remote copies, remote signals or barrier semaphores. Data moves between devices by JAX's collectives and lax.ppermute only.
A program may use at most 128 MiB of HBM per device.

v0:
```python
import math

import jax
import jax.numpy as jnp
from jax import lax
from jax.sharding import PartitionSpec as P

stencil_kind = (4, 4, 4, 1, 2, 3, 1, 2, 3, 1, 2, 3, 0, 0, 0, 0)
source_comp = (0, 1, 2, 0, 0, 0, 1, 1, 1, 2, 2, 2, 0, 1, 2, 1)
target_comp = (0, 1, 2, 0, 0, 0, 1, 1, 1, 2, 2, 2, 1, 2, 0, 0)


def padded_2(array, sides, width):
    for axis, dim in sides:
        devices, length = (lax.axis_size(axis), array.shape[dim])
        up = [(i, (i + 1) % devices) for i in range(devices - 1)]
        down = [(j, i) for i, j in up]
        last = lax.slice_in_dim(array, length - width, length, axis=dim)
        leading = lax.slice_in_dim(array, 0, width, axis=dim)
        before = lax.ppermute(last, axis, up)
        after = lax.ppermute(leading, axis, down)
        array = jnp.concatenate([before, array, after], axis=dim)
    return array


def apply_stencil(padded, kind):
    center = padded[..., 1:-1, 1:-1, 1:-1]
    if kind == 0:
        return center
    if kind == 1:
        return 0.5 * (padded[..., 2:, 1:-1, 1:-1] - padded[..., :-2, 1:-1, 1:-1])
    if kind == 2:
        return 0.5 * (padded[..., 1:-1, 2:, 1:-1] - padded[..., 1:-1, :-2, 1:-1])
    if kind == 3:
        return 0.5 * (padded[..., 1:-1, 1:-1, 2:] - padded[..., 1:-1, 1:-1, :-2])
    beside_all = padded[..., 2:, 1:-1, 1:-1] + padded[..., :-2, 1:-1, 1:-1]
    beside_all = beside_all + padded[..., 1:-1, 2:, 1:-1] + padded[..., 1:-1, :-2, 1:-1]
    beside_all = beside_all + padded[..., 1:-1, 1:-1, 2:] + padded[..., 1:-1, 1:-1, :-2]
    return beside_all - 6.0 * center


def mode_weight(factor, singular):
    return (factor / jnp.sqrt(singular)[None, :]).astype(jnp.bfloat16)


def shards(direct_snaps, adjoint_snaps, left_factor, right_factor, singular, term_coeff, term_slot):
    snap_count = lax.axis_size("snap")
    space_count = lax.axis_size("space")
    snap_index = lax.axis_index("snap")
    cols_local, components, width_x, width_y, width_z = direct_snaps.shape
    mode_total = right_factor.shape[1]
    mode_local = mode_total // snap_count
    cell_count = width_x * width_y * width_z
    state_local = components * cell_count
    norm_scale = 1.0 / math.sqrt(state_local * space_count)
    contract_state = (((1,), (1,)), ((), ()))
    contract_lead = (((0,), (0,)), ((), ()))
    flat_adjoint = adjoint_snaps.reshape(cols_local, state_local)
    direct_weight = mode_weight(right_factor, singular)
    adjoint_weight = mode_weight(left_factor, singular)
    own_modes = lax.dynamic_slice_in_dim(direct_weight, snap_index * mode_local, mode_local, 1)
    mode_count = own_modes.shape[1]
    portion = lax.all_gather(direct_snaps, "snap", axis=0, tiled=True)
    length = portion.shape[0]
    portion_rows = portion.reshape(length, state_local)
    gram_block = lax.dot_general(
        flat_adjoint, portion_rows, contract_state, preferred_element_type=jnp.float32
    )
    gram_part = gram_block
    mode_part = lax.dot_general(
        own_modes, portion_rows, contract_lead, preferred_element_type=jnp.float32
    )
    gram_part, mode_part = (gram_part, mode_part)
    gram_part = gram_part * norm_scale
    direct_modes = mode_part.astype(jnp.bfloat16).reshape(
        mode_count, components, width_x, width_y, width_z
    )
    adjoint_cells = None
    own_rows = lax.dynamic_slice_in_dim(adjoint_weight, snap_index * cols_local, cols_local, 0)
    adjoint_cells = lax.psum(
        lax.dot_general(own_rows, flat_adjoint, contract_lead, preferred_element_type=jnp.float32),
        "snap",
    ).reshape(mode_total, components, cell_count)
    faces = padded_2(direct_modes, (("space", 2),), 1)
    padded = jnp.pad(faces, ((0, 0), (0, 0), (0, 0), (1, 1), (1, 1))).astype(jnp.float32)
    term_total = len(stencil_kind)
    operator_parts = [None] * term_total
    for target in range(components):
        members = [
            term_index for term_index in range(term_total) if target_comp[term_index] == target
        ]
        weighted = []
        for term_index in members:
            shaped = (
                apply_stencil(padded[:, source_comp[term_index]], stencil_kind[term_index])
                * term_coeff[term_index][None]
            )
            weighted.append(shaped.astype(jnp.bfloat16).reshape(mode_count, cell_count))
        stacked = jnp.stack(weighted)
        products = lax.dot_general(
            adjoint_cells[:, target],
            stacked.astype(jnp.float32),
            (((1,), (2,)), ((), ())),
            precision=lax.Precision.HIGHEST,
            preferred_element_type=jnp.float32,
        )
        for position, term_index in enumerate(members):
            operator_parts[term_index] = products[:, position]
    operators = jnp.stack(operator_parts) * norm_scale
    selector = (term_slot[None, :] == jnp.arange(term_total, dtype=jnp.int32)[:, None]).astype(
        jnp.float32
    )
    ordered = jnp.einsum("kq,qij->kij", selector, operators, precision=lax.Precision.HIGHEST)
    operator_block = ordered.reshape(term_total * mode_total, mode_count)
    cross_gram = lax.psum_scatter(gram_part, "space", scatter_dimension=1, tiled=True)
    reduced_ops = lax.psum_scatter(operator_block, "space", scatter_dimension=0, tiled=True)
    return (cross_gram, reduced_ops)


def solution(mesh):
    return jax.shard_map(
        shards,
        mesh=mesh,
        in_specs=(
            P("snap", None, "space", None, None),
            P("snap", None, "space", None, None),
            P(),
            P(),
            P(),
            P(None, "space", None, None),
            P(),
        ),
        out_specs=(P("snap", "space"), P("space", "snap")),
        check_vma=False,
    )
```

profile of v0, /device:TPU:1, one launch (start us, length us, event | category | flops | bytes accessed | tf_op | source)
XLA Modules:
  0.0 433.9 jit_solution(3282626228920657524)
XLA Ops:
  7.2 3.3 copy.38
  11.3 1.9 copy.81
  14.2 73.0 %all-gather.2.cloned.1.call-done = bf16[256,3,4,8,128]{4,0,3,2,1:T(8,128)(2,1)} async-done(((bf16[64,3,4,8,128]{4,0,3,2,1:T(8,128)(2,1)}), bf16[256,3,4,8,128]{4,0,3,2,1:T(8,128)(2,1)}) %all-gather.2.cloned.1.call-update) | async-done | bytes 6291472 | tf_op jit(solution)/shard_map/all_gather | solution.py:63
  87.2 8.6 %copy.41 = bf16[256,3,4,8,128]{0,4,3,2,1:T(8,128)(2,1)} copy(bf16[256,3,4,8,128]{4,0,3,2,1:T(8,128)(2,1)} %all-gather.2.cloned.1.call-done) | data formatting | bytes 12582912 | tf_op jit(solution)/shard_map/all_gather | solution.py:63
  95.8 4.7 %fusion.12 = bf16[2,8,96,128]{3,1,2,0:T(8,128)(2,1)S(1)} fusion(bf16[256,12288]{0,1:T(8,128)(2,1)} %bitcast.176, f32[256,64]{0,1:T(8,128)} %param.10, s32[]{:T(128)S(6)} %select_n.7, f32[16]{0:T(128)S(1)} %dynamic-slice.4), kind=kOutput, calls=%fused_computation.20 | convolution fusion | flops 100868096 | bytes 6701124 | tf_op jit(solution)/shard_map/dot_general | solution.py:70
  100.8 2.6 collective-permute-start.1
  103.4 3.0 collective-permute-start
  106.4 2.6 fusion.16
  112.4 64.3 %all-reduce.7.cloned.1.call-done = f32[64,3,4096]{2,0,1:T(8,128)} async-done(((f32[64,3,4096]{2,0,1:T(8,128)}), f32[64,3,4096]{2,0,1:T(8,128)}) %all-reduce.7.cloned.1.call-update) | async-done | bytes 3145744 | tf_op jit(solution)/shard_map/psum | solution.py:80
  176.8 2.0 fusion.21
  182.1 1.8 stack_reshape.55
  183.8 1.6 copy.53
  185.4 1.6 stack_reshape.56
  187.0 1.6 copy.54
  188.6 1.6 stack_reshape.57
  190.9 1.6 stack_reshape.58
  192.5 1.6 copy.56
  194.1 1.6 stack_reshape.59
  195.7 1.6 constant_dynamic-update-slice_fusion.15
  197.3 1.6 copy.57
  198.8 1.6 stack_reshape.60
  201.1 1.7 stack_reshape.61
  203.5 1.7 stack_reshape.62
  205.1 1.6 copy.60
  206.7 1.6 stack_reshape.63
  209.0 1.6 constant_dynamic-update-slice_fusion.8
  210.6 1.6 constant_dynamic-update-slice_fusion.7
  212.1 1.6 constant_dynamic-update-slice_fusion.6
  213.7 1.8 fusion.20
  218.7 1.8 fusion.19
  231.1 1.3 dynamic-slice
  233.7 191.2 %all-reduce.9.cloned.1.call-done = (f32[64,256]{0,1:T(8,128)}, f32[1024,16]{1,0:T(8,128)}) async-done(((f32[64,256]{0,1:T(8,128)}, f32[1024,16]{1,0:T(8,128)}), (f32[64,256]{0,1:T(8,128)}, f32[1024,16]{1,0:T(8,128)})) %all-reduce.9.cloned.1.call-update) | async-done | bytes 131088
  (100 shorter events, 27.5 us)
Async XLA Ops:
  7.2 3.4 copy-start.13
  7.2 3.4 copy-start.1
  7.2 3.4 copy-start.11
  7.2 80.0 %all-gather.2.cloned.1.call-start = ((), (), s32[]{:S(2)}) async-start(), calls=%async_computation | async-start | bytes 7864320 | tf_op jit(solution)/shard_map/all_gather | solution.py:63
  10.5 166.2 %all-reduce.7.cloned.1.call-start = ((), (), s32[]{:S(2)}) async-start(), calls=%async_computation.1 | async-start | bytes 6291456 | tf_op jit(solution)/shard_map/psum | solution.py:80
  13.2 0.9 copy-start.8
  13.2 411.7 %all-reduce.9.cloned.1.call-start = ((), (), s32[]{:S(2)}) async-start(), calls=%async_computation.2 | async-start | bytes 1310720
  95.8 10.6 %copy-start = (bf16[256,3,4,8,128]{4,0,3,2,1:T(8,128)(2,1)S(1)}, bf16[256,3,4,8,128]{4,0,3,2,1:T(8,128)(2,1)}, u32[]{:S(2)}) copy-start(bf16[256,3,4,8,128]{4,0,3,2,1:T(8,128)(2,1)} %all-gather.2.cloned.1.call-done) | copy-start | bytes 18874372
  100.8 8.2 %collective-permute-start.1 = (bf16[16,3,1,8,128]{4,0,3,2,1:T(8,128)(2,1)S(1)}, bf16[16,3,1,8,128]{4,0,3,2,1:T(8,128)(2,1)S(1)}, u32[]{:S(2)}, u32[]{:S(2)}) collective-permute-start(bf16[16,3,1,8,128]{4,0,3,2,1:T(8,128)(2,1)S(1)} %get-tuple-element.23), channel_id=1, source_target_pairs={{4,0},{8,4},{12,8},{16,12},{20,16},{24,20},{28,24},{32,28},{36,32}... | collective-permute-start | bytes 294920 | tf_op jit(solution)/shard_map/ppermute | solution.py:21
  103.4 5.6 %collective-permute-start = (bf16[16,3,1,8,128]{4,0,3,2,1:T(8,128)(2,1)S(1)}, bf16[16,3,1,8,128]{4,0,3,2,1:T(8,128)(2,1)S(1)}, u32[]{:S(2)}, u32[]{:S(2)}) collective-permute-start(bf16[16,3,1,8,128]{4,0,3,2,1:T(8,128)(2,1)S(1)} %get-tuple-element.22), channel_id=1, source_target_pairs={{0,4},{4,8},{8,12},{12,16},{16,20},{20,24},{24,28},{28,32},{32,36}... | collective-permute-start | bytes 294920 | tf_op jit(solution)/shard_map/ppermute | solution.py:20
  178.8 2.6 copy-start.9
  182.1 31.6 %copy-start.2 = (f32[64,3,4096]{2,0,1:T(8,128)S(1)}, f32[64,3,4096]{2,0,1:T(8,128)}, u32[]{:S(2)}) copy-start(f32[64,3,4096]{2,0,1:T(8,128)} %all-reduce.7.cloned.1.call-done) | copy-start | bytes 9437188
  190.9 17.5 %copy-start.3 = (bf16[1,16,4096]{2,1,0:T(8,128)(2,1)S(1)}, bf16[1,16,4096]{2,1,0:T(8,128)(2,1)}, u32[]{:S(2)}) copy-start(bf16[1,16,4096]{2,1,0:T(8,128)(2,1)} %stack_reshape.55) | copy-start | bytes 393220
  201.1 15.0 %copy-start.4 = (bf16[1,16,4096]{2,1,0:T(8,128)(2,1)S(1)}, bf16[1,16,4096]{2,1,0:T(8,128)(2,1)}, u32[]{:S(2)}) copy-start(bf16[1,16,4096]{2,1,0:T(8,128)(2,1)} %stack_reshape.60) | copy-start | bytes 393220
  203.5 13.3 %copy-start.5 = (bf16[1,16,4096]{2,1,0:T(8,128)(2,1)S(1)}, bf16[1,16,4096]{2,1,0:T(8,128)(2,1)}, u32[]{:S(2)}) copy-start(bf16[1,16,4096]{2,1,0:T(8,128)(2,1)} %stack_reshape.61) | copy-start | bytes 393220
  208.3 9.1 %copy-start.6 = (bf16[1,16,4096]{2,1,0:T(8,128)(2,1)S(1)}, bf16[1,16,4096]{2,1,0:T(8,128)(2,1)}, u32[]{:S(2)}) copy-start(bf16[1,16,4096]{2,1,0:T(8,128)(2,1)} %stack_reshape.62) | copy-start | bytes 393220
  208.3 9.7 %copy-start.7 = (bf16[1,16,4096]{2,1,0:T(8,128)(2,1)S(1)}, bf16[1,16,4096]{2,1,0:T(8,128)(2,1)}, u32[]{:S(2)}) copy-start(bf16[1,16,4096]{2,1,0:T(8,128)(2,1)} %stack_reshape.63) | copy-start | bytes 393220
  208.3 12.8 %copy-start.10 = (f32[64,6,16]{0,2,1:T(8,128)S(1)}, f32[64,6,16]{0,2,1:T(8,128)}, u32[]{:S(2)}) copy-start(f32[64,6,16]{0,2,1:T(8,128)} %copy-done.9) | copy-start | bytes 73732
  209.0 20.8 %copy-start.12 = (s32[16]{0:T(128)S(1)}, s32[16]{0:T(128)}, u32[]{:S(2)}) copy-start(s32[16]{0:T(128)} %param.13) | copy-start | bytes 196
Sparse Core Ops, SparseCore 0:
  10.7 76.4 all-gather.1
  89.5 87.2 all-reduce.6
  231.2 193.6 all-reduce.8
where the time goes:
time: 435 us; the launch traced here: 434 us
  waiting for transfers between devices  329 us (76%)
  local copies, waits for them, and re-layouts  65.9 us (15%)
  between operations  15.4 us (4%)
  matrix products  13.8 us (3%)
  starting transfers between devices  5.72 us (1%)
  other arithmetic  4.52 us (1%)
    unnamed x4, waiting for transfers between devices  191 us
    all_gather x1, waiting for transfers between devices, shards(): portion = lax.all_gather(direct_snaps, 'snap', axis=0, tiled=True)  73 us
    psum x1, waiting for transfers between devices, shards(): lax.psum(lax.dot_general(own_rows, flat_adjoint, contract_lead, preferred...  64.3 us
    unnamed x61, local copies, waits for them, and re-layouts  24.9 us
    another operation x19, local copies, waits for them, and re-layouts, shards(): stacked = jnp.stack(weighted)  17.4 us
    convert_element_type x16, local copies, waits for them, and re-layouts, shards(): weighted.append(shaped.astype(jnp.bfloat16).reshape(mode_count, cell_count))  10.9 us
  transfers between devices with their start and end apart: 5, of which 3 were waited for; matrix products, arithmetic and copies ran while one was open for 5% of the time, Pallas kernels for 0%

commit v1 on v0

v1 whole, which is shorter than its diff:
```python
import functools
import math

import jax
import jax.numpy as jnp
from jax import lax
from jax.experimental import pallas as pl
from jax.experimental.pallas import tpu as pltpu
from jax.sharding import Mesh, PartitionSpec as P

stencil_kind = (4, 4, 4, 1, 2, 3, 1, 2, 3, 1, 2, 3, 0, 0, 0, 0)
source_comp = (0, 1, 2, 0, 0, 0, 1, 1, 1, 2, 2, 2, 0, 1, 2, 1)
target_comp = (0, 1, 2, 0, 0, 0, 1, 1, 1, 2, 2, 2, 1, 2, 0, 0)
TERMS = len(stencil_kind)
COMPONENTS = 3
MEMBERS = tuple(
    tuple(q for q in range(TERMS) if target_comp[q] == target) for target in range(COMPONENTS)
)
ORDER = tuple(q for members in MEMBERS for q in members)
M = 256
R = 64
NY = 8
NZ = 128
CELLS = NY * NZ
SNAP = 4
COLS = M // SNAP
OWN = R // SNAP
SPACE = ("z", "y", "core")
CHUNKS = 8
LIMIT = 50 * 1024 * 1024


def mode_weight(factor, singular):
    return (factor / jnp.sqrt(singular)[None, :]).astype(jnp.bfloat16)


def columns(ref, comp, rows):
    return jnp.concatenate(
        [jnp.concatenate([ref[s, comp, y] for s in range(SNAP)], axis=0) for y in rows], axis=1
    )


def modes_kernel(snaps_ref, weight_ref, out_ref):
    weight = weight_ref[...]
    for comp in range(COMPONENTS):
        for y in range(0, NY, 2):
            block = columns(snaps_ref, comp, (y, y + 1))
            modes = jnp.dot(weight, block, preferred_element_type=jnp.float32)
            modes = modes.astype(jnp.bfloat16)
            out_ref[comp, y] = modes[:, :NZ]
            out_ref[comp, y + 1] = modes[:, NZ:]


def weighted_kernel(modes_ref, before_ref, after_ref, coeff_ref, out_ref):
    lane = lax.broadcasted_iota(jnp.int32, (R, NZ), 1)
    zero = jnp.zeros((R, NZ), jnp.float32)
    base = [0]
    for members in MEMBERS:
        base.append(base[-1] + len(members) * R)

    def put(q, y, value):
        target = target_comp[q]
        count = len(MEMBERS[target])
        at = MEMBERS[target].index(q)
        value = (value * coeff_ref[q, y : y + 1, :]).astype(jnp.bfloat16)
        for block in range(SNAP):
            row = base[target] + (block * count + at) * OWN
            out_ref[row : row + OWN, y * NZ : (y + 1) * NZ] = value[block * OWN : (block + 1) * OWN]

    for comp in range(COMPONENTS):
        field = [modes_ref[comp, y].astype(jnp.float32) for y in range(NY)]
        for y in range(NY):
            center = field[y]
            x_up = after_ref[comp, y].astype(jnp.float32)
            x_down = before_ref[comp, y].astype(jnp.float32)
            y_up = field[y + 1] if y + 1 < NY else zero
            y_down = field[y - 1] if y > 0 else zero
            z_up = jnp.where(lane == NZ - 1, 0.0, pltpu.roll(center, NZ - 1, 1))
            z_down = jnp.where(lane == 0, 0.0, pltpu.roll(center, 1, 1))
            for q in range(TERMS):
                if source_comp[q] != comp:
                    continue
                kind = stencil_kind[q]
                if kind == 0:
                    value = center
                elif kind == 1:
                    value = 0.5 * (x_up - x_down)
                elif kind == 2:
                    value = 0.5 * (y_up - y_down)
                elif kind == 3:
                    value = 0.5 * (z_up - z_down)
                else:
                    beside = x_up + x_down
                    beside = beside + y_up + y_down
                    beside = beside + z_up + z_down
                    value = beside - 6.0 * center
                put(q, y, value)


def products_kernel(scale, adjoint_ref, direct_ref, weight_ref, weighted_ref, out_ref, gram_ref, parts_ref):
    transposed = (((1,), (1,)), ((), ()))
    weight = weight_ref[...]
    gram = jnp.zeros((M, M), jnp.float32)
    for comp in range(COMPONENTS):
        for y in range(0, NY, 2):
            adjoint = columns(adjoint_ref, comp, (y, y + 1))
            direct = columns(direct_ref, comp, (y, y + 1))
            gram = gram + lax.dot_general(
                direct, adjoint, transposed, preferred_element_type=jnp.float32
            )
            modes = jnp.dot(weight, adjoint, preferred_element_type=jnp.float32)
            high = modes.astype(jnp.bfloat16)
            rest = modes - high.astype(jnp.float32)
            middle = rest.astype(jnp.bfloat16)
            low = (rest - middle.astype(jnp.float32)).astype(jnp.bfloat16)
            for part, value in enumerate((high, middle, low)):
                parts_ref[comp, part * R : (part + 1) * R, y * NZ : (y + 2) * NZ] = value
    gram = gram * scale
    gram_ref[0] = gram[:, :NZ]
    gram_ref[1] = gram[:, NZ:]
    for core in range(2):
        for snap in range(SNAP):
            half, at = snap // 2, (snap % 2) * COLS
            halves = [
                gram_ref[half, pl.ds(2 * core + t, M // 4, stride=4), :][:, at : at + COLS]
                for t in range(2)
            ]
            out_ref[core * SNAP + snap, :64, :] = jnp.concatenate(halves, axis=1)
    blocks = []
    row = 0
    for target, members in enumerate(MEMBERS):
        count = len(members) * R
        product = lax.dot_general(
            parts_ref[target],
            weighted_ref[row : row + count, :],
            transposed,
            preferred_element_type=jnp.float32,
        )
        row += count
        blocks.append((product[:R] + (product[R : 2 * R] + product[2 * R :])) * scale)
    for snap in range(SNAP):
        own = jnp.concatenate(
            [
                block[:, snap * (block.shape[1] // SNAP) : (snap + 1) * (block.shape[1] // SNAP)]
                for block in blocks
            ],
            axis=1,
        )
        for core in range(2):
            for w in range(4):
                rows = own[(2 * w + core) * 8 : (2 * w + core + 1) * 8]
                out_ref[core * SNAP + snap, 64 + w * 8 : 64 + w * 8 + 8, :] = rows[:, :NZ]
                out_ref[core * SNAP + snap, 96 + w * 8 : 96 + w * 8 + 8, :] = rows[:, NZ:]


def call(kernel, out_shape, flops, moved, scratch=()):
    return pl.pallas_call(
        kernel,
        out_shape=out_shape,
        scratch_shapes=list(scratch),
        compiler_params=pltpu.CompilerParams(vmem_limit_bytes=LIMIT),
        cost_estimate=pl.CostEstimate(flops=flops, bytes_accessed=moved, transcendentals=0),
    )


def shards(direct_snaps, adjoint_snaps, left_factor, right_factor, singular, term_coeff, term_slot):
    scale = 1.0 / math.sqrt(1572864)
    snap = lax.axis_index("snap")
    direct_weight = mode_weight(right_factor, singular).T
    adjoint_weight = mode_weight(left_factor, singular).T
    coeff = lax.dynamic_index_in_dim(term_coeff, snap, 1, keepdims=False)

    def spread(snaps):
        layers = snaps.transpose(2, 1, 3, 0, 4)
        return lax.all_to_all(layers, "snap", 0, 0, tiled=True)

    direct = spread(direct_snaps)
    adjoint = spread(adjoint_snaps)
    mode_shape = jax.ShapeDtypeStruct((COMPONENTS, NY, R, NZ), jnp.bfloat16)
    modes = call(modes_kernel, mode_shape, 2 * R * M * 3 * CELLS, 2 << 20)(direct, direct_weight)
    flat = SPACE + ("snap",)
    up = [(i, i + 1) for i in range(511)]
    before = lax.ppermute(modes, flat, up)
    after = lax.ppermute(modes, flat, [(j, i) for i, j in up])
    weighted = call(
        weighted_kernel, jax.ShapeDtypeStruct((TERMS * R, CELLS), jnp.bfloat16), 1 << 26, 3 << 20
    )(modes, before, after, coeff)
    terms = call(
        functools.partial(products_kernel, scale),
        jax.ShapeDtypeStruct((CHUNKS, 128, NZ), jnp.float32),
        1 << 30,
        6 << 20,
        (
            pltpu.VMEM((2, M, NZ), jnp.float32),
            pltpu.VMEM((COMPONENTS, 3 * R, CELLS), jnp.bfloat16),
        ),
    )(adjoint, direct, adjoint_weight, weighted)
    near = lax.all_to_all(terms, ("core", "snap"), 0, 0, tiled=True).sum(axis=0)
    gram = near[:64]
    operators = near[64:].reshape(2, 4, 8, 8, OWN).transpose(0, 3, 1, 2, 4).reshape(TERMS, 4 * NZ)
    selector = (
        term_slot[jnp.array(ORDER)][None, :] == jnp.arange(TERMS, dtype=jnp.int32)[:, None]
    ).astype(jnp.float32)
    ordered = jnp.dot(selector, operators, precision=lax.Precision.HIGHEST)
    owned = jnp.stack([gram, ordered.reshape(64, NZ)], axis=1)
    final = lax.all_to_all(owned, ("z", "y"), 0, 0, tiled=True).sum(axis=0)
    return (final[0].reshape(2, COLS).T, final[1].reshape(8, OWN))


def solution(mesh):
    parts = Mesh(mesh.devices.reshape(8, 8, 2, 4), SPACE + ("snap",))
    return jax.shard_map(
        shards,
        mesh=parts,
        in_specs=(
            P("snap", None, SPACE, None, None),
            P("snap", None, SPACE, None, None),
            P(),
            P(),
            P(),
            P(None, SPACE, None, None),
            P(),
        ),
        out_specs=(P("snap", SPACE), P(SPACE, "snap")),
        check_vma=False,
    )
```

time: 435 us -> 114 us (0.26)
  waiting for transfers between devices: 329 us -> 35.2 us
  local copies, waits for them, and re-layouts: 65.9 us -> 9.48 us
  blocking collectives: 0 us -> 32.3 us
  starting transfers between devices: 5.72 us -> 27.8 us
  between operations: 15.4 us -> 0.81 us
  matrix products: 13.8 us -> 0.14 us
  Pallas kernels: 0 us -> 6.51 us
    unnamed x4 -> x0, waiting for transfers between devices: 191 us -> none
    all_gather x1 -> x0, waiting for transfers between devices: 73 us -> none  [shards(): portion = lax.all_gather(direct_snaps, 'snap', axis=0, tiled=True)]
    psum x1 -> x0, waiting for transfers between devices: 64.3 us -> none  [shards(): lax.psum(lax.dot_general(own_rows, flat_adjoint, contract_lead, preferred...]
    all_to_all x0 -> x1, blocking collectives: none -> 32.3 us  [shards(): final = lax.all_to_all(owned, ('z', 'y'), 0, 0, tiled=True).sum(axis=0)]
    all_to_all x0 -> x3, waiting for transfers between devices: none -> 21.8 us  [the longest x2 13.1 us: spread(): return lax.all_to_all(layers, 'snap', 0, 0, tiled=True)]
    unnamed x61 -> x18, local copies, waits for them, and re-layouts: 24.9 us -> 7.12 us
    another operation x20 -> x3, local copies, waits for them, and re-layouts: 18 us -> 1.32 us  [the longest x2 1.32 us: shards(): return (final[0].reshape(2, COLS).T, final[1].reshape(8, OWN))]
    all_to_all x0 -> x3, starting transfers between devices: none -> 14.4 us  [the longest x2 8.67 us: spread(): return lax.all_to_all(layers, 'snap', 0, 0, tiled=True)]
  transfers between devices with their start and end apart: 5 -> 5, of which waited for: 3 -> 4; matrix products, arithmetic and copies ran while one was open for 5% -> 3% of each run, Pallas kernels for 0% -> 3%
where the time goes in v1:
time: 114 us; the launch traced here: 113 us
  waiting for transfers between devices  35.2 us (31%)
  blocking collectives  32.3 us (28%)
  starting transfers between devices  27.8 us (24%)
  local copies, waits for them, and re-layouts  9.48 us (8%)
  Pallas kernels  6.51 us (6%)
    all_to_all x1, blocking collectives, shards(): final = lax.all_to_all(owned, ('z', 'y'), 0, 0, tiled=True).sum(axis=0)  32.3 us
    all_to_all x2, waiting for transfers between devices, spread(): return lax.all_to_all(layers, 'snap', 0, 0, tiled=True)  13.1 us
    ppermute x1, starting transfers between devices, shards(): after = lax.ppermute(modes, flat, [(j, i) for i, j in up])  10.1 us
    all_to_all x1, waiting for transfers between devices, shards(): near = lax.all_to_all(terms, ('core', 'snap'), 0, 0, tiled=True).sum(axis=0)  8.69 us
    all_to_all x2, starting transfers between devices, spread(): return lax.all_to_all(layers, 'snap', 0, 0, tiled=True)  8.67 us
    unnamed x18, local copies, waits for them, and re-layouts  7.12 us
    ppermute x1, waiting for transfers between devices, shards(): before = lax.ppermute(modes, flat, up)  6.79 us
    ppermute x1, waiting for transfers between devices, shards(): after = lax.ppermute(modes, flat, [(j, i) for i, j in up])  6.61 us
  transfers between devices with their start and end apart: 5, of which 4 were waited for; matrix products, arithmetic and copies ran while one was open for 3% of the time, Pallas kernels for 3%

profile of v1, /device:TPU:1, one launch (start us, length us, event | category | flops | bytes accessed | tf_op | source)
XLA Modules:
  0.0 113.3 jit_solution(10609799161052478502)
XLA Ops:
  0.6 0.0 copy-start
  0.6 3.2 %copy.23 = bf16[64,3,4,8,128]{4,0,3,1,2:T(8,128)(2,1)} copy(bf16[64,3,4,8,128]{4,3,2,1,0:T(8,128)(2,1)} %param.8) | data formatting | bytes 3145728 | tf_op args[0]
  3.9 5.0 %all-to-all-start.1 = ((bf16[4,3,8,64,128]{4,3,2,1,0:T(8,128)(2,1)}), bf16[4,3,8,64,128]{4,3,2,1,0:T(8,128)(2,1)S(1)}, u32[]{:S(2)}, u32[]{:S(2)}) async-start(bf16[4,3,8,64,128]{4,3,2,1,0:T(8,128)(2,1)} %bitcast.17), calls=%async_computation.1 | async-start | bytes 3145728 | tf_op jit(solution)/shard_map/all_to_all | solution.py:175
  8.8 0.0 copy-done.4
  8.8 1.8 %copy.24 = bf16[64,3,4,8,128]{4,0,3,1,2:T(8,128)(2,1)} copy(bf16[64,3,4,8,128]{4,3,2,1,0:T(8,128)(2,1)S(1)} %copy-done.4) | data formatting | bytes 3145728 | tf_op args[1]
  10.6 13.1 %all-to-all-done.1.snaps_ref.direct_ref = bf16[4,3,8,64,128]{4,3,2,1,0:T(8,128)(2,1)S(1)} async-done(((bf16[4,3,8,64,128]{4,3,2,1,0:T(8,128)(2,1)}), bf16[4,3,8,64,128]{4,3,2,1,0:T(8,128)(2,1)S(1)}, u32[]{:S(2)}, u32[]{:S(2)}) %all-to-all-start.1) | async-done | bytes 1572896 | tf_op jit(solution)/shard_map/all_to_all | solution.py:175
  23.7 3.7 %all-to-all-start = ((bf16[4,3,8,64,128]{4,3,2,1,0:T(8,128)(2,1)}), bf16[4,3,8,64,128]{4,3,2,1,0:T(8,128)(2,1)S(1)}, u32[]{:S(2)}, u32[]{:S(2)}) async-start(bf16[4,3,8,64,128]{4,3,2,1,0:T(8,128)(2,1)} %bitcast.19), calls=%async_computation | async-start | bytes 3145728 | tf_op jit(solution)/shard_map/all_to_all | solution.py:175
  27.4 0.0 copy-done.7
  27.4 0.0 copy-done.5
  27.4 0.9 fusion.1
  28.4 1.1 %shard_map.95.modes_ref = bf16[3,8,64,128]{3,2,1,0:T(8,128)(2,1)} custom-call(bf16[4,3,8,64,128]{4,3,2,1,0:T(8,128)(2,1)S(1)} %all-to-all-done.1.snaps_ref.direct_ref, bf16[64,256]{1,0:T(8,128)(2,1)S(1)} %get-tuple-element.6.weight_ref), custom_call_target="tpu_custom_call" | custom-call | flops 100663296 | bytes 2097152 | tf_op jit(solution)/shard_map/pallas_call | solution.py:180
  29.5 3.3 %collective-permute-start = (bf16[3,8,64,128]{3,2,1,0:T(8,128)(2,1)}, bf16[3,8,64,128]{3,2,1,0:T(8,128)(2,1)}, u32[]{:S(2)}, u32[]{:S(2)}) collective-permute-start(bf16[3,8,64,128]{3,2,1,0:T(8,128)(2,1)} %shard_map.95.modes_ref), channel_id=1, source_target_pairs={{0,1},{1,2},{2,3},{3,4},{4,5},{5,6},{6,7},{7,8},{8,9},{9,10},{10,1... | collective-permute-start | bytes 1179656 | tf_op jit(solution)/shard_map/ppermute | solution.py:183
  32.8 10.1 %collective-permute-start.1 = (bf16[3,8,64,128]{3,2,1,0:T(8,128)(2,1)}, bf16[3,8,64,128]{3,2,1,0:T(8,128)(2,1)}, u32[]{:S(2)}, u32[]{:S(2)}) collective-permute-start(bf16[3,8,64,128]{3,2,1,0:T(8,128)(2,1)} %shard_map.95.modes_ref), channel_id=1, source_target_pairs={{1,0},{2,1},{3,2},{4,3},{5,4},{6,5},{7,6},{8,7},{9,8},{10,9},{11,1... | collective-permute-start | bytes 1179656 | tf_op jit(solution)/shard_map/ppermute | solution.py:184
  43.0 6.8 %collective-permute-done.before_ref = bf16[3,8,64,128]{3,2,1,0:T(8,128)(2,1)} collective-permute-done((bf16[3,8,64,128]{3,2,1,0:T(8,128)(2,1)}, bf16[3,8,64,128]{3,2,1,0:T(8,128)(2,1)}, u32[]{:S(2)}, u32[]{:S(2)}) %collective-permute-start) | collective-permute-done | bytes 393248 | tf_op jit(solution)/shard_map/ppermute | solution.py:183
  49.8 6.6 %collective-permute-done.1.after_ref = bf16[3,8,64,128]{3,2,1,0:T(8,128)(2,1)} collective-permute-done((bf16[3,8,64,128]{3,2,1,0:T(8,128)(2,1)}, bf16[3,8,64,128]{3,2,1,0:T(8,128)(2,1)}, u32[]{:S(2)}, u32[]{:S(2)}) %collective-permute-start.1) | collective-permute-done | bytes 393248 | tf_op jit(solution)/shard_map/ppermute | solution.py:184
  56.4 2.0 %shard_map.96.weighted_ref = bf16[1024,1024]{1,0:T(8,128)(2,1)S(1)} custom-call(bf16[3,8,64,128]{3,2,1,0:T(8,128)(2,1)} %shard_map.95.modes_ref, bf16[3,8,64,128]{3,2,1,0:T(8,128)(2,1)} %collective-permute-done.before_ref, bf16[3,8,64,128]{3,2,1,0:T(8,128)(2,1)} %collective-permute-done.1.after_ref, f32[16,8,128]{2,1,0:T(8,128)S(1)} %dynamic-slice_bitcast_fusion.coeff_ref), custom_call_target="tpu_custom_call" | custom-call | flops 67108864 | bytes 3145728 | tf_op jit(solution)/shard_map/pallas_call | solution.py:185
  58.4 1.3 %copy-done.1 = bf16[1024,1024]{1,0:T(8,128)(2,1)} copy-done((bf16[1024,1024]{1,0:T(8,128)(2,1)}, bf16[1024,1024]{1,0:T(8,128)(2,1)S(1)}, u32[]{:S(2)}) %copy-start.1) | copy-done | bytes 2097176
  59.8 0.0 all-to-all-done.adjoint_ref
  59.8 3.3 %shard_map.97 = f32[8,128,128]{2,1,0:T(8,128)S(1)} custom-call(bf16[4,3,8,64,128]{4,3,2,1,0:T(8,128)(2,1)S(1)} %all-to-all-done.adjoint_ref, bf16[4,3,8,64,128]{4,3,2,1,0:T(8,128)(2,1)S(1)} %all-to-all-done.1.snaps_ref.direct_ref, bf16[64,256]{1,0:T(8,128)(2,1)S(1)} %get-tuple-element.7.weight_ref, bf16[1024,1024]{1,0:T(8,128)(2,1)} %copy-done.1), custom_call_target="tpu_custom_call" | custom-call | flops 1073741824 | bytes 6291456 | tf_op jit(solution)/shard_map/pallas_call | solution.py:188
  63.1 0.8 copy-done.2
  63.9 5.7 %all-to-all-start.2 = ((f32[8,128,128]{2,1,0:T(8,128)}), f32[8,128,128]{2,1,0:T(8,128)S(1)}, u32[]{:S(2)}, u32[]{:S(2)}) async-start(f32[8,128,128]{2,1,0:T(8,128)} %copy-done.2), calls=%async_computation.2 | async-start | bytes 1048576 | tf_op jit(solution)/shard_map/all_to_all | solution.py:198
  69.7 0.7 gather_fusion
  70.3 8.7 %all-to-all-done.2 = f32[8,128,128]{2,1,0:T(8,128)S(1)} async-done(((f32[8,128,128]{2,1,0:T(8,128)}), f32[8,128,128]{2,1,0:T(8,128)S(1)}, u32[]{:S(2)}, u32[]{:S(2)}) %all-to-all-start.2) | async-done | bytes 524320 | tf_op jit(solution)/shard_map/all_to_all | solution.py:198
  79.1 0.1 reshape.12
  79.2 0.1 copy.19
  79.3 0.2 reshape.13
  79.4 0.1 fusion.2
  79.6 0.1 pad_maximum_fusion
  79.6 32.3 %all_to_all.20 = f32[64,2,128]{2,1,0:T(2,128)S(1)} all-to-all(f32[64,2,128]{2,1,0:T(2,128)S(1)} %pad_maximum_fusion), channel_id=1, replica_groups=mesh['z'=8,'y'=8,'core'=2,'snap'=4] {'z','y'}, dimensions={0} | all-to-all | bytes 131072 | tf_op jit(solution)/shard_map/all_to_all | solution.py:206
  111.9 0.1 reduce_sum.19
  112.0 0.6 reshape_squeeze.6
  112.7 0.7 reshape_squeeze.7
  (17 shorter events, 0.1 us)
Async XLA Ops:
  0.6 42.3 %copy-start = (f32[16,4,8,128]{3,2,1,0:T(8,128)S(1)}, f32[16,4,8,128]{3,2,1,0:T(8,128)}, u32[]{:S(2)}) copy-start(f32[16,4,8,128]{3,2,1,0:T(8,128)} %param.13) | copy-start | bytes 786436
  3.9 5.0 %copy-start.4 = (bf16[64,3,4,8,128]{4,3,2,1,0:T(8,128)(2,1)S(1)}, bf16[64,3,4,8,128]{4,3,2,1,0:T(8,128)(2,1)}, u32[]{:S(2)}) copy-start(bf16[64,3,4,8,128]{4,3,2,1,0:T(8,128)(2,1)} %param.9) | copy-start | bytes 4718596
  3.9 19.9 %all-to-all-start.1 = ((bf16[4,3,8,64,128]{4,3,2,1,0:T(8,128)(2,1)}), bf16[4,3,8,64,128]{4,3,2,1,0:T(8,128)(2,1)S(1)}, u32[]{:S(2)}, u32[]{:S(2)}) async-start(bf16[4,3,8,64,128]{4,3,2,1,0:T(8,128)(2,1)} %bitcast.17), calls=%async_computation.1 | async-start | bytes 3145728 | tf_op jit(solution)/shard_map/all_to_all | solution.py:175
  23.7 3.7 %copy-start.7 = (f32[64]{0:T(128)S(1)}, f32[64]{0:T(128)}, u32[]{:S(2)}) copy-start(f32[64]{0:T(128)} %param.12) | copy-start | bytes 772
  23.7 3.7 %copy-start.5 = (f32[256,64]{0,1:T(8,128)S(1)}, f32[256,64]{0,1:T(8,128)}, u32[]{:S(2)}) copy-start(f32[256,64]{0,1:T(8,128)} %param.11) | copy-start | bytes 196612
  23.7 36.1 %all-to-all-start = ((bf16[4,3,8,64,128]{4,3,2,1,0:T(8,128)(2,1)}), bf16[4,3,8,64,128]{4,3,2,1,0:T(8,128)(2,1)S(1)}, u32[]{:S(2)}, u32[]{:S(2)}) async-start(bf16[4,3,8,64,128]{4,3,2,1,0:T(8,128)(2,1)} %bitcast.19), calls=%async_computation | async-start | bytes 3145728 | tf_op jit(solution)/shard_map/all_to_all | solution.py:175
  29.5 20.2 %collective-permute-start = (bf16[3,8,64,128]{3,2,1,0:T(8,128)(2,1)}, bf16[3,8,64,128]{3,2,1,0:T(8,128)(2,1)}, u32[]{:S(2)}, u32[]{:S(2)}) collective-permute-start(bf16[3,8,64,128]{3,2,1,0:T(8,128)(2,1)} %shard_map.95.modes_ref), channel_id=1, source_target_pairs={{0,1},{1,2},{2,3},{3,4},{4,5},{5,6},{6,7},{7,8},{8,9},{9,10},{10,1... | collective-permute-start | bytes 1179656 | tf_op jit(solution)/shard_map/ppermute | solution.py:183
  32.8 23.5 %collective-permute-start.1 = (bf16[3,8,64,128]{3,2,1,0:T(8,128)(2,1)}, bf16[3,8,64,128]{3,2,1,0:T(8,128)(2,1)}, u32[]{:S(2)}, u32[]{:S(2)}) collective-permute-start(bf16[3,8,64,128]{3,2,1,0:T(8,128)(2,1)} %shard_map.95.modes_ref), channel_id=1, source_target_pairs={{1,0},{2,1},{3,2},{4,3},{5,4},{6,5},{7,6},{8,7},{9,8},{10,9},{11,1... | collective-permute-start | bytes 1179656 | tf_op jit(solution)/shard_map/ppermute | solution.py:184
  58.4 1.3 %copy-start.1 = (bf16[1024,1024]{1,0:T(8,128)(2,1)}, bf16[1024,1024]{1,0:T(8,128)(2,1)S(1)}, u32[]{:S(2)}) copy-start(bf16[1024,1024]{1,0:T(8,128)(2,1)S(1)} %shard_map.96.weighted_ref) | copy-start | bytes 6291460
  59.8 9.9 %copy-start.6 = (s32[16]{0:T(128)S(1)}, s32[16]{0:T(128)}, u32[]{:S(2)}) copy-start(s32[16]{0:T(128)} %constant.25) | copy-start | bytes 196
  59.8 9.9 %copy-start.3 = (s32[16]{0:T(128)S(1)}, s32[16]{0:T(128)}, u32[]{:S(2)}) copy-start(s32[16]{0:T(128)} %param.14) | copy-start | bytes 196
  63.1 0.8 copy-start.2
  63.9 15.1 %all-to-all-start.2 = ((f32[8,128,128]{2,1,0:T(8,128)}), f32[8,128,128]{2,1,0:T(8,128)S(1)}, u32[]{:S(2)}, u32[]{:S(2)}) async-start(f32[8,128,128]{2,1,0:T(8,128)} %copy-done.2), calls=%async_computation.2 | async-start | bytes 1048576 | tf_op jit(solution)/shard_map/all_to_all | solution.py:198

commit v2 on v1

v2 whole, which is shorter than its diff:
```python
import functools
import math

import jax
import jax.numpy as jnp
from jax import lax
from jax.experimental import pallas as pl
from jax.experimental.pallas import tpu as pltpu
from jax.sharding import Mesh, PartitionSpec as P

stencil_kind = (4, 4, 4, 1, 2, 3, 1, 2, 3, 1, 2, 3, 0, 0, 0, 0)
source_comp = (0, 1, 2, 0, 0, 0, 1, 1, 1, 2, 2, 2, 0, 1, 2, 1)
target_comp = (0, 1, 2, 0, 0, 0, 1, 1, 1, 2, 2, 2, 1, 2, 0, 0)
TERMS = len(stencil_kind)
COMPONENTS = 3
MEMBERS = tuple(
    tuple(q for q in range(TERMS) if target_comp[q] == target) for target in range(COMPONENTS)
)
ORDER = tuple(q for members in MEMBERS for q in members)
M = 256
R = 64
NY = 8
NZ = 128
CELLS = NY * NZ
SNAP = 4
COLS = M // SNAP
OWN = R // SNAP
SPACE = ("z", "y", "core")
CHUNKS = 8
LIMIT = 24 * 1024 * 1024


def mode_weight(factor, singular):
    return (factor / jnp.sqrt(singular)[None, :]).astype(jnp.bfloat16)


TILES = 8
GROUP = NZ // SNAP


def spread_tiles(snaps_ref, out_ref):
    for comp in range(COMPONENTS):
        for x in range(4):
            rows = jnp.swapaxes(snaps_ref[:, comp, x], 0, 1)
            for half in range(2):
                group = [rows[half * 4 + i] for i in range(4)]
                for quarter in range(SNAP):
                    at = quarter * GROUP
                    out_ref[quarter, comp * TILES + x * 2 + half] = jnp.concatenate(
                        [row[:, at : at + GROUP] for row in group], axis=1
                    )


def direct_kernel(snaps_ref, out_ref):
    spread_tiles(snaps_ref, out_ref)


def adjoint_kernel(
    snap_ref, snaps_ref, left_ref, right_ref, coeff_ref, out_ref, left_out, right_out, coeff_out
):
    spread_tiles(snaps_ref, out_ref)
    left_out[...] = left_ref[...]
    right_out[...] = right_ref[...]
    shift = lax.rem(NZ - GROUP * snap_ref[0], NZ)
    for q in range(TERMS):
        for x in range(4):
            own = pltpu.roll(coeff_ref[q, x], shift, 1)
            for half in range(2):
                coeff_out[q, x * 2 + half : x * 2 + half + 1, :] = jnp.concatenate(
                    [own[half * 4 + i : half * 4 + i + 1, :GROUP] for i in range(4)], axis=1
                )


def columns(ref, comp, tiles):
    return jnp.concatenate(
        [
            jnp.concatenate([ref[s, comp * TILES + t] for s in range(SNAP)], axis=0)
            for t in tiles
        ],
        axis=1,
    )


def modes_kernel(snaps_ref, weight_ref, out_ref, first_ref, last_ref, low_ref, high_ref):
    weight = weight_ref[...]
    place = lax.rem(lax.broadcasted_iota(jnp.int32, (R, NZ), 1), GROUP)
    low = jnp.zeros((R, NZ), jnp.float32)
    high = jnp.zeros((R, NZ), jnp.float32)
    for comp in range(COMPONENTS):
        for t in range(0, TILES, 2):
            block = columns(snaps_ref, comp, (t, t + 1))
            modes = jnp.dot(weight, block, preferred_element_type=jnp.float32)
            modes = modes.astype(jnp.bfloat16)
            for half in range(2):
                tile = modes[:, half * NZ : (half + 1) * NZ]
                index = comp * TILES + t + half
                out_ref[index] = tile
                if t == 0:
                    first_ref[comp * 2 + half] = tile
                if t == TILES - 2:
                    last_ref[comp * 2 + half] = tile
                wide = tile.astype(jnp.float32)
                edge = jnp.where(place == 0, wide, 0.0)
                low = low + (pltpu.roll(edge, index, 1) if index else edge)
                edge = jnp.where(place == GROUP - 1, wide, 0.0)
                high = high + pltpu.roll(edge, NZ + index - (GROUP - 1), 1)
    low_ref[...] = low.astype(jnp.bfloat16)
    high_ref[...] = high.astype(jnp.bfloat16)


def weighted_kernel(
    modes_ref, before_ref, after_ref, below_ref, above_ref, coeff_ref, out_ref
):
    lane = lax.broadcasted_iota(jnp.int32, (R, NZ), 1)
    place = lax.rem(lane, GROUP)
    below = below_ref[...].astype(jnp.float32)
    above = above_ref[...].astype(jnp.float32)
    base = [0]
    for members in MEMBERS:
        base.append(base[-1] + len(members) * R)

    def put(q, t, value):
        target = target_comp[q]
        count = len(MEMBERS[target])
        at = MEMBERS[target].index(q)
        value = (value * coeff_ref[q, t : t + 1, :]).astype(jnp.bfloat16)
        for block in range(SNAP):
            row = base[target] + (block * count + at) * OWN
            out_ref[row : row + OWN, t * NZ : (t + 1) * NZ] = value[block * OWN : (block + 1) * OWN]

    for comp in range(COMPONENTS):
        field = [modes_ref[comp * TILES + t].astype(jnp.float32) for t in range(TILES)]
        down = [before_ref[comp * 2 + h].astype(jnp.float32) for h in range(2)] + field[:-2]
        up = field[2:] + [after_ref[comp * 2 + h].astype(jnp.float32) for h in range(2)]
        for x in range(4):
            pair = field[2 * x : 2 * x + 2]
            ahead = [pltpu.roll(v, NZ - GROUP, 1) for v in pair]
            behind = [pltpu.roll(v, GROUP, 1) for v in pair]
            for half in range(2):
                t = 2 * x + half
                index = comp * TILES + t
                center = pair[half]
                x_up, x_down = up[t], down[t]
                y_up = jnp.where(lane >= NZ - GROUP, ahead[1] if half == 0 else 0.0, ahead[half])
                y_down = jnp.where(lane < GROUP, behind[0] if half == 1 else 0.0, behind[half])
                z_up = jnp.where(
                    place == GROUP - 1,
                    pltpu.roll(above, GROUP - 1 - index, 1),
                    pltpu.roll(center, NZ - 1, 1),
                )
                z_down = jnp.where(
                    place == 0,
                    pltpu.roll(below, NZ - index, 1) if index else below,
                    pltpu.roll(center, 1, 1),
                )
                for q in range(TERMS):
                    if source_comp[q] != comp:
                        continue
                    kind = stencil_kind[q]
                    if kind == 0:
                        value = center
                    elif kind == 1:
                        value = 0.5 * (x_up - x_down)
                    elif kind == 2:
                        value = 0.5 * (y_up - y_down)
                    elif kind == 3:
                        value = 0.5 * (z_up - z_down)
                    else:
                        beside = x_up + x_down
                        beside = beside + y_up + y_down
                        beside = beside + z_up + z_down
                        value = beside - 6.0 * center
                    put(q, t, value)


def products_kernel(scale, adjoint_ref, direct_ref, weight_ref, weighted_ref, out_ref, gram_ref, parts_ref):
    transposed = (((1,), (1,)), ((), ()))
    weight = weight_ref[...]
    gram = jnp.zeros((M, M), jnp.float32)
    for comp in range(COMPONENTS):
        for t in range(0, TILES, 2):
            adjoint = columns(adjoint_ref, comp, (t, t + 1))
            direct = columns(direct_ref, comp, (t, t + 1))
            gram = gram + lax.dot_general(
                direct, adjoint, transposed, preferred_element_type=jnp.float32
            )
            modes = jnp.dot(weight, adjoint, preferred_element_type=jnp.float32)
            high = modes.astype(jnp.bfloat16)
            rest = modes - high.astype(jnp.float32)
            middle = rest.astype(jnp.bfloat16)
            low = (rest - middle.astype(jnp.float32)).astype(jnp.bfloat16)
            for part, value in enumerate((high, middle, low)):
                parts_ref[comp, part * R : (part + 1) * R, t * NZ : (t + 2) * NZ] = value
    gram = gram * scale
    gram_ref[0] = gram[:, :NZ]
    gram_ref[1] = gram[:, NZ:]
    for core in range(2):
        for snap in range(SNAP):
            half, at = snap // 2, (snap % 2) * COLS
            halves = [
                gram_ref[half, pl.ds(2 * core + t, M // 4, stride=4), :][:, at : at + COLS]
                for t in range(2)
            ]
            out_ref[core * SNAP + snap, :64, :] = jnp.concatenate(halves, axis=1)
    blocks = []
    row = 0
    for target, members in enumerate(MEMBERS):
        count = len(members) * R
        product = lax.dot_general(
            parts_ref[target],
            weighted_ref[row : row + count, :],
            transposed,
            preferred_element_type=jnp.float32,
        )
        row += count
        blocks.append((product[:R] + (product[R : 2 * R] + product[2 * R :])) * scale)
    for snap in range(SNAP):
        own = jnp.concatenate(
            [
                block[:, snap * (block.shape[1] // SNAP) : (snap + 1) * (block.shape[1] // SNAP)]
                for block in blocks
            ],
            axis=1,
        )
        for core in range(2):
            for w in range(4):
                rows = own[(2 * w + core) * 8 : (2 * w + core + 1) * 8]
                out_ref[core * SNAP + snap, 64 + w * 8 : 64 + w * 8 + 8, :] = rows[:, :NZ]
                out_ref[core * SNAP + snap, 96 + w * 8 : 96 + w * 8 + 8, :] = rows[:, NZ:]


def call(kernel, out_shape, flops, moved, scratch=(), smem=0):
    def run(*operands):
        spaces = [pltpu.SMEM] * smem + [pltpu.VMEM] * (len(operands) - smem)
        return pl.pallas_call(
            kernel,
            out_shape=out_shape,
            in_specs=[pl.BlockSpec(memory_space=space) for space in spaces],
            scratch_shapes=list(scratch),
            compiler_params=pltpu.CompilerParams(vmem_limit_bytes=LIMIT),
            cost_estimate=pl.CostEstimate(flops=flops, bytes_accessed=moved, transcendentals=0),
        )(*operands)

    return run


def shards(direct_snaps, adjoint_snaps, left_factor, right_factor, singular, term_coeff, term_slot):
    scale = 1.0 / math.sqrt(1572864)
    left = mode_weight(left_factor, singular).T
    right = mode_weight(right_factor, singular).T
    tiles = COMPONENTS * TILES

    def shape(*dims, dtype=jnp.bfloat16):
        return jax.ShapeDtypeStruct(dims, dtype)

    spread_shape = shape(SNAP, tiles, COLS, NZ)
    ready = call(direct_kernel, spread_shape, 0, 3 << 20)(direct_snaps)
    direct = lax.all_to_all(ready, "snap", 0, 0, tiled=True)
    here = lax.axis_index("snap").astype(jnp.int32).reshape(1)
    ready, adjoint_weight, direct_weight, coeff = call(
        adjoint_kernel,
        (
            spread_shape,
            shape(R, M),
            shape(R, M),
            shape(TERMS, TILES, NZ, dtype=jnp.float32),
        ),
        0,
        3 << 20,
        smem=1,
    )(here, adjoint_snaps, left, right, term_coeff)
    adjoint = lax.all_to_all(ready, "snap", 0, 0, tiled=True)
    modes, first, last, low, high = call(
        modes_kernel,
        (shape(tiles, R, NZ), shape(6, R, NZ), shape(6, R, NZ), shape(R, NZ), shape(R, NZ)),
        2 * R * M * 3 * CELLS,
        2 << 20,
    )(direct, direct_weight)
    slabs, quarters = ([(i, i + 1) for i in range(n - 1)] for n in (128, SNAP))
    before = lax.ppermute(last, SPACE, slabs)
    after = lax.ppermute(first, SPACE, [(j, i) for i, j in slabs])
    below = lax.ppermute(high, "snap", quarters)
    above = lax.ppermute(low, "snap", [(j, i) for i, j in quarters])
    weighted = call(weighted_kernel, shape(TERMS * R, CELLS), 1 << 26, 3 << 20)(
        modes, before, after, below, above, coeff
    )
    terms = call(
        functools.partial(products_kernel, scale),
        jax.ShapeDtypeStruct((CHUNKS, 128, NZ), jnp.float32),
        1 << 30,
        6 << 20,
        (
            pltpu.VMEM((2, M, NZ), jnp.float32),
            pltpu.VMEM((COMPONENTS, 3 * R, CELLS), jnp.bfloat16),
        ),
    )(adjoint, direct, adjoint_weight, weighted)
    near = lax.all_to_all(terms, ("core", "snap"), 0, 0, tiled=True).sum(axis=0)
    gram = near[:64]
    operators = near[64:].reshape(2, 4, 8, 8, OWN).transpose(0, 3, 1, 2, 4).reshape(TERMS, 4 * NZ)
    selector = (
        term_slot[jnp.array(ORDER)][None, :] == jnp.arange(TERMS, dtype=jnp.int32)[:, None]
    ).astype(jnp.float32)
    ordered = jnp.dot(selector, operators, precision=lax.Precision.HIGHEST)
    owned = jnp.stack([gram, ordered.reshape(64, NZ)], axis=1)
    final = lax.all_to_all(owned, ("z", "y"), 0, 0, tiled=True).sum(axis=0)
    return (final[0].reshape(2, COLS).T, final[1].reshape(8, OWN))


def solution(mesh):
    parts = Mesh(mesh.devices.reshape(8, 8, 2, 4), SPACE + ("snap",))
    return jax.shard_map(
        shards,
        mesh=parts,
        in_specs=(
            P("snap", None, SPACE, None, None),
            P("snap", None, SPACE, None, None),
            P(),
            P(),
            P(),
            P(None, SPACE, None, None),
            P(),
        ),
        out_specs=(P("snap", SPACE), P(SPACE, "snap")),
        check_vma=False,
    )
```

time: 114 us -> 103 us (0.904)
  waiting for transfers between devices: 35.2 us -> 21 us
  Pallas kernels: 6.51 us -> 10.4 us
  starting transfers between devices: 27.8 us -> 29 us
    ppermute x2 -> x4, waiting for transfers between devices: 13.4 us -> 3.48 us  [the longest x1 3.47 us: shards(): above = lax.ppermute(low, 'snap', [(j, i) for i, j in quarters])]
    all_to_all x2, waiting for transfers between devices: 13.1 us -> 8.82 us  [the longest x1 8.82 us: shards(): direct = lax.all_to_all(ready, 'snap', 0, 0, tiled=True)]
    pallas_call x3 -> x5, Pallas kernels: 6.51 us -> 10.4 us  [run(): pl.pallas_call(kernel, out_shape=out_shape, in_specs=[pl.BlockSpec(memory...]
    ppermute x2 -> x4, starting transfers between devices: 13.4 us -> 16.7 us  [the longest x1 9.88 us: shards(): before = lax.ppermute(last, SPACE, slabs)]
    all_to_all x1, starting transfers between devices: 5.73 us -> 3.78 us  [shards(): near = lax.all_to_all(terms, ('core', 'snap'), 0, 0, tiled=True).sum(axis=0)]
    unnamed x18 -> x24, local copies, waits for them, and re-layouts: 7.12 us -> 6.3 us
  transfers between devices with their start and end apart: 5 -> 7, of which waited for: 4 -> 3; matrix products, arithmetic and copies ran while one was open for 3% -> 1% of each run, Pallas kernels for 3% -> 6%
where the time goes in v2:
time: 103 us; the launch traced here: 102 us
  blocking collectives  32.1 us (31%)
  starting transfers between devices  29 us (28%)
  waiting for transfers between devices  21 us (20%)
  Pallas kernels  10.4 us (10%)
  local copies, waits for them, and re-layouts  8.64 us (8%)
    all_to_all x1, blocking collectives, shards(): final = lax.all_to_all(owned, ('z', 'y'), 0, 0, tiled=True).sum(axis=0)  32.1 us
    pallas_call x5, Pallas kernels, run(): pl.pallas_call(kernel, out_shape=out_shape, in_specs=[pl.BlockSpec(memory...  10.4 us
    ppermute x1, starting transfers between devices, shards(): before = lax.ppermute(last, SPACE, slabs)  9.88 us
    all_to_all x1, waiting for transfers between devices, shards(): direct = lax.all_to_all(ready, 'snap', 0, 0, tiled=True)  8.82 us
    all_to_all x1, waiting for transfers between devices, shards(): near = lax.all_to_all(terms, ('core', 'snap'), 0, 0, tiled=True).sum(axis=0)  8.69 us
    unnamed x24, local copies, waits for them, and re-layouts  6.3 us
    all_to_all x1, starting transfers between devices, shards(): direct = lax.all_to_all(ready, 'snap', 0, 0, tiled=True)  4.99 us
    all_to_all x1, starting transfers between devices, shards(): near = lax.all_to_all(terms, ('core', 'snap'), 0, 0, tiled=True).sum(axis=0)  3.78 us
  transfers between devices with their start and end apart: 7, of which 3 were waited for; matrix products, arithmetic and copies ran while one was open for 1% of the time, Pallas kernels for 6%

profile of v2, /device:TPU:1, one launch (start us, length us, event | category | flops | bytes accessed | tf_op | source)
XLA Modules:
  0.0 102.5 jit_solution(6552029501743514738)
XLA Ops:
  0.6 0.0 copy-start
  0.7 1.4 %copy-done.4 = bf16[64,3,4,8,128]{4,3,2,1,0:T(8,128)(2,1)S(1)} copy-done((bf16[64,3,4,8,128]{4,3,2,1,0:T(8,128)(2,1)S(1)}, bf16[64,3,4,8,128]{4,3,2,1,0:T(8,128)(2,1)}, u32[]{:S(2)}) %copy-start.4) | copy-done | bytes 1572888
  2.1 2.5 %shard_map.96 = bf16[4,24,64,128]{3,2,1,0:T(8,128)(2,1)} custom-call(bf16[64,3,4,8,128]{4,3,2,1,0:T(8,128)(2,1)S(1)} %copy-done.4), custom_call_target="tpu_custom_call" | custom-call | bytes 3145728 | tf_op jit(solution)/shard_map/pallas_call | solution.py:235
  4.6 5.0 %all-to-all-start.1 = ((bf16[4,24,64,128]{3,2,1,0:T(8,128)(2,1)}), bf16[4,24,64,128]{3,2,1,0:T(8,128)(2,1)S(1)}, u32[]{:S(2)}, u32[]{:S(2)}) async-start(bf16[4,24,64,128]{3,2,1,0:T(8,128)(2,1)} %shard_map.96), calls=%async_computation.1 | async-start | bytes 3145728 | tf_op jit(solution)/shard_map/all_to_all | solution.py:258
  9.6 0.1 fusion.1
  9.7 4.7 %shard_map.95 = (bf16[4,24,64,128]{3,2,1,0:T(8,128)(2,1)S(1)}, bf16[64,256]{1,0:T(8,128)(2,1)S(1)}, bf16[64,256]{1,0:T(8,128)(2,1)S(1)}, f32[16,8,128]{2,1,0:T(8,128)S(1)}) custom-call(s32[1]{0:T(128)} %bitcast.snap_ref, bf16[64,3,4,8,128]{4,3,2,1,0:T(8,128)(2,1)S(1)} %copy-done.6, bf16[64,256]{1,0:T(8,128)(2,1)S(1)} %get-tuple-element.25.left_ref, ...), custom_call_target="tpu_custom_call" | custom-call | bytes 3145728 | tf_op jit(solution)/shard_map/pallas_call | solution.py:235
  14.4 1.2 %copy-done.5 = bf16[4,24,64,128]{3,2,1,0:T(8,128)(2,1)} copy-done((bf16[4,24,64,128]{3,2,1,0:T(8,128)(2,1)}, bf16[4,24,64,128]{3,2,1,0:T(8,128)(2,1)S(1)}, u32[]{:S(2)}) %copy-start.5) | copy-done | bytes 1572888
  15.6 8.8 %all-to-all-done.1.snaps_ref.direct_ref = bf16[4,24,64,128]{3,2,1,0:T(8,128)(2,1)S(1)} async-done(((bf16[4,24,64,128]{3,2,1,0:T(8,128)(2,1)}), bf16[4,24,64,128]{3,2,1,0:T(8,128)(2,1)S(1)}, u32[]{:S(2)}, u32[]{:S(2)}) %all-to-all-start.1) | async-done | bytes 1572896 | tf_op jit(solution)/shard_map/all_to_all | solution.py:258
  24.4 3.6 %all-to-all-start = ((bf16[4,24,64,128]{3,2,1,0:T(8,128)(2,1)}), bf16[4,24,64,128]{3,2,1,0:T(8,128)(2,1)S(1)}, u32[]{:S(2)}, u32[]{:S(2)}) async-start(bf16[4,24,64,128]{3,2,1,0:T(8,128)(2,1)} %copy-done.5), calls=%async_computation | async-start | bytes 3145728 | tf_op jit(solution)/shard_map/all_to_all | solution.py:272
  28.0 0.5 shard_map.97
  28.5 9.9 %collective-permute-start = (bf16[6,64,128]{2,1,0:T(8,128)(2,1)S(1)}, bf16[6,64,128]{2,1,0:T(8,128)(2,1)S(1)}, u32[]{:S(2)}, u32[]{:S(2)}) collective-permute-start(bf16[6,64,128]{2,1,0:T(8,128)(2,1)S(1)} %get-tuple-element.15), channel_id=1, source_target_pairs={{0,4},{4,8},{8,12},{12,16},{16,20},{20,24},{24,28},{28,32},{32,36}... | collective-permute-start | bytes 294920 | tf_op jit(solution)/shard_map/ppermute | solution.py:280
  38.4 1.9 %collective-permute-start.1 = (bf16[6,64,128]{2,1,0:T(8,128)(2,1)S(1)}, bf16[6,64,128]{2,1,0:T(8,128)(2,1)S(1)}, u32[]{:S(2)}, u32[]{:S(2)}) collective-permute-start(bf16[6,64,128]{2,1,0:T(8,128)(2,1)S(1)} %get-tuple-element.16), channel_id=1, source_target_pairs={{4,0},{8,4},{12,8},{16,12},{20,16},{24,20},{28,24},{32,28},{36,32}... | collective-permute-start | bytes 294920 | tf_op jit(solution)/shard_map/ppermute | solution.py:281
  40.3 3.6 %collective-permute-start.2 = (bf16[64,128]{1,0:T(8,128)(2,1)S(1)}, bf16[64,128]{1,0:T(8,128)(2,1)S(1)}, u32[]{:S(2)}, u32[]{:S(2)}) collective-permute-start(bf16[64,128]{1,0:T(8,128)(2,1)S(1)} %get-tuple-element.17), channel_id=1, source_target_pairs={{0,1},{1,2},{2,3},{4,5},{5,6},{6,7},{8,9},{9,10},{10,11},{12,13},{... | collective-permute-start | bytes 49160 | tf_op jit(solution)/shard_map/ppermute | solution.py:282
  43.9 1.3 %collective-permute-start.3 = (bf16[64,128]{1,0:T(8,128)(2,1)S(1)}, bf16[64,128]{1,0:T(8,128)(2,1)S(1)}, u32[]{:S(2)}, u32[]{:S(2)}) collective-permute-start(bf16[64,128]{1,0:T(8,128)(2,1)S(1)} %get-tuple-element.18), channel_id=1, source_target_pairs={{1,0},{2,1},{3,2},{5,4},{6,5},{7,6},{9,8},{10,9},{11,10},{13,12},{... | collective-permute-start | bytes 49160 | tf_op jit(solution)/shard_map/ppermute | solution.py:283
  45.2 3.5 %collective-permute-done.3.above_ref = bf16[64,128]{1,0:T(8,128)(2,1)S(1)} collective-permute-done((bf16[64,128]{1,0:T(8,128)(2,1)S(1)}, bf16[64,128]{1,0:T(8,128)(2,1)S(1)}, u32[]{:S(2)}, u32[]{:S(2)}) %collective-permute-start.3) | collective-permute-done | bytes 16416 | tf_op jit(solution)/shard_map/ppermute | solution.py:283
  48.7 1.0 shard_map.98.weighted_ref
  49.7 1.3 %copy-done.1 = bf16[1024,1024]{1,0:T(8,128)(2,1)} copy-done((bf16[1024,1024]{1,0:T(8,128)(2,1)}, bf16[1024,1024]{1,0:T(8,128)(2,1)S(1)}, u32[]{:S(2)}) %copy-start.1) | copy-done | bytes 2097176
  51.1 1.6 %copy-done.2 = bf16[1024,1024]{1,0:T(8,128)(2,1)S(1)} copy-done((bf16[1024,1024]{1,0:T(8,128)(2,1)S(1)}, bf16[1024,1024]{1,0:T(8,128)(2,1)}, u32[]{:S(2)}) %copy-start.2) | copy-done | bytes 2097176
  52.7 1.7 %shard_map.99 = f32[8,128,128]{2,1,0:T(8,128)S(1)} custom-call(bf16[4,24,64,128]{3,2,1,0:T(8,128)(2,1)S(1)} %all-to-all-done.adjoint_ref, bf16[4,24,64,128]{3,2,1,0:T(8,128)(2,1)S(1)} %all-to-all-done.1.snaps_ref.direct_ref, bf16[64,256]{1,0:T(8,128)(2,1)S(1)} %get-tuple-element.12.weight_ref, bf16[1024,1024]{1,0:T(8,128)(2,1)S(1)} %copy-done.2), custom_call_target="tpu_custom_call" | custom-call | flops 1073741824 | bytes 6291456 | tf_op jit(solution)/shard_map/pallas_call | solution.py:235
  54.4 0.8 copy-done.3
  55.2 3.8 %all-to-all-start.2 = ((f32[8,128,128]{2,1,0:T(8,128)}), f32[8,128,128]{2,1,0:T(8,128)S(1)}, u32[]{:S(2)}, u32[]{:S(2)}) async-start(f32[8,128,128]{2,1,0:T(8,128)} %copy-done.3), calls=%async_computation.2 | async-start | bytes 1048576 | tf_op jit(solution)/shard_map/all_to_all | solution.py:297
  59.0 0.7 gather_fusion
  59.6 8.7 %all-to-all-done.2 = f32[8,128,128]{2,1,0:T(8,128)S(1)} async-done(((f32[8,128,128]{2,1,0:T(8,128)}), f32[8,128,128]{2,1,0:T(8,128)S(1)}, u32[]{:S(2)}, u32[]{:S(2)}) %all-to-all-start.2) | async-done | bytes 524320 | tf_op jit(solution)/shard_map/all_to_all | solution.py:297
  68.4 0.1 reshape.16
  68.5 0.1 copy.11
  68.6 0.2 reshape.17
  68.7 0.1 fusion.2
  68.9 0.1 pad_maximum_fusion
  68.9 32.1 %all_to_all.20 = f32[64,2,128]{2,1,0:T(2,128)S(1)} all-to-all(f32[64,2,128]{2,1,0:T(2,128)S(1)} %pad_maximum_fusion), channel_id=1, replica_groups=mesh['z'=8,'y'=8,'core'=2,'snap'=4] {'z','y'}, dimensions={0} | all-to-all | bytes 131072 | tf_op jit(solution)/shard_map/all_to_all | solution.py:305
  101.1 0.1 reduce_sum.19
  101.2 0.6 reshape_squeeze.6
  101.8 0.7 reshape_squeeze.7
  (28 shorter events, 0.1 us)
Async XLA Ops:
  0.6 58.3 %copy-start = (s32[16]{0:T(128)S(1)}, s32[16]{0:T(128)}, u32[]{:S(2)}) copy-start(s32[16]{0:T(128)} %param.14) | copy-start | bytes 196
  0.6 1.4 %copy-start.4 = (bf16[64,3,4,8,128]{4,3,2,1,0:T(8,128)(2,1)S(1)}, bf16[64,3,4,8,128]{4,3,2,1,0:T(8,128)(2,1)}, u32[]{:S(2)}) copy-start(bf16[64,3,4,8,128]{4,3,2,1,0:T(8,128)(2,1)} %snaps_ref.3) | copy-start | bytes 4718596
  4.5 5.0 %copy-start.11 = (f32[64]{0:T(128)S(1)}, f32[64]{0:T(128)}, u32[]{:S(2)}) copy-start(f32[64]{0:T(128)} %param.12) | copy-start | bytes 772
  4.5 5.0 %copy-start.8 = (f32[256,64]{0,1:T(8,128)S(1)}, f32[256,64]{0,1:T(8,128)}, u32[]{:S(2)}) copy-start(f32[256,64]{0,1:T(8,128)} %param.11) | copy-start | bytes 196612
  4.5 5.0 %copy-start.9 = (f32[256,64]{0,1:T(8,128)S(1)}, f32[256,64]{0,1:T(8,128)}, u32[]{:S(2)}) copy-start(f32[256,64]{0,1:T(8,128)} %param.10) | copy-start | bytes 196612
  4.5 5.1 %copy-start.6 = (bf16[64,3,4,8,128]{4,3,2,1,0:T(8,128)(2,1)S(1)}, bf16[64,3,4,8,128]{4,3,2,1,0:T(8,128)(2,1)}, u32[]{:S(2)}) copy-start(bf16[64,3,4,8,128]{4,3,2,1,0:T(8,128)(2,1)} %snaps_ref.2) | copy-start | bytes 4718596
  4.5 5.1 %copy-start.7 = (f32[16,4,8,128]{3,2,1,0:T(8,128)S(1)}, f32[16,4,8,128]{3,2,1,0:T(8,128)}, u32[]{:S(2)}) copy-start(f32[16,4,8,128]{3,2,1,0:T(8,128)} %coeff_ref.1) | copy-start | bytes 786436
  4.6 19.9 %all-to-all-start.1 = ((bf16[4,24,64,128]{3,2,1,0:T(8,128)(2,1)}), bf16[4,24,64,128]{3,2,1,0:T(8,128)(2,1)S(1)}, u32[]{:S(2)}, u32[]{:S(2)}) async-start(bf16[4,24,64,128]{3,2,1,0:T(8,128)(2,1)} %shard_map.96), calls=%async_computation.1 | async-start | bytes 3145728 | tf_op jit(solution)/shard_map/all_to_all | solution.py:258
  14.4 1.2 %copy-start.5 = (bf16[4,24,64,128]{3,2,1,0:T(8,128)(2,1)}, bf16[4,24,64,128]{3,2,1,0:T(8,128)(2,1)S(1)}, u32[]{:S(2)}) copy-start(bf16[4,24,64,128]{3,2,1,0:T(8,128)(2,1)S(1)} %get-tuple-element.11) | copy-start | bytes 4718596
  24.4 26.6 %all-to-all-start = ((bf16[4,24,64,128]{3,2,1,0:T(8,128)(2,1)}), bf16[4,24,64,128]{3,2,1,0:T(8,128)(2,1)S(1)}, u32[]{:S(2)}, u32[]{:S(2)}) async-start(bf16[4,24,64,128]{3,2,1,0:T(8,128)(2,1)} %copy-done.5), calls=%async_computation | async-start | bytes 3145728 | tf_op jit(solution)/shard_map/all_to_all | solution.py:272
  28.5 20.2 %collective-permute-start = (bf16[6,64,128]{2,1,0:T(8,128)(2,1)S(1)}, bf16[6,64,128]{2,1,0:T(8,128)(2,1)S(1)}, u32[]{:S(2)}, u32[]{:S(2)}) collective-permute-start(bf16[6,64,128]{2,1,0:T(8,128)(2,1)S(1)} %get-tuple-element.15), channel_id=1, source_target_pairs={{0,4},{4,8},{8,12},{12,16},{16,20},{20,24},{24,28},{28,32},{32,36}... | collective-permute-start | bytes 294920 | tf_op jit(solution)/shard_map/ppermute | solution.py:280
  38.4 10.3 %collective-permute-start.1 = (bf16[6,64,128]{2,1,0:T(8,128)(2,1)S(1)}, bf16[6,64,128]{2,1,0:T(8,128)(2,1)S(1)}, u32[]{:S(2)}, u32[]{:S(2)}) collective-permute-start(bf16[6,64,128]{2,1,0:T(8,128)(2,1)S(1)} %get-tuple-element.16), channel_id=1, source_target_pairs={{4,0},{8,4},{12,8},{16,12},{20,16},{24,20},{28,24},{32,28},{36,32}... | collective-permute-start | bytes 294920 | tf_op jit(solution)/shard_map/ppermute | solution.py:281
  40.3 4.9 %collective-permute-start.2 = (bf16[64,128]{1,0:T(8,128)(2,1)S(1)}, bf16[64,128]{1,0:T(8,128)(2,1)S(1)}, u32[]{:S(2)}, u32[]{:S(2)}) collective-permute-start(bf16[64,128]{1,0:T(8,128)(2,1)S(1)} %get-tuple-element.17), channel_id=1, source_target_pairs={{0,1},{1,2},{2,3},{4,5},{5,6},{6,7},{8,9},{9,10},{10,11},{12,13},{... | collective-permute-start | bytes 49160 | tf_op jit(solution)/shard_map/ppermute | solution.py:282
  43.9 4.8 %collective-permute-start.3 = (bf16[64,128]{1,0:T(8,128)(2,1)S(1)}, bf16[64,128]{1,0:T(8,128)(2,1)S(1)}, u32[]{:S(2)}, u32[]{:S(2)}) collective-permute-start(bf16[64,128]{1,0:T(8,128)(2,1)S(1)} %get-tuple-element.18), channel_id=1, source_target_pairs={{1,0},{2,1},{3,2},{5,4},{6,5},{7,6},{9,8},{10,9},{11,10},{13,12},{... | collective-permute-start | bytes 49160 | tf_op jit(solution)/shard_map/ppermute | solution.py:283
  49.7 1.3 %copy-start.1 = (bf16[1024,1024]{1,0:T(8,128)(2,1)}, bf16[1024,1024]{1,0:T(8,128)(2,1)S(1)}, u32[]{:S(2)}) copy-start(bf16[1024,1024]{1,0:T(8,128)(2,1)S(1)} %shard_map.98.weighted_ref) | copy-start | bytes 6291460
  51.1 1.6 %copy-start.2 = (bf16[1024,1024]{1,0:T(8,128)(2,1)S(1)}, bf16[1024,1024]{1,0:T(8,128)(2,1)}, u32[]{:S(2)}) copy-start(bf16[1024,1024]{1,0:T(8,128)(2,1)} %copy-done.1) | copy-start | bytes 6291460
  52.7 6.3 %copy-start.10 = (s32[16]{0:T(128)S(1)}, s32[16]{0:T(128)}, u32[]{:S(2)}) copy-start(s32[16]{0:T(128)} %constant.20) | copy-start | bytes 196
  54.4 0.8 copy-start.3
  55.2 13.2 %all-to-all-start.2 = ((f32[8,128,128]{2,1,0:T(8,128)}), f32[8,128,128]{2,1,0:T(8,128)S(1)}, u32[]{:S(2)}, u32[]{:S(2)}) async-start(f32[8,128,128]{2,1,0:T(8,128)} %copy-done.3), calls=%async_computation.2 | async-start | bytes 1048576 | tf_op jit(solution)/shard_map/all_to_all | solution.py:297

commit v3 on v2

--- a/solution.py
+++ b/solution.py
@@ -28,6 +28,7 @@
 SPACE = ("z", "y", "core")
 CHUNKS = 8
 LIMIT = 24 * 1024 * 1024
+WHOLE = 60 * 1024 * 1024
 
 
 def mode_weight(factor, singular):
@@ -38,27 +39,42 @@
 GROUP = NZ // SNAP
 
 
-def spread_tiles(snaps_ref, out_ref):
-    for comp in range(COMPONENTS):
-        for x in range(4):
-            rows = jnp.swapaxes(snaps_ref[:, comp, x], 0, 1)
-            for half in range(2):
-                group = [rows[half * 4 + i] for i in range(4)]
-                for quarter in range(SNAP):
-                    at = quarter * GROUP
-                    out_ref[quarter, comp * TILES + x * 2 + half] = jnp.concatenate(
-                        [row[:, at : at + GROUP] for row in group], axis=1
-                    )
-
-
-def direct_kernel(snaps_ref, out_ref):
-    spread_tiles(snaps_ref, out_ref)
+def spread_rows(layer, out_ref, first):
+    rows = jnp.swapaxes(layer, 0, 1)
+    for half in range(2):
+        group = [rows[half * 4 + i] for i in range(4)]
+        for quarter in range(SNAP):
+            at = quarter * GROUP
+            out_ref[quarter, first + half] = jnp.concatenate(
+                [row[:, at : at + GROUP] for row in group], axis=1
+            )
+
+
+def direct_kernel(snaps_ref, out_ref, raw, spread, arrived, sent):
+    pieces = [(comp, x) for comp in range(COMPONENTS) for x in range(4)]
+    arrivals = [
+        pltpu.make_async_copy(snaps_ref.at[:, comp, x], raw.at[n], arrived.at[n])
+        for n, (comp, x) in enumerate(pieces)
+    ]
+    for copy in arrivals:
+        copy.start()
+    departures = []
+    for n, (comp, x) in enumerate(pieces):
+        arrivals[n].wait()
+        spread_rows(raw[n], spread, 2 * n)
+        tiles = pl.ds(2 * n, 2)
+        departures.append(pltpu.make_async_copy(spread.at[:, tiles], out_ref.at[:, tiles], sent.at[n]))
+        departures[-1].start()
+    for copy in departures:
+        copy.wait()
 
 
 def adjoint_kernel(
     snap_ref, snaps_ref, left_ref, right_ref, coeff_ref, out_ref, left_out, right_out, coeff_out
 ):
-    spread_tiles(snaps_ref, out_ref)
+    for comp in range(COMPONENTS):
+        for x in range(4):
+            spread_rows(snaps_ref[:, comp, x], out_ref, comp * TILES + x * 2)
     left_out[...] = left_ref[...]
     right_out[...] = right_ref[...]
     shift = lax.rem(NZ - GROUP * snap_ref[0], NZ)
@@ -81,11 +97,16 @@
     )
 
 
-def modes_kernel(snaps_ref, weight_ref, out_ref, first_ref, last_ref, low_ref, high_ref):
+def modes_kernel(
+    odd_ref, snaps_ref, weight_ref, out_ref, x_near_ref, x_far_ref, z_near_ref, z_far_ref
+):
+    x_odd = odd_ref[0] == 1
+    z_odd = odd_ref[1] == 1
     weight = weight_ref[...]
     place = lax.rem(lax.broadcasted_iota(jnp.int32, (R, NZ), 1), GROUP)
     low = jnp.zeros((R, NZ), jnp.float32)
     high = jnp.zeros((R, NZ), jnp.float32)
+    first, last = [], []
     for comp in range(COMPONENTS):
         for t in range(0, TILES, 2):
             block = columns(snaps_ref, comp, (t, t + 1))
@@ -96,25 +117,36 @@
                 index = comp * TILES + t + half
                 out_ref[index] = tile
                 if t == 0:
-                    first_ref[comp * 2 + half] = tile
+                    first.append(tile)
                 if t == TILES - 2:
-                    last_ref[comp * 2 + half] = tile
+                    last.append(tile)
                 wide = tile.astype(jnp.float32)
                 edge = jnp.where(place == 0, wide, 0.0)
                 low = low + (pltpu.roll(edge, index, 1) if index else edge)
                 edge = jnp.where(place == GROUP - 1, wide, 0.0)
                 high = high + pltpu.roll(edge, NZ + index - (GROUP - 1), 1)
-    low_ref[...] = low.astype(jnp.bfloat16)
-    high_ref[...] = high.astype(jnp.bfloat16)
+    z_near_ref[...] = jnp.where(z_odd, low, high).astype(jnp.bfloat16)
+    z_far_ref[...] = jnp.where(z_odd, high, low).astype(jnp.bfloat16)
+    for n in range(6):
+        x_near_ref[n] = jnp.where(x_odd, first[n], last[n])
+        x_far_ref[n] = jnp.where(x_odd, last[n], first[n])
 
 
 def weighted_kernel(
-    modes_ref, before_ref, after_ref, below_ref, above_ref, coeff_ref, out_ref
+    odd_ref, modes_ref, x_near_ref, x_far_ref, z_near_ref, z_far_ref, coeff_ref, out_ref
 ):
     lane = lax.broadcasted_iota(jnp.int32, (R, NZ), 1)
     place = lax.rem(lane, GROUP)
-    below = below_ref[...].astype(jnp.float32)
-    above = above_ref[...].astype(jnp.float32)
+    x_odd = odd_ref[0] == 1
+    z_odd = odd_ref[1] == 1
+    z_near = z_near_ref[...].astype(jnp.float32)
+    z_far = z_far_ref[...].astype(jnp.float32)
+    below = jnp.where(z_odd, z_near, z_far)
+    above = jnp.where(z_odd, z_far, z_near)
+    x_near = [x_near_ref[n].astype(jnp.float32) for n in range(6)]
+    x_far = [x_far_ref[n].astype(jnp.float32) for n in range(6)]
+    before = [jnp.where(x_odd, near, far) for near, far in zip(x_near, x_far)]
+    after = [jnp.where(x_odd, far, near) for near, far in zip(x_near, x_far)]
     base = [0]
     for members in MEMBERS:
         base.append(base[-1] + len(members) * R)
@@ -130,8 +162,8 @@
 
     for comp in range(COMPONENTS):
         field = [modes_ref[comp * TILES + t].astype(jnp.float32) for t in range(TILES)]
-        down = [before_ref[comp * 2 + h].astype(jnp.float32) for h in range(2)] + field[:-2]
-        up = field[2:] + [after_ref[comp * 2 + h].astype(jnp.float32) for h in range(2)]
+        down = before[comp * 2 : comp * 2 + 2] + field[:-2]
+        up = field[2:] + after[comp * 2 : comp * 2 + 2]
         for x in range(4):
             pair = field[2 * x : 2 * x + 2]
             ahead = [pltpu.roll(v, NZ - GROUP, 1) for v in pair]
@@ -173,7 +205,25 @@
                     put(q, t, value)
 
 
-def products_kernel(scale, adjoint_ref, direct_ref, weight_ref, weighted_ref, out_ref, gram_ref, parts_ref):
+def products_kernel(
+    scale,
+    adjoint_ref,
+    direct_ref,
+    weight_ref,
+    weighted_hbm,
+    out_hbm,
+    gram_ref,
+    parts_ref,
+    weighted_ref,
+    out_ref,
+    sems,
+):
+    fetch = pltpu.make_async_copy(weighted_hbm, weighted_ref, sems.at[2])
+    fetch.start()
+    stores = [
+        pltpu.make_async_copy(out_ref.at[:, rows], out_hbm.at[:, rows], sems.at[n])
+        for n, rows in enumerate((pl.ds(0, 64), pl.ds(64, 64)))
+    ]
     transposed = (((1,), (1,)), ((), ()))
     weight = weight_ref[...]
     gram = jnp.zeros((M, M), jnp.float32)
@@ -202,8 +252,10 @@
                 for t in range(2)
             ]
             out_ref[core * SNAP + snap, :64, :] = jnp.concatenate(halves, axis=1)
+    stores[0].start()
     blocks = []
     row = 0
+    fetch.wait()
     for target, members in enumerate(MEMBERS):
         count = len(members) * R
         product = lax.dot_general(
@@ -227,17 +279,23 @@
                 rows = own[(2 * w + core) * 8 : (2 * w + core + 1) * 8]
                 out_ref[core * SNAP + snap, 64 + w * 8 : 64 + w * 8 + 8, :] = rows[:, :NZ]
                 out_ref[core * SNAP + snap, 96 + w * 8 : 96 + w * 8 + 8, :] = rows[:, NZ:]
-
-
-def call(kernel, out_shape, flops, moved, scratch=(), smem=0):
+    stores[1].start()
+    for store in stores:
+        store.wait()
+
+
+def call(kernel, out_shape, flops, moved, scratch=(), inputs=None, outputs=None, limit=LIMIT):
     def run(*operands):
-        spaces = [pltpu.SMEM] * smem + [pltpu.VMEM] * (len(operands) - smem)
+        spaces = dict.fromkeys(range(len(operands)), pltpu.VMEM) | (inputs or {})
+        results = pl.BlockSpec(memory_space=outputs or pltpu.VMEM)
+        several = isinstance(out_shape, tuple)
         return pl.pallas_call(
             kernel,
             out_shape=out_shape,
-            in_specs=[pl.BlockSpec(memory_space=space) for space in spaces],
+            in_specs=[pl.BlockSpec(memory_space=space) for space in spaces.values()],
+            out_specs=[results] * len(out_shape) if several else results,
             scratch_shapes=list(scratch),
-            compiler_params=pltpu.CompilerParams(vmem_limit_bytes=LIMIT),
+            compiler_params=pltpu.CompilerParams(vmem_limit_bytes=limit),
             cost_estimate=pl.CostEstimate(flops=flops, bytes_accessed=moved, transcendentals=0),
         )(*operands)
 
@@ -254,7 +312,21 @@
         return jax.ShapeDtypeStruct(dims, dtype)
 
     spread_shape = shape(SNAP, tiles, COLS, NZ)
-    ready = call(direct_kernel, spread_shape, 0, 3 << 20)(direct_snaps)
+    ready = call(
+        direct_kernel,
+        spread_shape,
+        0,
+        3 << 20,
+        (
+            pltpu.VMEM((12, COLS, NY, NZ), jnp.bfloat16),
+            pltpu.VMEM((SNAP, tiles, COLS, NZ), jnp.bfloat16),
+            pltpu.SemaphoreType.DMA((12,)),
+            pltpu.SemaphoreType.DMA((12,)),
+        ),
+        {0: pl.ANY},
+        pl.ANY,
+        WHOLE,
+    )(direct_snaps)
     direct = lax.all_to_all(ready, "snap", 0, 0, tiled=True)
     here = lax.axis_index("snap").astype(jnp.int32).reshape(1)
     ready, adjoint_weight, direct_weight, coeff = call(
@@ -267,33 +339,48 @@
         ),
         0,
         3 << 20,
-        smem=1,
+        inputs={0: pltpu.SMEM},
     )(here, adjoint_snaps, left, right, term_coeff)
     adjoint = lax.all_to_all(ready, "snap", 0, 0, tiled=True)
-    modes, first, last, low, high = call(
+    odd = jnp.stack([lax.axis_index("core"), lax.axis_index("snap") % 2]).astype(jnp.int32)
+    modes, *edges = call(
         modes_kernel,
         (shape(tiles, R, NZ), shape(6, R, NZ), shape(6, R, NZ), shape(R, NZ), shape(R, NZ)),
         2 * R * M * 3 * CELLS,
         2 << 20,
-    )(direct, direct_weight)
-    slabs, quarters = ([(i, i + 1) for i in range(n - 1)] for n in (128, SNAP))
-    before = lax.ppermute(last, SPACE, slabs)
-    after = lax.ppermute(first, SPACE, [(j, i) for i, j in slabs])
-    below = lax.ppermute(high, "snap", quarters)
-    above = lax.ppermute(low, "snap", [(j, i) for i, j in quarters])
-    weighted = call(weighted_kernel, shape(TERMS * R, CELLS), 1 << 26, 3 << 20)(
-        modes, before, after, below, above, coeff
-    )
+        inputs={0: pltpu.SMEM},
+    )(odd, direct, direct_weight)
+
+    def swap(array, axis, count, start):
+        pairs = [(i, i + 1) for i in range(start, count - 1, 2)]
+        return lax.ppermute(array, axis, pairs + [(j, i) for i, j in pairs])
+
+    x_near = swap(edges[0], SPACE, 128, 0)
+    z_near = swap(edges[2], "snap", SNAP, 0)
+    x_far = swap(edges[1], SPACE, 128, 1)
+    z_far = swap(edges[3], "snap", SNAP, 1)
+    weighted = call(
+        weighted_kernel,
+        pltpu.HBM((TERMS * R, CELLS), jnp.bfloat16),
+        1 << 26,
+        3 << 20,
+        inputs={0: pltpu.SMEM},
+    )(odd, modes, x_near, x_far, z_near, z_far, coeff)
     terms = call(
         functools.partial(products_kernel, scale),
-        jax.ShapeDtypeStruct((CHUNKS, 128, NZ), jnp.float32),
+        pltpu.HBM((CHUNKS, 128, NZ), jnp.float32),
         1 << 30,
         6 << 20,
         (
             pltpu.VMEM((2, M, NZ), jnp.float32),
             pltpu.VMEM((COMPONENTS, 3 * R, CELLS), jnp.bfloat16),
+            pltpu.VMEM((TERMS * R, CELLS), jnp.bfloat16),
+            pltpu.VMEM((CHUNKS, 128, NZ), jnp.float32),
+            pltpu.SemaphoreType.DMA((3,)),
         ),
-    )(adjoint, direct, adjoint_weight, weighted)
+        {3: pltpu.HBM},
+        pltpu.HBM,
+    )(adjoint, direct, adjoint_weight, pltpu.with_memory_space_constraint(weighted, pltpu.HBM))
     near = lax.all_to_all(terms, ("core", "snap"), 0, 0, tiled=True).sum(axis=0)
     gram = near[:64]
     operators = near[64:].reshape(2, 4, 8, 8, OWN).transpose(0, 3, 1, 2, 4).reshape(TERMS, 4 * NZ)

time: 103 us -> 103 us (level)
  Pallas kernels: 10.4 us -> 16.4 us
  local copies, waits for them, and re-layouts: 8.64 us -> 3.55 us
  waiting for transfers between devices: 21 us -> 17.7 us
  starting transfers between devices: 29 us -> 31.5 us
    pallas_call x5, Pallas kernels: 10.4 us -> 16.4 us  [run(): pl.pallas_call(kernel, out_shape=out_shape, in_specs=[pl.BlockSpec(memory...]
    unnamed x24 -> x14, local copies, waits for them, and re-layouts: 6.3 us -> 1.2 us
    all_to_all x1, starting transfers between devices: 3.78 us -> 6.91 us  [shards(): near = lax.all_to_all(terms, ('core', 'snap'), 0, 0, tiled=True).sum(axis=0)]
    ppermute x4, waiting for transfers between devices: 3.48 us -> 0.99 us  [swap(): return lax.ppermute(array, axis, pairs + [(j, i) for i, j in pairs])]
  transfers between devices with their start and end apart: 7 -> 7, of which waited for: 3 -> 3; matrix products, arithmetic and copies ran while one was open for 1% -> 2% of each run, Pallas kernels for 6% -> 8%
where the time goes in v3:
time: 103 us
  starting transfers between devices  31.5 us (31%)
  blocking collectives  31.5 us (31%)
  waiting for transfers between devices  17.7 us (17%)
  Pallas kernels  16.4 us (16%)
  local copies, waits for them, and re-layouts  3.55 us (3%)
  other arithmetic  1.18 us (1%)
    all_to_all x1, blocking collectives, shards(): final = lax.all_to_all(owned, ('z', 'y'), 0, 0, tiled=True).sum(axis=0)  31.5 us
    pallas_call x5, Pallas kernels, run(): pl.pallas_call(kernel, out_shape=out_shape, in_specs=[pl.BlockSpec(memory...  16.4 us
    ppermute x4, starting transfers between devices, swap(): return lax.ppermute(array, axis, pairs + [(j, i) for i, j in pairs])  16.1 us
    all_to_all x1, waiting for transfers between devices, shards(): near = lax.all_to_all(terms, ('core', 'snap'), 0, 0, tiled=True).sum(axis=0)  8.69 us
    all_to_all x1, waiting for transfers between devices, shards(): direct = lax.all_to_all(ready, 'snap', 0, 0, tiled=True)  7.98 us
    all_to_all x1, starting transfers between devices, shards(): near = lax.all_to_all(terms, ('core', 'snap'), 0, 0, tiled=True).sum(axis=0)  6.91 us
    all_to_all x1, starting transfers between devices, shards(): direct = lax.all_to_all(ready, 'snap', 0, 0, tiled=True)  4.99 us
    all_to_all x1, starting transfers between devices, shards(): adjoint = lax.all_to_all(ready, 'snap', 0, 0, tiled=True)  3.56 us
  transfers between devices with their start and end apart: 7, of which 3 were waited for; matrix products, arithmetic and copies ran while one was open for 2% of the time, Pallas kernels for 8%

profile of v3, /device:TPU:1, one launch (start us, length us, event | category | flops | bytes accessed | tf_op | source)
XLA Modules:
  0.0 102.8 jit_solution(4058329459333899500)
XLA Ops:
  0.6 0.0 copy-start
  0.6 4.1 %shard_map.96 = bf16[4,24,64,128]{3,2,1,0:T(8,128)(2,1)} custom-call(bf16[64,3,4,8,128]{4,3,2,1,0:T(8,128)(2,1)} %snaps_ref.3), custom_call_target="tpu_custom_call" | custom-call | bytes 3145728 | tf_op jit(solution)/shard_map/pallas_call | solution.py:292
  4.7 0.0 copy-start.6
  4.7 0.0 copy-start.2
  4.8 0.0 copy-start.3
  4.8 5.0 %all-to-all-start.1 = ((bf16[4,24,64,128]{3,2,1,0:T(8,128)(2,1)}), bf16[4,24,64,128]{3,2,1,0:T(8,128)(2,1)S(1)}, u32[]{:S(2)}, u32[]{:S(2)}) async-start(bf16[4,24,64,128]{3,2,1,0:T(8,128)(2,1)} %shard_map.96), calls=%async_computation.1 | async-start | bytes 3145728 | tf_op jit(solution)/shard_map/all_to_all | solution.py:330
  9.8 0.9 fusion.1
  10.7 4.7 %shard_map.95 = (bf16[4,24,64,128]{3,2,1,0:T(8,128)(2,1)S(1)}, bf16[64,256]{1,0:T(8,128)(2,1)S(1)}, bf16[64,256]{1,0:T(8,128)(2,1)S(1)}, f32[16,8,128]{2,1,0:T(8,128)S(1)}) custom-call(s32[1]{0:T(128)} %bitcast.snap_ref, bf16[64,3,4,8,128]{4,3,2,1,0:T(8,128)(2,1)S(1)} %copy-done.2, bf16[64,256]{1,0:T(8,128)(2,1)S(1)} %get-tuple-element.25.left_ref, ...), custom_call_target="tpu_custom_call" | custom-call | bytes 3145728 | tf_op jit(solution)/shard_map/pallas_call | solution.py:292
  15.5 1.2 %copy-done.1 = bf16[4,24,64,128]{3,2,1,0:T(8,128)(2,1)} copy-done((bf16[4,24,64,128]{3,2,1,0:T(8,128)(2,1)}, bf16[4,24,64,128]{3,2,1,0:T(8,128)(2,1)S(1)}, u32[]{:S(2)}) %copy-start.1) | copy-done | bytes 1572888
  16.7 8.0 %all-to-all-done.1.snaps_ref.direct_ref = bf16[4,24,64,128]{3,2,1,0:T(8,128)(2,1)S(1)} async-done(((bf16[4,24,64,128]{3,2,1,0:T(8,128)(2,1)}), bf16[4,24,64,128]{3,2,1,0:T(8,128)(2,1)S(1)}, u32[]{:S(2)}, u32[]{:S(2)}) %all-to-all-start.1) | async-done | bytes 1572896 | tf_op jit(solution)/shard_map/all_to_all | solution.py:330
  24.6 3.6 %all-to-all-start = ((bf16[4,24,64,128]{3,2,1,0:T(8,128)(2,1)}), bf16[4,24,64,128]{3,2,1,0:T(8,128)(2,1)S(1)}, u32[]{:S(2)}, u32[]{:S(2)}) async-start(bf16[4,24,64,128]{3,2,1,0:T(8,128)(2,1)} %copy-done.1), calls=%async_computation | async-start | bytes 3145728 | tf_op jit(solution)/shard_map/all_to_all | solution.py:344
  28.2 0.1 pad_add_fusion.odd_ref
  28.3 1.0 %shard_map.97 = (bf16[24,64,128]{2,1,0:T(8,128)(2,1)S(1)}, bf16[6,64,128]{2,1,0:T(8,128)(2,1)S(1)}, bf16[6,64,128]{2,1,0:T(8,128)(2,1)S(1)}, bf16[64,128]{1,0:T(8,128)(2,1)S(1)}, bf16[64,128]{1,0:T(8,128)(2,1)S(1)}) custom-call(s32[2]{0:T(128)S(1)} %pad_add_fusion.odd_ref, bf16[4,24,64,128]{3,2,1,0:T(8,128)(2,1)S(1)} %all-to-all-done.1.snaps_ref.direct_ref, ...), custom_call_target="tpu_custom_call" | custom-call | flops 100663296 | bytes 2097152 | tf_op jit(solution)/shard_map/pallas_call | solution.py:292
  29.3 8.7 %collective-permute-start = (bf16[6,64,128]{2,1,0:T(8,128)(2,1)S(1)}, bf16[6,64,128]{2,1,0:T(8,128)(2,1)S(1)}, u32[]{:S(2)}, u32[]{:S(2)}) collective-permute-start(bf16[6,64,128]{2,1,0:T(8,128)(2,1)S(1)} %get-tuple-element.15), channel_id=1, source_target_pairs={{0,4},{8,12},{16,20},{24,28},{32,36},{40,44},{48,52},{56,60},{64,6... | collective-permute-start | bytes 294920 | tf_op jit(solution)/shard_map/ppermute | solution.py:356
  38.0 3.1 %collective-permute-start.1 = (bf16[6,64,128]{2,1,0:T(8,128)(2,1)S(1)}, bf16[6,64,128]{2,1,0:T(8,128)(2,1)S(1)}, u32[]{:S(2)}, u32[]{:S(2)}) collective-permute-start(bf16[6,64,128]{2,1,0:T(8,128)(2,1)S(1)} %get-tuple-element.16), channel_id=1, source_target_pairs={{4,8},{12,16},{20,24},{28,32},{36,40},{44,48},{52,56},{60,64},{68,... | collective-permute-start | bytes 294920 | tf_op jit(solution)/shard_map/ppermute | solution.py:356
  41.2 3.6 %collective-permute-start.2 = (bf16[64,128]{1,0:T(8,128)(2,1)S(1)}, bf16[64,128]{1,0:T(8,128)(2,1)S(1)}, u32[]{:S(2)}, u32[]{:S(2)}) collective-permute-start(bf16[64,128]{1,0:T(8,128)(2,1)S(1)} %get-tuple-element.17), channel_id=1, source_target_pairs={{0,1},{2,3},{1,0},{3,2},{4,5},{6,7},{5,4},{7,6},{8,9},{10,11},{9,8... | collective-permute-start | bytes 49160 | tf_op jit(solution)/shard_map/ppermute | solution.py:356
  44.8 0.7 collective-permute-start.3
  45.4 1.0 collective-permute-done.2.z_near_ref
  46.4 2.9 %shard_map.98.weighted_hbm = bf16[1024,1024]{1,0:T(8,128)(2,1)} custom-call(s32[2]{0:T(128)S(1)} %pad_add_fusion.odd_ref, bf16[24,64,128]{2,1,0:T(8,128)(2,1)S(1)} %get-tuple-element.14.modes_ref, bf16[6,64,128]{2,1,0:T(8,128)(2,1)S(1)} %collective-permute-done.x_near_ref, bf16[6,64,128]{2,1,0:T(8,128)(2,1)S(1)} %collective-permute-done.1.x_far_ref, ...), custom_call_target="tpu_custom_call" | custom-call | flops 67108864 | bytes 3145728 | tf_op jit(solution)/shard_map/pallas_call | solution.py:292
  49.3 3.6 %shard_map.99 = f32[8,128,128]{2,1,0:T(8,128)} custom-call(bf16[4,24,64,128]{3,2,1,0:T(8,128)(2,1)S(1)} %all-to-all-done.adjoint_ref, bf16[4,24,64,128]{3,2,1,0:T(8,128)(2,1)S(1)} %all-to-all-done.1.snaps_ref.direct_ref, bf16[64,256]{1,0:T(8,128)(2,1)S(1)} %get-tuple-element.12.weight_ref, bf16[1024,1024]{1,0:T(8,128)(2,1)} %shard_map.98.weighted_hbm), custom_call_target="tpu_custom_call" | custom-call | flops 1073741824 | bytes 6291456 | tf_op jit(solution)/shard_map/pallas_call | solution.py:292
  53.0 6.9 %all-to-all-start.2 = ((f32[8,128,128]{2,1,0:T(8,128)}), f32[8,128,128]{2,1,0:T(8,128)S(1)}, u32[]{:S(2)}, u32[]{:S(2)}) async-start(f32[8,128,128]{2,1,0:T(8,128)} %shard_map.99), calls=%async_computation.2 | async-start | bytes 1048576 | tf_op jit(solution)/shard_map/all_to_all | solution.py:384
  59.9 0.7 gather_fusion
  60.6 8.7 %all-to-all-done.2 = f32[8,128,128]{2,1,0:T(8,128)S(1)} async-done(((f32[8,128,128]{2,1,0:T(8,128)}), f32[8,128,128]{2,1,0:T(8,128)S(1)}, u32[]{:S(2)}, u32[]{:S(2)}) %all-to-all-start.2) | async-done | bytes 524320 | tf_op jit(solution)/shard_map/all_to_all | solution.py:384
  69.3 0.1 reshape.16
  69.4 0.1 copy.11
  69.5 0.2 reshape.17
  69.7 0.1 fusion.2
  69.8 0.1 pad_maximum_fusion
  69.9 31.5 %all_to_all.20 = f32[64,2,128]{2,1,0:T(2,128)S(1)} all-to-all(f32[64,2,128]{2,1,0:T(2,128)S(1)} %pad_maximum_fusion), channel_id=1, replica_groups=mesh['z'=8,'y'=8,'core'=2,'snap'=4] {'z','y'}, dimensions={0} | all-to-all | bytes 131072 | tf_op jit(solution)/shard_map/all_to_all | solution.py:392
  101.4 0.1 reduce_sum.19
  101.5 0.6 reshape_squeeze.6
  102.1 0.7 reshape_squeeze.7
  (19 shorter events, 0.1 us)
Async XLA Ops:
  0.6 59.3 %copy-start = (s32[16]{0:T(128)S(1)}, s32[16]{0:T(128)}, u32[]{:S(2)}) copy-start(s32[16]{0:T(128)} %param.14) | copy-start | bytes 196
  4.7 5.0 %copy-start.6 = (f32[64]{0:T(128)S(1)}, f32[64]{0:T(128)}, u32[]{:S(2)}) copy-start(f32[64]{0:T(128)} %param.12) | copy-start | bytes 772
  4.7 5.0 %copy-start.4 = (f32[256,64]{0,1:T(8,128)S(1)}, f32[256,64]{0,1:T(8,128)}, u32[]{:S(2)}) copy-start(f32[256,64]{0,1:T(8,128)} %param.11) | copy-start | bytes 196612
  4.7 6.0 %copy-start.2 = (bf16[64,3,4,8,128]{4,3,2,1,0:T(8,128)(2,1)S(1)}, bf16[64,3,4,8,128]{4,3,2,1,0:T(8,128)(2,1)}, u32[]{:S(2)}) copy-start(bf16[64,3,4,8,128]{4,3,2,1,0:T(8,128)(2,1)} %snaps_ref.2) | copy-start | bytes 4718596
  4.8 6.0 %copy-start.3 = (f32[16,4,8,128]{3,2,1,0:T(8,128)S(1)}, f32[16,4,8,128]{3,2,1,0:T(8,128)}, u32[]{:S(2)}) copy-start(f32[16,4,8,128]{3,2,1,0:T(8,128)} %coeff_ref.1) | copy-start | bytes 786436
  4.8 19.9 %all-to-all-start.1 = ((bf16[4,24,64,128]{3,2,1,0:T(8,128)(2,1)}), bf16[4,24,64,128]{3,2,1,0:T(8,128)(2,1)S(1)}, u32[]{:S(2)}, u32[]{:S(2)}) async-start(bf16[4,24,64,128]{3,2,1,0:T(8,128)(2,1)} %shard_map.96), calls=%async_computation.1 | async-start | bytes 3145728 | tf_op jit(solution)/shard_map/all_to_all | solution.py:330
  15.5 1.2 %copy-start.1 = (bf16[4,24,64,128]{3,2,1,0:T(8,128)(2,1)}, bf16[4,24,64,128]{3,2,1,0:T(8,128)(2,1)S(1)}, u32[]{:S(2)}) copy-start(bf16[4,24,64,128]{3,2,1,0:T(8,128)(2,1)S(1)} %get-tuple-element.11) | copy-start | bytes 4718596
  24.6 24.7 %all-to-all-start = ((bf16[4,24,64,128]{3,2,1,0:T(8,128)(2,1)}), bf16[4,24,64,128]{3,2,1,0:T(8,128)(2,1)S(1)}, u32[]{:S(2)}, u32[]{:S(2)}) async-start(bf16[4,24,64,128]{3,2,1,0:T(8,128)(2,1)} %copy-done.1), calls=%async_computation | async-start | bytes 3145728 | tf_op jit(solution)/shard_map/all_to_all | solution.py:344
  29.3 17.1 %collective-permute-start = (bf16[6,64,128]{2,1,0:T(8,128)(2,1)S(1)}, bf16[6,64,128]{2,1,0:T(8,128)(2,1)S(1)}, u32[]{:S(2)}, u32[]{:S(2)}) collective-permute-start(bf16[6,64,128]{2,1,0:T(8,128)(2,1)S(1)} %get-tuple-element.15), channel_id=1, source_target_pairs={{0,4},{8,12},{16,20},{24,28},{32,36},{40,44},{48,52},{56,60},{64,6... | collective-permute-start | bytes 294920 | tf_op jit(solution)/shard_map/ppermute | solution.py:356
  38.0 8.4 %collective-permute-start.1 = (bf16[6,64,128]{2,1,0:T(8,128)(2,1)S(1)}, bf16[6,64,128]{2,1,0:T(8,128)(2,1)S(1)}, u32[]{:S(2)}, u32[]{:S(2)}) collective-permute-start(bf16[6,64,128]{2,1,0:T(8,128)(2,1)S(1)} %get-tuple-element.16), channel_id=1, source_target_pairs={{4,8},{12,16},{20,24},{28,32},{36,40},{44,48},{52,56},{60,64},{68,... | collective-permute-start | bytes 294920 | tf_op jit(solution)/shard_map/ppermute | solution.py:356
  41.2 5.3 %collective-permute-start.2 = (bf16[64,128]{1,0:T(8,128)(2,1)S(1)}, bf16[64,128]{1,0:T(8,128)(2,1)S(1)}, u32[]{:S(2)}, u32[]{:S(2)}) collective-permute-start(bf16[64,128]{1,0:T(8,128)(2,1)S(1)} %get-tuple-element.17), channel_id=1, source_target_pairs={{0,1},{2,3},{1,0},{3,2},{4,5},{6,7},{5,4},{7,6},{8,9},{10,11},{9,8... | collective-permute-start | bytes 49160 | tf_op jit(solution)/shard_map/ppermute | solution.py:356
  44.8 1.7 %collective-permute-start.3 = (bf16[64,128]{1,0:T(8,128)(2,1)S(1)}, bf16[64,128]{1,0:T(8,128)(2,1)S(1)}, u32[]{:S(2)}, u32[]{:S(2)}) collective-permute-start(bf16[64,128]{1,0:T(8,128)(2,1)S(1)} %get-tuple-element.18), channel_id=1, source_target_pairs={{1,2},{2,1},{5,6},{6,5},{9,10},{10,9},{13,14},{14,13},{17,18},{18,... | collective-permute-start | bytes 49160 | tf_op jit(solution)/shard_map/ppermute | solution.py:356
  49.3 10.6 %copy-start.5 = (s32[16]{0:T(128)S(1)}, s32[16]{0:T(128)}, u32[]{:S(2)}) copy-start(s32[16]{0:T(128)} %constant.37) | copy-start | bytes 196
  53.0 16.3 %all-to-all-start.2 = ((f32[8,128,128]{2,1,0:T(8,128)}), f32[8,128,128]{2,1,0:T(8,128)S(1)}, u32[]{:S(2)}, u32[]{:S(2)}) async-start(f32[8,128,128]{2,1,0:T(8,128)} %shard_map.99), calls=%async_computation.2 | async-start | bytes 1048576 | tf_op jit(solution)/shard_map/all_to_all | solution.py:384

commit v4 on v3

--- a/solution.py
+++ b/solution.py
@@ -27,6 +27,7 @@
 OWN = R // SNAP
 SPACE = ("z", "y", "core")
 CHUNKS = 8
+PIECES = 4
 LIMIT = 24 * 1024 * 1024
 WHOLE = 60 * 1024 * 1024
 
@@ -39,31 +40,35 @@
 GROUP = NZ // SNAP
 
 
-def spread_rows(layer, out_ref, first):
+def spread_rows(layer, out_ref, first, at):
     rows = jnp.swapaxes(layer, 0, 1)
     for half in range(2):
         group = [rows[half * 4 + i] for i in range(4)]
         for quarter in range(SNAP):
-            at = quarter * GROUP
-            out_ref[quarter, first + half] = jnp.concatenate(
-                [row[:, at : at + GROUP] for row in group], axis=1
+            lanes = slice(quarter * GROUP, (quarter + 1) * GROUP)
+            out_ref[quarter, first + half, at : at + layer.shape[0]] = jnp.concatenate(
+                [row[:, lanes] for row in group], axis=1
             )
 
 
 def direct_kernel(snaps_ref, out_ref, raw, spread, arrived, sent):
-    pieces = [(comp, x) for comp in range(COMPONENTS) for x in range(4)]
+    count = COLS // PIECES
+    parts = [pl.ds(n * count, count) for n in range(PIECES)]
     arrivals = [
-        pltpu.make_async_copy(snaps_ref.at[:, comp, x], raw.at[n], arrived.at[n])
-        for n, (comp, x) in enumerate(pieces)
+        pltpu.make_async_copy(snaps_ref.at[part], raw.at[part], arrived.at[n])
+        for n, part in enumerate(parts)
     ]
     for copy in arrivals:
         copy.start()
     departures = []
-    for n, (comp, x) in enumerate(pieces):
+    for n, part in enumerate(parts):
         arrivals[n].wait()
-        spread_rows(raw[n], spread, 2 * n)
-        tiles = pl.ds(2 * n, 2)
-        departures.append(pltpu.make_async_copy(spread.at[:, tiles], out_ref.at[:, tiles], sent.at[n]))
+        for comp in range(COMPONENTS):
+            for x in range(4):
+                spread_rows(raw[part, comp, x], spread, comp * TILES + x * 2, n * count)
+        departures.append(
+            pltpu.make_async_copy(spread.at[:, :, part], out_ref.at[:, :, part], sent.at[n])
+        )
         departures[-1].start()
     for copy in departures:
         copy.wait()
@@ -74,7 +79,7 @@
 ):
     for comp in range(COMPONENTS):
         for x in range(4):
-            spread_rows(snaps_ref[:, comp, x], out_ref, comp * TILES + x * 2)
+            spread_rows(snaps_ref[:, comp, x], out_ref, comp * TILES + x * 2, 0)
     left_out[...] = left_ref[...]
     right_out[...] = right_ref[...]
     shift = lax.rem(NZ - GROUP * snap_ref[0], NZ)
@@ -132,11 +137,97 @@
         x_far_ref[n] = jnp.where(x_odd, last[n], first[n])
 
 
-def weighted_kernel(
-    odd_ref, modes_ref, x_near_ref, x_far_ref, z_near_ref, z_far_ref, coeff_ref, out_ref
-):
+def weighted_terms(comp, modes_ref, before, after, below, above, coeff_ref, out_ref):
     lane = lax.broadcasted_iota(jnp.int32, (R, NZ), 1)
     place = lax.rem(lane, GROUP)
+    base = [0]
+    for members in MEMBERS:
+        base.append(base[-1] + len(members) * R)
+
+    def put(q, t, value):
+        target = target_comp[q]
+        count = len(MEMBERS[target])
+        at = MEMBERS[target].index(q)
+        value = (value * coeff_ref[q, t : t + 1, :]).astype(jnp.bfloat16)
+        for block in range(SNAP):
+            row = base[target] + (block * count + at) * OWN
+            out_ref[row : row + OWN, t * NZ : (t + 1) * NZ] = value[block * OWN : (block + 1) * OWN]
+
+    field = [modes_ref[comp * TILES + t].astype(jnp.float32) for t in range(TILES)]
+    down = before[comp * 2 : comp * 2 + 2] + field[:-2]
+    up = field[2:] + after[comp * 2 : comp * 2 + 2]
+    for x in range(4):
+        pair = field[2 * x : 2 * x + 2]
+        ahead = [pltpu.roll(v, NZ - GROUP, 1) for v in pair]
+        behind = [pltpu.roll(v, GROUP, 1) for v in pair]
+        for half in range(2):
+            t = 2 * x + half
+            index = comp * TILES + t
+            center = pair[half]
+            x_up, x_down = up[t], down[t]
+            y_up = jnp.where(lane >= NZ - GROUP, ahead[1] if half == 0 else 0.0, ahead[half])
+            y_down = jnp.where(lane < GROUP, behind[0] if half == 1 else 0.0, behind[half])
+            z_up = jnp.where(
+                place == GROUP - 1,
+                pltpu.roll(above, GROUP - 1 - index, 1),
+                pltpu.roll(center, NZ - 1, 1),
+            )
+            z_down = jnp.where(
+                place == 0,
+                pltpu.roll(below, NZ - index, 1) if index else below,
+                pltpu.roll(center, 1, 1),
+            )
+            for q in range(TERMS):
+                if source_comp[q] != comp:
+                    continue
+                kind = stencil_kind[q]
+                if kind == 0:
+                    value = center
+                elif kind == 1:
+                    value = 0.5 * (x_up - x_down)
+                elif kind == 2:
+                    value = 0.5 * (y_up - y_down)
+                elif kind == 3:
+                    value = 0.5 * (z_up - z_down)
+                else:
+                    beside = x_up + x_down
+                    beside = beside + y_up + y_down
+                    beside = beside + z_up + z_down
+                    value = beside - 6.0 * center
+                put(q, t, value)
+
+
+def products_kernel(
+    scale,
+    odd_ref,
+    adjoint_ref,
+    direct_ref,
+    *refs,
+):
+    sources, (out_hbm, gram_ref, parts_ref, weighted_ref, out_ref, *held, sems, fetched) = refs[:7], refs[7:]
+    fetches = [
+        pltpu.make_async_copy(source, target, fetched.at[n])
+        for n, (source, target) in enumerate(zip(sources, held))
+    ]
+    for fetch in fetches:
+        fetch.start()
+    weight_ref, modes_ref, x_near_ref, x_far_ref, z_near_ref, z_far_ref, coeff_ref = held
+    stores = [
+        pltpu.make_async_copy(out_ref.at[:, rows], out_hbm.at[:, rows], sems.at[n])
+        for n, rows in enumerate((pl.ds(0, 64), pl.ds(64, 64)))
+    ]
+    transposed = (((1,), (1,)), ((), ()))
+    gram = jnp.zeros((M, M), jnp.float32)
+    for comp in range(COMPONENTS):
+        for t in range(0, TILES, 2):
+            gram = gram + lax.dot_general(
+                columns(direct_ref, comp, (t, t + 1)),
+                columns(adjoint_ref, comp, (t, t + 1)),
+                transposed,
+                preferred_element_type=jnp.float32,
+            )
+    for fetch in fetches:
+        fetch.wait()
     x_odd = odd_ref[0] == 1
     z_odd = odd_ref[1] == 1
     z_near = z_near_ref[...].astype(jnp.float32)
@@ -147,93 +238,10 @@
     x_far = [x_far_ref[n].astype(jnp.float32) for n in range(6)]
     before = [jnp.where(x_odd, near, far) for near, far in zip(x_near, x_far)]
     after = [jnp.where(x_odd, far, near) for near, far in zip(x_near, x_far)]
-    base = [0]
-    for members in MEMBERS:
-        base.append(base[-1] + len(members) * R)
-
-    def put(q, t, value):
-        target = target_comp[q]
-        count = len(MEMBERS[target])
-        at = MEMBERS[target].index(q)
-        value = (value * coeff_ref[q, t : t + 1, :]).astype(jnp.bfloat16)
-        for block in range(SNAP):
-            row = base[target] + (block * count + at) * OWN
-            out_ref[row : row + OWN, t * NZ : (t + 1) * NZ] = value[block * OWN : (block + 1) * OWN]
-
-    for comp in range(COMPONENTS):
-        field = [modes_ref[comp * TILES + t].astype(jnp.float32) for t in range(TILES)]
-        down = before[comp * 2 : comp * 2 + 2] + field[:-2]
-        up = field[2:] + after[comp * 2 : comp * 2 + 2]
-        for x in range(4):
-            pair = field[2 * x : 2 * x + 2]
-            ahead = [pltpu.roll(v, NZ - GROUP, 1) for v in pair]
-            behind = [pltpu.roll(v, GROUP, 1) for v in pair]
-            for half in range(2):
-                t = 2 * x + half
-                index = comp * TILES + t
-                center = pair[half]
-                x_up, x_down = up[t], down[t]
-                y_up = jnp.where(lane >= NZ - GROUP, ahead[1] if half == 0 else 0.0, ahead[half])
-                y_down = jnp.where(lane < GROUP, behind[0] if half == 1 else 0.0, behind[half])
-                z_up = jnp.where(
-                    place == GROUP - 1,
-                    pltpu.roll(above, GROUP - 1 - index, 1),
-                    pltpu.roll(center, NZ - 1, 1),
-                )
-                z_down = jnp.where(
-                    place == 0,
-                    pltpu.roll(below, NZ - index, 1) if index else below,
-                    pltpu.roll(center, 1, 1),
-                )
-                for q in range(TERMS):
-                    if source_comp[q] != comp:
-                        continue
-                    kind = stencil_kind[q]
-                    if kind == 0:
-                        value = center
-                    elif kind == 1:
-                        value = 0.5 * (x_up - x_down)
-                    elif kind == 2:
-                        value = 0.5 * (y_up - y_down)
-                    elif kind == 3:
-                        value = 0.5 * (z_up - z_down)
-                    else:
-                        beside = x_up + x_down
-                        beside = beside + y_up + y_down
-                        beside = beside + z_up + z_down
-                        value = beside - 6.0 * center
-                    put(q, t, value)
-
-
-def products_kernel(
-    scale,
-    adjoint_ref,
-    direct_ref,
-    weight_ref,
-    weighted_hbm,
-    out_hbm,
-    gram_ref,
-    parts_ref,
-    weighted_ref,
-    out_ref,
-    sems,
-):
-    fetch = pltpu.make_async_copy(weighted_hbm, weighted_ref, sems.at[2])
-    fetch.start()
-    stores = [
-        pltpu.make_async_copy(out_ref.at[:, rows], out_hbm.at[:, rows], sems.at[n])
-        for n, rows in enumerate((pl.ds(0, 64), pl.ds(64, 64)))
-    ]
-    transposed = (((1,), (1,)), ((), ()))
     weight = weight_ref[...]
-    gram = jnp.zeros((M, M), jnp.float32)
     for comp in range(COMPONENTS):
         for t in range(0, TILES, 2):
             adjoint = columns(adjoint_ref, comp, (t, t + 1))
-            direct = columns(direct_ref, comp, (t, t + 1))
-            gram = gram + lax.dot_general(
-                direct, adjoint, transposed, preferred_element_type=jnp.float32
-            )
             modes = jnp.dot(weight, adjoint, preferred_element_type=jnp.float32)
             high = modes.astype(jnp.bfloat16)
             rest = modes - high.astype(jnp.float32)
@@ -241,6 +249,7 @@
             low = (rest - middle.astype(jnp.float32)).astype(jnp.bfloat16)
             for part, value in enumerate((high, middle, low)):
                 parts_ref[comp, part * R : (part + 1) * R, t * NZ : (t + 2) * NZ] = value
+        weighted_terms(comp, modes_ref, before, after, below, above, coeff_ref, weighted_ref)
     gram = gram * scale
     gram_ref[0] = gram[:, :NZ]
     gram_ref[1] = gram[:, NZ:]
@@ -255,7 +264,6 @@
     stores[0].start()
     blocks = []
     row = 0
-    fetch.wait()
     for target, members in enumerate(MEMBERS):
         count = len(members) * R
         product = lax.dot_general(
@@ -284,6 +292,14 @@
         store.wait()
 
 
+def finish_kernel(sums_ref, gram_ref, reduced_ref):
+    total = jnp.sum(sums_ref[...], axis=0)
+    gram_ref[...] = jnp.concatenate([total[0:1, :COLS], total[0:1, COLS:]], axis=0)
+    reduced_ref[...] = jnp.concatenate(
+        [total[1:2, v * OWN : (v + 1) * OWN] for v in range(8)], axis=0
+    )
+
+
 def call(kernel, out_shape, flops, moved, scratch=(), inputs=None, outputs=None, limit=LIMIT):
     def run(*operands):
         spaces = dict.fromkeys(range(len(operands)), pltpu.VMEM) | (inputs or {})
@@ -314,17 +330,17 @@
     spread_shape = shape(SNAP, tiles, COLS, NZ)
     ready = call(
         direct_kernel,
-        spread_shape,
+        pltpu.HBM(spread_shape.shape, jnp.bfloat16),
         0,
         3 << 20,
         (
-            pltpu.VMEM((12, COLS, NY, NZ), jnp.bfloat16),
+            pltpu.VMEM(direct_snaps.shape, jnp.bfloat16),
             pltpu.VMEM((SNAP, tiles, COLS, NZ), jnp.bfloat16),
-            pltpu.SemaphoreType.DMA((12,)),
-            pltpu.SemaphoreType.DMA((12,)),
+            pltpu.SemaphoreType.DMA((PIECES,)),
+            pltpu.SemaphoreType.DMA((PIECES,)),
         ),
         {0: pl.ANY},
-        pl.ANY,
+        pltpu.HBM,
         WHOLE,
     )(direct_snaps)
     direct = lax.all_to_all(ready, "snap", 0, 0, tiled=True)
@@ -333,9 +349,9 @@
         adjoint_kernel,
         (
             spread_shape,
-            shape(R, M),
-            shape(R, M),
-            shape(TERMS, TILES, NZ, dtype=jnp.float32),
+            pltpu.HBM((R, M), jnp.bfloat16),
+            pltpu.HBM((R, M), jnp.bfloat16),
+            pltpu.HBM((TERMS, TILES, NZ), jnp.float32),
         ),
         0,
         3 << 20,
@@ -359,13 +375,10 @@
     z_near = swap(edges[2], "snap", SNAP, 0)
     x_far = swap(edges[1], SPACE, 128, 1)
     z_far = swap(edges[3], "snap", SNAP, 1)
-    weighted = call(
-        weighted_kernel,
-        pltpu.HBM((TERMS * R, CELLS), jnp.bfloat16),
-        1 << 26,
-        3 << 20,
-        inputs={0: pltpu.SMEM},
-    )(odd, modes, x_near, x_far, z_near, z_far, coeff)
+    adjoint_weight, coeff = (
+        pltpu.with_memory_space_constraint(array, pltpu.HBM) for array in (adjoint_weight, coeff)
+    )
+    fetched = (adjoint_weight, modes, x_near, x_far, z_near, z_far, coeff)
     terms = call(
         functools.partial(products_kernel, scale),
         pltpu.HBM((CHUNKS, 128, NZ), jnp.float32),
@@ -376,11 +389,13 @@
             pltpu.VMEM((COMPONENTS, 3 * R, CELLS), jnp.bfloat16),
             pltpu.VMEM((TERMS * R, CELLS), jnp.bfloat16),
             pltpu.VMEM((CHUNKS, 128, NZ), jnp.float32),
-            pltpu.SemaphoreType.DMA((3,)),
+            *(pltpu.VMEM(array.shape, array.dtype) for array in fetched),
+            pltpu.SemaphoreType.DMA((2,)),
+            pltpu.SemaphoreType.DMA((len(fetched),)),
         ),
-        {3: pltpu.HBM},
+        {0: pltpu.SMEM} | dict.fromkeys(range(3, 3 + len(fetched)), pl.ANY),
         pltpu.HBM,
-    )(adjoint, direct, adjoint_weight, pltpu.with_memory_space_constraint(weighted, pltpu.HBM))
+    )(odd, adjoint, direct, *fetched)
     near = lax.all_to_all(terms, ("core", "snap"), 0, 0, tiled=True).sum(axis=0)
     gram = near[:64]
     operators = near[64:].reshape(2, 4, 8, 8, OWN).transpose(0, 3, 1, 2, 4).reshape(TERMS, 4 * NZ)
@@ -389,8 +404,10 @@
     ).astype(jnp.float32)
     ordered = jnp.dot(selector, operators, precision=lax.Precision.HIGHEST)
     owned = jnp.stack([gram, ordered.reshape(64, NZ)], axis=1)
-    final = lax.all_to_all(owned, ("z", "y"), 0, 0, tiled=True).sum(axis=0)
-    return (final[0].reshape(2, COLS).T, final[1].reshape(8, OWN))
+    sums = lax.all_to_all(owned, ("z", "y"), 0, 0, tiled=True)
+    outs = (shape(2, COLS, dtype=jnp.float32), shape(8, OWN, dtype=jnp.float32))
+    gram, reduced = call(finish_kernel, outs, 0, 1 << 16)(sums)
+    return (gram.T, reduced)
 
 
 def solution(mesh):

time: 103 us -> 101 us (0.981)
    another operation x2 -> x0, local copies, waits for them, and re-layouts: 1.32 us -> none  [shards(): return (final[0].reshape(2, COLS).T, final[1].reshape(8, OWN))]
  transfers between devices with their start and end apart: 7 -> 7, of which waited for: 3 -> 3; matrix products, arithmetic and copies ran while one was open for 2% -> 1% of each run, Pallas kernels for 8% -> 7%
where the time goes in v4:
time: 101 us
  starting transfers between devices  32.2 us (32%)
  blocking collectives  30.6 us (30%)
  waiting for transfers between devices  17.5 us (17%)
  Pallas kernels  16.2 us (16%)
  local copies, waits for them, and re-layouts  3.02 us (3%)
    all_to_all x1, blocking collectives, shards(): sums = lax.all_to_all(owned, ('z', 'y'), 0, 0, tiled=True)  30.6 us
    ppermute x4, starting transfers between devices, swap(): return lax.ppermute(array, axis, pairs + [(j, i) for i, j in pairs])  16.7 us
    pallas_call x5, Pallas kernels, run(): pl.pallas_call(kernel, out_shape=out_shape, in_specs=[pl.BlockSpec(memory...  16.2 us
    all_to_all x1, waiting for transfers between devices, shards(): near = lax.all_to_all(terms, ('core', 'snap'), 0, 0, tiled=True).sum(axis=0)  8.69 us
    all_to_all x1, waiting for transfers between devices, shards(): direct = lax.all_to_all(ready, 'snap', 0, 0, tiled=True)  8.2 us
    all_to_all x1, starting transfers between devices, shards(): near = lax.all_to_all(terms, ('core', 'snap'), 0, 0, tiled=True).sum(axis=0)  7.01 us
    all_to_all x1, starting transfers between devices, shards(): direct = lax.all_to_all(ready, 'snap', 0, 0, tiled=True)  4.99 us
    all_to_all x1, starting transfers between devices, shards(): adjoint = lax.all_to_all(ready, 'snap', 0, 0, tiled=True)  3.56 us
  transfers between devices with their start and end apart: 7, of which 3 were waited for; matrix products, arithmetic and copies ran while one was open for 1% of the time, Pallas kernels for 7%

profile of v4, /device:TPU:1, one launch (start us, length us, event | category | flops | bytes accessed | tf_op | source)
XLA Modules:
  0.0 100.8 jit_solution(2148316407466214965)
XLA Ops:
  0.6 0.0 copy-start
  0.6 3.4 %shard_map.96 = bf16[4,24,64,128]{3,2,1,0:T(8,128)(2,1)} custom-call(bf16[64,3,4,8,128]{4,3,2,1,0:T(8,128)(2,1)} %snaps_ref.3), custom_call_target="tpu_custom_call" | custom-call | bytes 3145728 | tf_op jit(solution)/shard_map/pallas_call | solution.py:308
  4.1 0.0 copy-start.8
  4.1 0.0 copy-start.5
  4.1 0.0 copy-start.6
  4.1 0.0 copy-start.2
  4.1 5.0 %all-to-all-start.1 = ((bf16[4,24,64,128]{3,2,1,0:T(8,128)(2,1)}), bf16[4,24,64,128]{3,2,1,0:T(8,128)(2,1)S(1)}, u32[]{:S(2)}, u32[]{:S(2)}) async-start(bf16[4,24,64,128]{3,2,1,0:T(8,128)(2,1)} %shard_map.96), calls=%async_computation.1 | async-start | bytes 3145728 | tf_op jit(solution)/shard_map/all_to_all | solution.py:346
  9.1 0.1 fusion.1
  9.2 5.4 %shard_map.95 = (bf16[4,24,64,128]{3,2,1,0:T(8,128)(2,1)S(1)}, bf16[64,256]{1,0:T(8,128)(2,1)}, bf16[64,256]{1,0:T(8,128)(2,1)}, f32[16,8,128]{2,1,0:T(8,128)}) custom-call(s32[1]{0:T(128)} %bitcast.2.snap_ref, bf16[64,3,4,8,128]{4,3,2,1,0:T(8,128)(2,1)S(1)} %copy-done.2, bf16[64,256]{1,0:T(8,128)(2,1)S(1)} %get-tuple-element.27.left_ref, ...), custom_call_target="tpu_custom_call" | custom-call | bytes 3145728 | tf_op jit(solution)/shard_map/pallas_call | solution.py:308
  14.6 1.2 %copy-done.1 = bf16[4,24,64,128]{3,2,1,0:T(8,128)(2,1)} copy-done((bf16[4,24,64,128]{3,2,1,0:T(8,128)(2,1)}, bf16[4,24,64,128]{3,2,1,0:T(8,128)(2,1)S(1)}, u32[]{:S(2)}) %copy-start.1) | copy-done | bytes 1572888
  15.8 8.2 %all-to-all-done.1.snaps_ref.direct_ref = bf16[4,24,64,128]{3,2,1,0:T(8,128)(2,1)S(1)} async-done(((bf16[4,24,64,128]{3,2,1,0:T(8,128)(2,1)}), bf16[4,24,64,128]{3,2,1,0:T(8,128)(2,1)S(1)}, u32[]{:S(2)}, u32[]{:S(2)}) %all-to-all-start.1) | async-done | bytes 1572896 | tf_op jit(solution)/shard_map/all_to_all | solution.py:346
  24.0 3.6 %all-to-all-start = ((bf16[4,24,64,128]{3,2,1,0:T(8,128)(2,1)}), bf16[4,24,64,128]{3,2,1,0:T(8,128)(2,1)S(1)}, u32[]{:S(2)}, u32[]{:S(2)}) async-start(bf16[4,24,64,128]{3,2,1,0:T(8,128)(2,1)} %copy-done.1), calls=%async_computation | async-start | bytes 3145728 | tf_op jit(solution)/shard_map/all_to_all | solution.py:360
  27.6 0.1 pad_add_fusion.odd_ref
  27.6 0.8 copy-done.4
  28.4 1.7 %shard_map.97 = (bf16[24,64,128]{2,1,0:T(8,128)(2,1)S(1)}, bf16[6,64,128]{2,1,0:T(8,128)(2,1)}, bf16[6,64,128]{2,1,0:T(8,128)(2,1)}, bf16[64,128]{1,0:T(8,128)(2,1)}, bf16[64,128]{1,0:T(8,128)(2,1)}) custom-call(s32[2]{0:T(128)S(1)} %pad_add_fusion.odd_ref, bf16[4,24,64,128]{3,2,1,0:T(8,128)(2,1)S(1)} %all-to-all-done.1.snaps_ref.direct_ref, ...), custom_call_target="tpu_custom_call" | custom-call | flops 100663296 | bytes 2097152 | tf_op jit(solution)/shard_map/pallas_call | solution.py:308
  30.1 8.7 %collective-permute-start = (bf16[6,64,128]{2,1,0:T(8,128)(2,1)}, bf16[6,64,128]{2,1,0:T(8,128)(2,1)}, u32[]{:S(2)}, u32[]{:S(2)}) collective-permute-start(bf16[6,64,128]{2,1,0:T(8,128)(2,1)} %get-tuple-element.17), channel_id=1, source_target_pairs={{0,4},{8,12},{16,20},{24,28},{32,36},{40,44},{48,52},{56,60},{64,6... | collective-permute-start | bytes 294920 | tf_op jit(solution)/shard_map/ppermute | solution.py:372
  38.8 3.1 %collective-permute-start.1 = (bf16[6,64,128]{2,1,0:T(8,128)(2,1)}, bf16[6,64,128]{2,1,0:T(8,128)(2,1)}, u32[]{:S(2)}, u32[]{:S(2)}) collective-permute-start(bf16[6,64,128]{2,1,0:T(8,128)(2,1)} %get-tuple-element.18), channel_id=1, source_target_pairs={{4,8},{12,16},{20,24},{28,32},{36,40},{44,48},{52,56},{60,64},{68,... | collective-permute-start | bytes 294920 | tf_op jit(solution)/shard_map/ppermute | solution.py:372
  41.9 3.6 %collective-permute-start.2 = (bf16[64,128]{1,0:T(8,128)(2,1)}, bf16[64,128]{1,0:T(8,128)(2,1)}, u32[]{:S(2)}, u32[]{:S(2)}) collective-permute-start(bf16[64,128]{1,0:T(8,128)(2,1)} %get-tuple-element.19), channel_id=1, source_target_pairs={{0,1},{2,3},{1,0},{3,2},{4,5},{6,7},{5,4},{7,6},{8,9},{10,11},{9,8... | collective-permute-start | bytes 49160 | tf_op jit(solution)/shard_map/ppermute | solution.py:372
  45.5 1.3 %collective-permute-start.3 = (bf16[64,128]{1,0:T(8,128)(2,1)}, bf16[64,128]{1,0:T(8,128)(2,1)}, u32[]{:S(2)}, u32[]{:S(2)}) collective-permute-start(bf16[64,128]{1,0:T(8,128)(2,1)} %get-tuple-element.20), channel_id=1, source_target_pairs={{1,2},{2,1},{5,6},{6,5},{9,10},{10,9},{13,14},{14,13},{17,18},{18,... | collective-permute-start | bytes 49160 | tf_op jit(solution)/shard_map/ppermute | solution.py:372
  46.7 0.6 collective-permute-done.2.refs_4_
  47.3 0.0 copy-start.7
  47.4 5.1 %shard_map.98 = f32[8,128,128]{2,1,0:T(8,128)} custom-call(s32[2]{0:T(128)S(1)} %pad_add_fusion.odd_ref, bf16[4,24,64,128]{3,2,1,0:T(8,128)(2,1)S(1)} %all-to-all-done.adjoint_ref, bf16[4,24,64,128]{3,2,1,0:T(8,128)(2,1)S(1)} %all-to-all-done.1.snaps_ref.direct_ref, bf16[64,256]{1,0:T(8,128)(2,1)} %get-tuple-element.14.refs_0_, ...), custom_call_target="tpu_custom_call" | custom-call | flops 1073741824 | bytes 6291456 | tf_op jit(solution)/shard_map/pallas_call | solution.py:308
  52.4 7.0 %all-to-all-start.2 = ((f32[8,128,128]{2,1,0:T(8,128)}), f32[8,128,128]{2,1,0:T(8,128)S(1)}, u32[]{:S(2)}, u32[]{:S(2)}) async-start(f32[8,128,128]{2,1,0:T(8,128)} %shard_map.98), calls=%async_computation.2 | async-start | bytes 1048576 | tf_op jit(solution)/shard_map/all_to_all | solution.py:399
  59.5 0.7 gather_fusion
  60.1 8.7 %all-to-all-done.2 = f32[8,128,128]{2,1,0:T(8,128)S(1)} async-done(((f32[8,128,128]{2,1,0:T(8,128)}), f32[8,128,128]{2,1,0:T(8,128)S(1)}, u32[]{:S(2)}, u32[]{:S(2)}) %all-to-all-start.2) | async-done | bytes 524320 | tf_op jit(solution)/shard_map/all_to_all | solution.py:399
  68.8 0.1 reshape.16
  69.0 0.1 copy.12
  69.0 0.2 reshape.17
  69.2 0.1 fusion.2
  69.4 0.1 pad_maximum_fusion
  69.5 30.6 %all_to_all.20.sums_ref = f32[64,2,128]{2,1,0:T(2,128)S(1)} all-to-all(f32[64,2,128]{2,1,0:T(2,128)S(1)} %pad_maximum_fusion), channel_id=1, replica_groups=mesh['z'=8,'y'=8,'core'=2,'snap'=4] {'z','y'}, dimensions={0} | all-to-all | bytes 131072 | tf_op jit(solution)/shard_map/all_to_all | solution.py:407
  100.0 0.7 shard_map.99
  (19 shorter events, 0.1 us)
Async XLA Ops:
  0.6 58.8 %copy-start = (s32[16]{0:T(128)S(1)}, s32[16]{0:T(128)}, u32[]{:S(2)}) copy-start(s32[16]{0:T(128)} %param.14) | copy-start | bytes 196
  4.1 5.0 %copy-start.8 = (f32[64]{0:T(128)S(1)}, f32[64]{0:T(128)}, u32[]{:S(2)}) copy-start(f32[64]{0:T(128)} %param.12) | copy-start | bytes 772
  4.1 5.0 %copy-start.5 = (f32[256,64]{0,1:T(8,128)S(1)}, f32[256,64]{0,1:T(8,128)}, u32[]{:S(2)}) copy-start(f32[256,64]{0,1:T(8,128)} %param.11) | copy-start | bytes 196612
  4.1 5.0 %copy-start.6 = (f32[256,64]{0,1:T(8,128)S(1)}, f32[256,64]{0,1:T(8,128)}, u32[]{:S(2)}) copy-start(f32[256,64]{0,1:T(8,128)} %param.10) | copy-start | bytes 196612
  4.1 5.1 %copy-start.2 = (bf16[64,3,4,8,128]{4,3,2,1,0:T(8,128)(2,1)S(1)}, bf16[64,3,4,8,128]{4,3,2,1,0:T(8,128)(2,1)}, u32[]{:S(2)}) copy-start(bf16[64,3,4,8,128]{4,3,2,1,0:T(8,128)(2,1)} %snaps_ref.2) | copy-start | bytes 4718596
  4.1 5.1 %copy-start.3 = (f32[16,4,8,128]{3,2,1,0:T(8,128)S(1)}, f32[16,4,8,128]{3,2,1,0:T(8,128)}, u32[]{:S(2)}) copy-start(f32[16,4,8,128]{3,2,1,0:T(8,128)} %coeff_ref.1) | copy-start | bytes 786436
  4.1 19.9 %all-to-all-start.1 = ((bf16[4,24,64,128]{3,2,1,0:T(8,128)(2,1)}), bf16[4,24,64,128]{3,2,1,0:T(8,128)(2,1)S(1)}, u32[]{:S(2)}, u32[]{:S(2)}) async-start(bf16[4,24,64,128]{3,2,1,0:T(8,128)(2,1)} %shard_map.96), calls=%async_computation.1 | async-start | bytes 3145728 | tf_op jit(solution)/shard_map/all_to_all | solution.py:346
  14.6 1.2 %copy-start.1 = (bf16[4,24,64,128]{3,2,1,0:T(8,128)(2,1)}, bf16[4,24,64,128]{3,2,1,0:T(8,128)(2,1)S(1)}, u32[]{:S(2)}) copy-start(bf16[4,24,64,128]{3,2,1,0:T(8,128)(2,1)S(1)} %get-tuple-element.13) | copy-start | bytes 4718596
  24.0 22.8 %all-to-all-start = ((bf16[4,24,64,128]{3,2,1,0:T(8,128)(2,1)}), bf16[4,24,64,128]{3,2,1,0:T(8,128)(2,1)S(1)}, u32[]{:S(2)}, u32[]{:S(2)}) async-start(bf16[4,24,64,128]{3,2,1,0:T(8,128)(2,1)} %copy-done.1), calls=%async_computation | async-start | bytes 3145728 | tf_op jit(solution)/shard_map/all_to_all | solution.py:360
  27.6 0.8 copy-start.4
  30.1 17.3 %collective-permute-start = (bf16[6,64,128]{2,1,0:T(8,128)(2,1)}, bf16[6,64,128]{2,1,0:T(8,128)(2,1)}, u32[]{:S(2)}, u32[]{:S(2)}) collective-permute-start(bf16[6,64,128]{2,1,0:T(8,128)(2,1)} %get-tuple-element.17), channel_id=1, source_target_pairs={{0,4},{8,12},{16,20},{24,28},{32,36},{40,44},{48,52},{56,60},{64,6... | collective-permute-start | bytes 294920 | tf_op jit(solution)/shard_map/ppermute | solution.py:372
  38.8 8.6 %collective-permute-start.1 = (bf16[6,64,128]{2,1,0:T(8,128)(2,1)}, bf16[6,64,128]{2,1,0:T(8,128)(2,1)}, u32[]{:S(2)}, u32[]{:S(2)}) collective-permute-start(bf16[6,64,128]{2,1,0:T(8,128)(2,1)} %get-tuple-element.18), channel_id=1, source_target_pairs={{4,8},{12,16},{20,24},{28,32},{36,40},{44,48},{52,56},{60,64},{68,... | collective-permute-start | bytes 294920 | tf_op jit(solution)/shard_map/ppermute | solution.py:372
  41.9 5.5 %collective-permute-start.2 = (bf16[64,128]{1,0:T(8,128)(2,1)}, bf16[64,128]{1,0:T(8,128)(2,1)}, u32[]{:S(2)}, u32[]{:S(2)}) collective-permute-start(bf16[64,128]{1,0:T(8,128)(2,1)} %get-tuple-element.19), channel_id=1, source_target_pairs={{0,1},{2,3},{1,0},{3,2},{4,5},{6,7},{5,4},{7,6},{8,9},{10,11},{9,8... | collective-permute-start | bytes 49160 | tf_op jit(solution)/shard_map/ppermute | solution.py:372
  45.5 1.9 %collective-permute-start.3 = (bf16[64,128]{1,0:T(8,128)(2,1)}, bf16[64,128]{1,0:T(8,128)(2,1)}, u32[]{:S(2)}, u32[]{:S(2)}) collective-permute-start(bf16[64,128]{1,0:T(8,128)(2,1)} %get-tuple-element.20), channel_id=1, source_target_pairs={{1,2},{2,1},{5,6},{6,5},{9,10},{10,9},{13,14},{14,13},{17,18},{18,... | collective-permute-start | bytes 49160 | tf_op jit(solution)/shard_map/ppermute | solution.py:372
  47.3 12.1 %copy-start.7 = (s32[16]{0:T(128)S(1)}, s32[16]{0:T(128)}, u32[]{:S(2)}) copy-start(s32[16]{0:T(128)} %constant.37) | copy-start | bytes 196
  52.4 16.4 %all-to-all-start.2 = ((f32[8,128,128]{2,1,0:T(8,128)}), f32[8,128,128]{2,1,0:T(8,128)S(1)}, u32[]{:S(2)}, u32[]{:S(2)}) async-start(f32[8,128,128]{2,1,0:T(8,128)} %shard_map.98), calls=%async_computation.2 | async-start | bytes 1048576 | tf_op jit(solution)/shard_map/all_to_all | solution.py:399

commit v5 on v4

--- a/solution.py
+++ b/solution.py
@@ -38,6 +38,9 @@
 
 TILES = 8
 GROUP = NZ // SNAP
+WEIGHT_AT = COMPONENTS * TILES
+COEFF_AT = WEIGHT_AT + 2
+HELD = COEFF_AT + 2
 
 
 def spread_rows(layer, out_ref, first, at):
@@ -87,7 +90,8 @@
         for x in range(4):
             own = pltpu.roll(coeff_ref[q, x], shift, 1)
             for half in range(2):
-                coeff_out[q, x * 2 + half : x * 2 + half + 1, :] = jnp.concatenate(
+                row = q * TILES + x * 2 + half
+                coeff_out[row : row + 1, :] = jnp.concatenate(
                     [own[half * 4 + i : half * 4 + i + 1, :GROUP] for i in range(4)], axis=1
                 )
 
@@ -103,15 +107,24 @@
 
 
 def modes_kernel(
-    odd_ref, snaps_ref, weight_ref, out_ref, x_near_ref, x_far_ref, z_near_ref, z_far_ref
+    snaps_ref,
+    weight_ref,
+    adjoint_weight_ref,
+    coeff_ref,
+    held_ref,
+    first_ref,
+    last_ref,
+    low_ref,
+    high_ref,
 ):
-    x_odd = odd_ref[0] == 1
-    z_odd = odd_ref[1] == 1
+    for n in range(2):
+        wide = adjoint_weight_ref[:, n * NZ : (n + 1) * NZ].astype(jnp.float32)
+        held_ref[WEIGHT_AT + n] = wide
+        held_ref[COEFF_AT + n] = coeff_ref[n * R : (n + 1) * R, :]
     weight = weight_ref[...]
     place = lax.rem(lax.broadcasted_iota(jnp.int32, (R, NZ), 1), GROUP)
     low = jnp.zeros((R, NZ), jnp.float32)
     high = jnp.zeros((R, NZ), jnp.float32)
-    first, last = [], []
     for comp in range(COMPONENTS):
         for t in range(0, TILES, 2):
             block = columns(snaps_ref, comp, (t, t + 1))
@@ -120,24 +133,21 @@
             for half in range(2):
                 tile = modes[:, half * NZ : (half + 1) * NZ]
                 index = comp * TILES + t + half
-                out_ref[index] = tile
+                wide = tile.astype(jnp.float32)
+                held_ref[index] = wide
                 if t == 0:
-                    first.append(tile)
+                    first_ref[comp * 2 + half] = tile
                 if t == TILES - 2:
-                    last.append(tile)
-                wide = tile.astype(jnp.float32)
+                    last_ref[comp * 2 + half] = tile
                 edge = jnp.where(place == 0, wide, 0.0)
                 low = low + (pltpu.roll(edge, index, 1) if index else edge)
                 edge = jnp.where(place == GROUP - 1, wide, 0.0)
                 high = high + pltpu.roll(edge, NZ + index - (GROUP - 1), 1)
-    z_near_ref[...] = jnp.where(z_odd, low, high).astype(jnp.bfloat16)
-    z_far_ref[...] = jnp.where(z_odd, high, low).astype(jnp.bfloat16)
-    for n in range(6):
-        x_near_ref[n] = jnp.where(x_odd, first[n], last[n])
-        x_far_ref[n] = jnp.where(x_odd, last[n], first[n])
-
-
-def weighted_terms(comp, modes_ref, before, after, below, above, coeff_ref, out_ref):
+    low_ref[...] = low.astype(jnp.bfloat16)
+    high_ref[...] = high.astype(jnp.bfloat16)
+
+
+def weighted_terms(comp, held_ref, before, after, below, above, out_ref):
     lane = lax.broadcasted_iota(jnp.int32, (R, NZ), 1)
     place = lax.rem(lane, GROUP)
     base = [0]
@@ -148,12 +158,14 @@
         target = target_comp[q]
         count = len(MEMBERS[target])
         at = MEMBERS[target].index(q)
-        value = (value * coeff_ref[q, t : t + 1, :]).astype(jnp.bfloat16)
+        row = (q * TILES + t) % R
+        coeff = held_ref[COEFF_AT + q * TILES // R, row : row + 1, :]
+        value = (value * coeff).astype(jnp.bfloat16)
         for block in range(SNAP):
             row = base[target] + (block * count + at) * OWN
             out_ref[row : row + OWN, t * NZ : (t + 1) * NZ] = value[block * OWN : (block + 1) * OWN]
 
-    field = [modes_ref[comp * TILES + t].astype(jnp.float32) for t in range(TILES)]
+    field = [held_ref[comp * TILES + t] for t in range(TILES)]
     down = before[comp * 2 : comp * 2 + 2] + field[:-2]
     up = field[2:] + after[comp * 2 : comp * 2 + 2]
     for x in range(4):
@@ -199,19 +211,23 @@
 
 def products_kernel(
     scale,
-    odd_ref,
     adjoint_ref,
     direct_ref,
-    *refs,
+    held_hbm,
+    before_ref,
+    after_ref,
+    below_ref,
+    above_ref,
+    out_hbm,
+    held_ref,
+    gram_ref,
+    parts_ref,
+    weighted_ref,
+    out_ref,
+    sems,
 ):
-    sources, (out_hbm, gram_ref, parts_ref, weighted_ref, out_ref, *held, sems, fetched) = refs[:7], refs[7:]
-    fetches = [
-        pltpu.make_async_copy(source, target, fetched.at[n])
-        for n, (source, target) in enumerate(zip(sources, held))
-    ]
-    for fetch in fetches:
-        fetch.start()
-    weight_ref, modes_ref, x_near_ref, x_far_ref, z_near_ref, z_far_ref, coeff_ref = held
+    fetch = pltpu.make_async_copy(held_hbm, held_ref, sems.at[2])
+    fetch.start()
     stores = [
         pltpu.make_async_copy(out_ref.at[:, rows], out_hbm.at[:, rows], sems.at[n])
         for n, rows in enumerate((pl.ds(0, 64), pl.ds(64, 64)))
@@ -226,19 +242,13 @@
                 transposed,
                 preferred_element_type=jnp.float32,
             )
-    for fetch in fetches:
-        fetch.wait()
-    x_odd = odd_ref[0] == 1
-    z_odd = odd_ref[1] == 1
-    z_near = z_near_ref[...].astype(jnp.float32)
-    z_far = z_far_ref[...].astype(jnp.float32)
-    below = jnp.where(z_odd, z_near, z_far)
-    above = jnp.where(z_odd, z_far, z_near)
-    x_near = [x_near_ref[n].astype(jnp.float32) for n in range(6)]
-    x_far = [x_far_ref[n].astype(jnp.float32) for n in range(6)]
-    before = [jnp.where(x_odd, near, far) for near, far in zip(x_near, x_far)]
-    after = [jnp.where(x_odd, far, near) for near, far in zip(x_near, x_far)]
-    weight = weight_ref[...]
+    fetch.wait()
+    below = below_ref[...].astype(jnp.float32)
+    above = above_ref[...].astype(jnp.float32)
+    before = [before_ref[n].astype(jnp.float32) for n in range(6)]
+    after = [after_ref[n].astype(jnp.float32) for n in range(6)]
+    weight = jnp.concatenate([held_ref[WEIGHT_AT], held_ref[WEIGHT_AT + 1]], axis=1)
+    weight = weight.astype(jnp.bfloat16)
     for comp in range(COMPONENTS):
         for t in range(0, TILES, 2):
             adjoint = columns(adjoint_ref, comp, (t, t + 1))
@@ -249,7 +259,7 @@
             low = (rest - middle.astype(jnp.float32)).astype(jnp.bfloat16)
             for part, value in enumerate((high, middle, low)):
                 parts_ref[comp, part * R : (part + 1) * R, t * NZ : (t + 2) * NZ] = value
-        weighted_terms(comp, modes_ref, before, after, below, above, coeff_ref, weighted_ref)
+        weighted_terms(comp, held_ref, before, after, below, above, weighted_ref)
     gram = gram * scale
     gram_ref[0] = gram[:, :NZ]
     gram_ref[1] = gram[:, NZ:]
@@ -351,51 +361,47 @@
             spread_shape,
             pltpu.HBM((R, M), jnp.bfloat16),
             pltpu.HBM((R, M), jnp.bfloat16),
-            pltpu.HBM((TERMS, TILES, NZ), jnp.float32),
+            pltpu.HBM((TERMS * TILES, NZ), jnp.float32),
         ),
         0,
         3 << 20,
         inputs={0: pltpu.SMEM},
     )(here, adjoint_snaps, left, right, term_coeff)
     adjoint = lax.all_to_all(ready, "snap", 0, 0, tiled=True)
-    odd = jnp.stack([lax.axis_index("core"), lax.axis_index("snap") % 2]).astype(jnp.int32)
-    modes, *edges = call(
+    held, first, last, low, high = call(
         modes_kernel,
-        (shape(tiles, R, NZ), shape(6, R, NZ), shape(6, R, NZ), shape(R, NZ), shape(R, NZ)),
+        (
+            pltpu.HBM((HELD, R, NZ), jnp.float32),
+            shape(6, R, NZ),
+            shape(6, R, NZ),
+            shape(R, NZ),
+            shape(R, NZ),
+        ),
         2 * R * M * 3 * CELLS,
         2 << 20,
-        inputs={0: pltpu.SMEM},
-    )(odd, direct, direct_weight)
-
-    def swap(array, axis, count, start):
-        pairs = [(i, i + 1) for i in range(start, count - 1, 2)]
-        return lax.ppermute(array, axis, pairs + [(j, i) for i, j in pairs])
-
-    x_near = swap(edges[0], SPACE, 128, 0)
-    z_near = swap(edges[2], "snap", SNAP, 0)
-    x_far = swap(edges[1], SPACE, 128, 1)
-    z_far = swap(edges[3], "snap", SNAP, 1)
-    adjoint_weight, coeff = (
-        pltpu.with_memory_space_constraint(array, pltpu.HBM) for array in (adjoint_weight, coeff)
-    )
-    fetched = (adjoint_weight, modes, x_near, x_far, z_near, z_far, coeff)
+    )(direct, direct_weight, adjoint_weight, coeff)
+    held = pltpu.with_memory_space_constraint(held, pltpu.HBM)
+    slabs, quarters = ([(i, i + 1) for i in range(n - 1)] for n in (128, SNAP))
+    before = lax.ppermute(last, SPACE, slabs)
+    after = lax.ppermute(first, SPACE, [(j, i) for i, j in slabs])
+    below = lax.ppermute(high, "snap", quarters)
+    above = lax.ppermute(low, "snap", [(j, i) for i, j in quarters])
     terms = call(
         functools.partial(products_kernel, scale),
         pltpu.HBM((CHUNKS, 128, NZ), jnp.float32),
         1 << 30,
         6 << 20,
         (
+            pltpu.VMEM((HELD, R, NZ), jnp.float32),
             pltpu.VMEM((2, M, NZ), jnp.float32),
             pltpu.VMEM((COMPONENTS, 3 * R, CELLS), jnp.bfloat16),
             pltpu.VMEM((TERMS * R, CELLS), jnp.bfloat16),
             pltpu.VMEM((CHUNKS, 128, NZ), jnp.float32),
-            *(pltpu.VMEM(array.shape, array.dtype) for array in fetched),
-            pltpu.SemaphoreType.DMA((2,)),
-            pltpu.SemaphoreType.DMA((len(fetched),)),
+            pltpu.SemaphoreType.DMA((3,)),
         ),
-        {0: pltpu.SMEM} | dict.fromkeys(range(3, 3 + len(fetched)), pl.ANY),
+        {2: pltpu.HBM},
         pltpu.HBM,
-    )(odd, adjoint, direct, *fetched)
+    )(adjoint, direct, held, before, after, below, above)
     near = lax.all_to_all(terms, ("core", "snap"), 0, 0, tiled=True).sum(axis=0)
     gram = near[:64]
     operators = near[64:].reshape(2, 4, 8, 8, OWN).transpose(0, 3, 1, 2, 4).reshape(TERMS, 4 * NZ)

time: 101 us -> 100 us (0.990)
  starting transfers between devices: 32.2 us -> 29.3 us
  waiting for transfers between devices: 17.5 us -> 20.2 us
  Pallas kernels: 16.2 us -> 14.7 us
  blocking collectives: 30.6 us -> 32 us
    all_to_all x1, starting transfers between devices: 7.01 us -> 3.99 us  [shards(): near = lax.all_to_all(terms, ('core', 'snap'), 0, 0, tiled=True).sum(axis=0)]
    ppermute x4, waiting for transfers between devices: 0.6 us -> 3.26 us  [the longest x1 3.25 us: shards(): above = lax.ppermute(low, 'snap', [(j, i) for i, j in quarters])]
    pallas_call x5, Pallas kernels: 16.2 us -> 14.7 us  [run(): pl.pallas_call(kernel, out_shape=out_shape, in_specs=[pl.BlockSpec(memory...]
    all_to_all x1, blocking collectives: 30.6 us -> 32 us  [shards(): sums = lax.all_to_all(owned, ('z', 'y'), 0, 0, tiled=True)]
where the time goes in v5:
time: 100 us; the launch traced here: 99.7 us
  blocking collectives  32 us (32%)
  starting transfers between devices  29.3 us (29%)
  waiting for transfers between devices  20.2 us (20%)
  Pallas kernels  14.7 us (15%)
  local copies, waits for them, and re-layouts  2.26 us (2%)
    all_to_all x1, blocking collectives, shards(): sums = lax.all_to_all(owned, ('z', 'y'), 0, 0, tiled=True)  32 us
    pallas_call x5, Pallas kernels, run(): pl.pallas_call(kernel, out_shape=out_shape, in_specs=[pl.BlockSpec(memory...  14.7 us
    ppermute x1, starting transfers between devices, shards(): before = lax.ppermute(last, SPACE, slabs)  9.87 us
    all_to_all x1, waiting for transfers between devices, shards(): near = lax.all_to_all(terms, ('core', 'snap'), 0, 0, tiled=True).sum(axis=0)  8.69 us
    all_to_all x1, waiting for transfers between devices, shards(): direct = lax.all_to_all(ready, 'snap', 0, 0, tiled=True)  8.22 us
    all_to_all x1, starting transfers between devices, shards(): direct = lax.all_to_all(ready, 'snap', 0, 0, tiled=True)  4.99 us
    all_to_all x1, starting transfers between devices, shards(): near = lax.all_to_all(terms, ('core', 'snap'), 0, 0, tiled=True).sum(axis=0)  3.99 us
    all_to_all x1, starting transfers between devices, shards(): adjoint = lax.all_to_all(ready, 'snap', 0, 0, tiled=True)  3.69 us
  transfers between devices with their start and end apart: 7, of which 3 were waited for; matrix products, arithmetic and copies ran while one was open for 1% of the time, Pallas kernels for 7%

profile of v5, /device:TPU:1, one launch (start us, length us, event | category | flops | bytes accessed | tf_op | source)
XLA Modules:
  0.0 99.7 jit_solution(10962266922646877843)
XLA Ops:
  0.6 0.0 copy-start
  0.6 3.4 %shard_map.96 = bf16[4,24,64,128]{3,2,1,0:T(8,128)(2,1)} custom-call(bf16[64,3,4,8,128]{4,3,2,1,0:T(8,128)(2,1)} %snaps_ref.3), custom_call_target="tpu_custom_call" | custom-call | bytes 3145728 | tf_op jit(solution)/shard_map/pallas_call | solution.py:318
  4.0 0.0 copy-start.10
  4.1 0.0 copy-start.7
  4.1 0.0 copy-start.8
  4.1 0.0 copy-start.2
  4.1 0.0 copy-start.3
  4.1 5.0 %all-to-all-start.1 = ((bf16[4,24,64,128]{3,2,1,0:T(8,128)(2,1)}), bf16[4,24,64,128]{3,2,1,0:T(8,128)(2,1)S(1)}, u32[]{:S(2)}, u32[]{:S(2)}) async-start(bf16[4,24,64,128]{3,2,1,0:T(8,128)(2,1)} %shard_map.96), calls=%async_computation.1 | async-start | bytes 3145728 | tf_op jit(solution)/shard_map/all_to_all | solution.py:356
  9.1 0.1 fusion.1
  9.2 5.4 %shard_map.95 = (bf16[4,24,64,128]{3,2,1,0:T(8,128)(2,1)S(1)}, bf16[64,256]{1,0:T(8,128)(2,1)}, bf16[64,256]{1,0:T(8,128)(2,1)}, f32[128,128]{1,0:T(8,128)}) custom-call(s32[1]{0:T(128)} %bitcast.snap_ref, bf16[64,3,4,8,128]{4,3,2,1,0:T(8,128)(2,1)S(1)} %copy-done.2, bf16[64,256]{1,0:T(8,128)(2,1)S(1)} %get-tuple-element.27.left_ref, ...), custom_call_target="tpu_custom_call" | custom-call | bytes 3145728 | tf_op jit(solution)/shard_map/pallas_call | solution.py:318
  14.6 1.2 %copy-done.1 = bf16[4,24,64,128]{3,2,1,0:T(8,128)(2,1)} copy-done((bf16[4,24,64,128]{3,2,1,0:T(8,128)(2,1)}, bf16[4,24,64,128]{3,2,1,0:T(8,128)(2,1)S(1)}, u32[]{:S(2)}) %copy-start.1) | copy-done | bytes 1572888
  15.8 8.2 %all-to-all-done.1.snaps_ref.direct_ref = bf16[4,24,64,128]{3,2,1,0:T(8,128)(2,1)S(1)} async-done(((bf16[4,24,64,128]{3,2,1,0:T(8,128)(2,1)}), bf16[4,24,64,128]{3,2,1,0:T(8,128)(2,1)S(1)}, u32[]{:S(2)}, u32[]{:S(2)}) %all-to-all-start.1) | async-done | bytes 1572896 | tf_op jit(solution)/shard_map/all_to_all | solution.py:356
  24.0 3.7 %all-to-all-start = ((bf16[4,24,64,128]{3,2,1,0:T(8,128)(2,1)}), bf16[4,24,64,128]{3,2,1,0:T(8,128)(2,1)S(1)}, u32[]{:S(2)}, u32[]{:S(2)}) async-start(bf16[4,24,64,128]{3,2,1,0:T(8,128)(2,1)} %copy-done.1), calls=%async_computation | async-start | bytes 3145728 | tf_op jit(solution)/shard_map/all_to_all | solution.py:370
  27.7 1.4 %shard_map.97 = (f32[28,64,128]{2,1,0:T(8,128)}, bf16[6,64,128]{2,1,0:T(8,128)(2,1)S(1)}, bf16[6,64,128]{2,1,0:T(8,128)(2,1)}, bf16[64,128]{1,0:T(8,128)(2,1)S(1)}, bf16[64,128]{1,0:T(8,128)(2,1)S(1)}) custom-call(bf16[4,24,64,128]{3,2,1,0:T(8,128)(2,1)S(1)} %all-to-all-done.1.snaps_ref.direct_ref, bf16[64,256]{1,0:T(8,128)(2,1)S(1)} %copy-done.6, ...), custom_call_target="tpu_custom_call" | custom-call | flops 100663296 | bytes 2097152 | tf_op jit(solution)/shard_map/pallas_call | solution.py:318
  29.1 9.9 %collective-permute-start = (bf16[6,64,128]{2,1,0:T(8,128)(2,1)}, bf16[6,64,128]{2,1,0:T(8,128)(2,1)S(1)}, u32[]{:S(2)}, u32[]{:S(2)}) collective-permute-start(bf16[6,64,128]{2,1,0:T(8,128)(2,1)} %get-tuple-element.18), channel_id=1, source_target_pairs={{0,4},{4,8},{8,12},{12,16},{16,20},{20,24},{24,28},{28,32},{32,36}... | collective-permute-start | bytes 294920 | tf_op jit(solution)/shard_map/ppermute | solution.py:385
  39.0 1.9 %collective-permute-start.1 = (bf16[6,64,128]{2,1,0:T(8,128)(2,1)S(1)}, bf16[6,64,128]{2,1,0:T(8,128)(2,1)S(1)}, u32[]{:S(2)}, u32[]{:S(2)}) collective-permute-start(bf16[6,64,128]{2,1,0:T(8,128)(2,1)S(1)} %get-tuple-element.19), channel_id=1, source_target_pairs={{4,0},{8,4},{12,8},{16,12},{20,16},{24,20},{28,24},{32,28},{36,32}... | collective-permute-start | bytes 294920 | tf_op jit(solution)/shard_map/ppermute | solution.py:386
  40.9 3.6 %collective-permute-start.2 = (bf16[64,128]{1,0:T(8,128)(2,1)S(1)}, bf16[64,128]{1,0:T(8,128)(2,1)S(1)}, u32[]{:S(2)}, u32[]{:S(2)}) collective-permute-start(bf16[64,128]{1,0:T(8,128)(2,1)S(1)} %get-tuple-element.20), channel_id=1, source_target_pairs={{0,1},{1,2},{2,3},{4,5},{5,6},{6,7},{8,9},{9,10},{10,11},{12,13},{... | collective-permute-start | bytes 49160 | tf_op jit(solution)/shard_map/ppermute | solution.py:387
  44.5 1.3 %collective-permute-start.3 = (bf16[64,128]{1,0:T(8,128)(2,1)S(1)}, bf16[64,128]{1,0:T(8,128)(2,1)S(1)}, u32[]{:S(2)}, u32[]{:S(2)}) collective-permute-start(bf16[64,128]{1,0:T(8,128)(2,1)S(1)} %get-tuple-element.21), channel_id=1, source_target_pairs={{1,0},{2,1},{3,2},{5,4},{6,5},{7,6},{9,8},{10,9},{11,10},{13,12},{... | collective-permute-start | bytes 49160 | tf_op jit(solution)/shard_map/ppermute | solution.py:388
  45.8 3.3 %collective-permute-done.3.above_ref = bf16[64,128]{1,0:T(8,128)(2,1)S(1)} collective-permute-done((bf16[64,128]{1,0:T(8,128)(2,1)S(1)}, bf16[64,128]{1,0:T(8,128)(2,1)S(1)}, u32[]{:S(2)}, u32[]{:S(2)}) %collective-permute-start.3) | collective-permute-done | bytes 16416 | tf_op jit(solution)/shard_map/ppermute | solution.py:388
  49.1 0.0 collective-permute-done.before_ref
  49.1 0.0 collective-permute-done.1.after_ref
  49.1 3.8 %shard_map.98 = f32[8,128,128]{2,1,0:T(8,128)} custom-call(bf16[4,24,64,128]{3,2,1,0:T(8,128)(2,1)S(1)} %all-to-all-done.adjoint_ref, bf16[4,24,64,128]{3,2,1,0:T(8,128)(2,1)S(1)} %all-to-all-done.1.snaps_ref.direct_ref, f32[28,64,128]{2,1,0:T(8,128)} %get-tuple-element.17.held_hbm, bf16[6,64,128]{2,1,0:T(8,128)(2,1)S(1)} %collective-permute-done.before_ref, ...), custom_call_target="tpu_custom_call" | custom-call | flops 1073741824 | bytes 6291456 | tf_op jit(solution)/shard_map/pallas_call | solution.py:318
  52.9 4.0 %all-to-all-start.2 = ((f32[8,128,128]{2,1,0:T(8,128)}), f32[8,128,128]{2,1,0:T(8,128)S(1)}, u32[]{:S(2)}, u32[]{:S(2)}) async-start(f32[8,128,128]{2,1,0:T(8,128)} %shard_map.98), calls=%async_computation.2 | async-start | bytes 1048576 | tf_op jit(solution)/shard_map/all_to_all | solution.py:405
  57.0 0.7 gather_fusion
  57.6 8.7 %all-to-all-done.2 = f32[8,128,128]{2,1,0:T(8,128)S(1)} async-done(((f32[8,128,128]{2,1,0:T(8,128)}), f32[8,128,128]{2,1,0:T(8,128)S(1)}, u32[]{:S(2)}, u32[]{:S(2)}) %all-to-all-start.2) | async-done | bytes 524320 | tf_op jit(solution)/shard_map/all_to_all | solution.py:405
  66.4 0.1 reshape.16
  66.5 0.1 copy.12
  66.5 0.2 reshape.17
  66.7 0.1 fusion.2
  66.9 0.1 pad_maximum_fusion
  67.0 32.0 %all_to_all.20.sums_ref = f32[64,2,128]{2,1,0:T(2,128)S(1)} all-to-all(f32[64,2,128]{2,1,0:T(2,128)S(1)} %pad_maximum_fusion), channel_id=1, replica_groups=mesh['z'=8,'y'=8,'core'=2,'snap'=4] {'z','y'}, dimensions={0} | all-to-all | bytes 131072 | tf_op jit(solution)/shard_map/all_to_all | solution.py:413
  99.0 0.7 shard_map.99
  (22 shorter events, 0.1 us)
Async XLA Ops:
  0.6 56.3 %copy-start = (s32[16]{0:T(128)S(1)}, s32[16]{0:T(128)}, u32[]{:S(2)}) copy-start(s32[16]{0:T(128)} %param.14) | copy-start | bytes 196
  4.0 5.0 %copy-start.10 = (f32[64]{0:T(128)S(1)}, f32[64]{0:T(128)}, u32[]{:S(2)}) copy-start(f32[64]{0:T(128)} %param.12) | copy-start | bytes 772
  4.1 5.0 %copy-start.7 = (f32[256,64]{0,1:T(8,128)S(1)}, f32[256,64]{0,1:T(8,128)}, u32[]{:S(2)}) copy-start(f32[256,64]{0,1:T(8,128)} %param.11) | copy-start | bytes 196612
  4.1 5.0 %copy-start.8 = (f32[256,64]{0,1:T(8,128)S(1)}, f32[256,64]{0,1:T(8,128)}, u32[]{:S(2)}) copy-start(f32[256,64]{0,1:T(8,128)} %param.10) | copy-start | bytes 196612
  4.1 5.1 %copy-start.2 = (bf16[64,3,4,8,128]{4,3,2,1,0:T(8,128)(2,1)S(1)}, bf16[64,3,4,8,128]{4,3,2,1,0:T(8,128)(2,1)}, u32[]{:S(2)}) copy-start(bf16[64,3,4,8,128]{4,3,2,1,0:T(8,128)(2,1)} %snaps_ref.2) | copy-start | bytes 4718596
  4.1 5.1 %copy-start.3 = (f32[16,4,8,128]{3,2,1,0:T(8,128)S(1)}, f32[16,4,8,128]{3,2,1,0:T(8,128)}, u32[]{:S(2)}) copy-start(f32[16,4,8,128]{3,2,1,0:T(8,128)} %coeff_ref.1) | copy-start | bytes 786436
  4.1 19.9 %all-to-all-start.1 = ((bf16[4,24,64,128]{3,2,1,0:T(8,128)(2,1)}), bf16[4,24,64,128]{3,2,1,0:T(8,128)(2,1)S(1)}, u32[]{:S(2)}, u32[]{:S(2)}) async-start(bf16[4,24,64,128]{3,2,1,0:T(8,128)(2,1)} %shard_map.96), calls=%async_computation.1 | async-start | bytes 3145728 | tf_op jit(solution)/shard_map/all_to_all | solution.py:356
  14.6 1.2 %copy-start.1 = (bf16[4,24,64,128]{3,2,1,0:T(8,128)(2,1)}, bf16[4,24,64,128]{3,2,1,0:T(8,128)(2,1)S(1)}, u32[]{:S(2)}) copy-start(bf16[4,24,64,128]{3,2,1,0:T(8,128)(2,1)S(1)} %get-tuple-element.13) | copy-start | bytes 4718596
  24.0 3.7 %copy-start.4 = (f32[128,128]{1,0:T(8,128)S(1)}, f32[128,128]{1,0:T(8,128)}, u32[]{:S(2)}) copy-start(f32[128,128]{1,0:T(8,128)} %get-tuple-element.16.coeff_ref) | copy-start | bytes 196612
  24.0 3.7 %copy-start.5 = (bf16[64,256]{1,0:T(8,128)(2,1)S(1)}, bf16[64,256]{1,0:T(8,128)(2,1)}, u32[]{:S(2)}) copy-start(bf16[64,256]{1,0:T(8,128)(2,1)} %get-tuple-element.15.adjoint_weight_ref) | copy-start | bytes 98308
  24.0 3.7 %copy-start.6 = (bf16[64,256]{1,0:T(8,128)(2,1)S(1)}, bf16[64,256]{1,0:T(8,128)(2,1)}, u32[]{:S(2)}) copy-start(bf16[64,256]{1,0:T(8,128)(2,1)} %get-tuple-element.14.weight_ref) | copy-start | bytes 98308
  24.0 21.8 %all-to-all-start = ((bf16[4,24,64,128]{3,2,1,0:T(8,128)(2,1)}), bf16[4,24,64,128]{3,2,1,0:T(8,128)(2,1)S(1)}, u32[]{:S(2)}, u32[]{:S(2)}) async-start(bf16[4,24,64,128]{3,2,1,0:T(8,128)(2,1)} %copy-done.1), calls=%async_computation | async-start | bytes 3145728 | tf_op jit(solution)/shard_map/all_to_all | solution.py:370
  29.1 20.0 %collective-permute-start = (bf16[6,64,128]{2,1,0:T(8,128)(2,1)}, bf16[6,64,128]{2,1,0:T(8,128)(2,1)S(1)}, u32[]{:S(2)}, u32[]{:S(2)}) collective-permute-start(bf16[6,64,128]{2,1,0:T(8,128)(2,1)} %get-tuple-element.18), channel_id=1, source_target_pairs={{0,4},{4,8},{8,12},{12,16},{16,20},{20,24},{24,28},{28,32},{32,36}... | collective-permute-start | bytes 294920 | tf_op jit(solution)/shard_map/ppermute | solution.py:385
  39.0 10.1 %collective-permute-start.1 = (bf16[6,64,128]{2,1,0:T(8,128)(2,1)S(1)}, bf16[6,64,128]{2,1,0:T(8,128)(2,1)S(1)}, u32[]{:S(2)}, u32[]{:S(2)}) collective-permute-start(bf16[6,64,128]{2,1,0:T(8,128)(2,1)S(1)} %get-tuple-element.19), channel_id=1, source_target_pairs={{4,0},{8,4},{12,8},{16,12},{20,16},{24,20},{28,24},{32,28},{36,32}... | collective-permute-start | bytes 294920 | tf_op jit(solution)/shard_map/ppermute | solution.py:386
  40.9 4.9 %collective-permute-start.2 = (bf16[64,128]{1,0:T(8,128)(2,1)S(1)}, bf16[64,128]{1,0:T(8,128)(2,1)S(1)}, u32[]{:S(2)}, u32[]{:S(2)}) collective-permute-start(bf16[64,128]{1,0:T(8,128)(2,1)S(1)} %get-tuple-element.20), channel_id=1, source_target_pairs={{0,1},{1,2},{2,3},{4,5},{5,6},{6,7},{8,9},{9,10},{10,11},{12,13},{... | collective-permute-start | bytes 49160 | tf_op jit(solution)/shard_map/ppermute | solution.py:387
  44.5 4.6 %collective-permute-start.3 = (bf16[64,128]{1,0:T(8,128)(2,1)S(1)}, bf16[64,128]{1,0:T(8,128)(2,1)S(1)}, u32[]{:S(2)}, u32[]{:S(2)}) collective-permute-start(bf16[64,128]{1,0:T(8,128)(2,1)S(1)} %get-tuple-element.21), channel_id=1, source_target_pairs={{1,0},{2,1},{3,2},{5,4},{6,5},{7,6},{9,8},{10,9},{11,10},{13,12},{... | collective-permute-start | bytes 49160 | tf_op jit(solution)/shard_map/ppermute | solution.py:388
  49.1 7.8 %copy-start.9 = (s32[16]{0:T(128)S(1)}, s32[16]{0:T(128)}, u32[]{:S(2)}) copy-start(s32[16]{0:T(128)} %constant.20) | copy-start | bytes 196
  52.9 13.4 %all-to-all-start.2 = ((f32[8,128,128]{2,1,0:T(8,128)}), f32[8,128,128]{2,1,0:T(8,128)S(1)}, u32[]{:S(2)}, u32[]{:S(2)}) async-start(f32[8,128,128]{2,1,0:T(8,128)} %shard_map.98), calls=%async_computation.2 | async-start | bytes 1048576 | tf_op jit(solution)/shard_map/all_to_all | solution.py:405

commit v6 on v5

--- a/solution.py
+++ b/solution.py
@@ -26,7 +26,6 @@
 COLS = M // SNAP
 OWN = R // SNAP
 SPACE = ("z", "y", "core")
-CHUNKS = 8
 PIECES = 4
 LIMIT = 24 * 1024 * 1024
 WHOLE = 60 * 1024 * 1024
@@ -78,13 +77,24 @@
 
 
 def adjoint_kernel(
-    snap_ref, snaps_ref, left_ref, right_ref, coeff_ref, out_ref, left_out, right_out, coeff_out
+    snap_ref,
+    snaps_ref,
+    left_ref,
+    right_ref,
+    coeff_ref,
+    selector_ref,
+    out_ref,
+    left_out,
+    right_out,
+    coeff_out,
+    selector_out,
 ):
     for comp in range(COMPONENTS):
         for x in range(4):
             spread_rows(snaps_ref[:, comp, x], out_ref, comp * TILES + x * 2, 0)
     left_out[...] = left_ref[...]
     right_out[...] = right_ref[...]
+    selector_out[...] = selector_ref[...]
     shift = lax.rem(NZ - GROUP * snap_ref[0], NZ)
     for q in range(TERMS):
         for x in range(4):
@@ -218,20 +228,17 @@
     after_ref,
     below_ref,
     above_ref,
-    out_hbm,
+    keep_ref,
+    send_ref,
     held_ref,
     gram_ref,
     parts_ref,
     weighted_ref,
     out_ref,
-    sems,
+    sem,
 ):
-    fetch = pltpu.make_async_copy(held_hbm, held_ref, sems.at[2])
+    fetch = pltpu.make_async_copy(held_hbm, held_ref, sem)
     fetch.start()
-    stores = [
-        pltpu.make_async_copy(out_ref.at[:, rows], out_hbm.at[:, rows], sems.at[n])
-        for n, rows in enumerate((pl.ds(0, 64), pl.ds(64, 64)))
-    ]
     transposed = (((1,), (1,)), ((), ()))
     gram = jnp.zeros((M, M), jnp.float32)
     for comp in range(COMPONENTS):
@@ -271,7 +278,6 @@
                 for t in range(2)
             ]
             out_ref[core * SNAP + snap, :64, :] = jnp.concatenate(halves, axis=1)
-    stores[0].start()
     blocks = []
     row = 0
     for target, members in enumerate(MEMBERS):
@@ -297,9 +303,9 @@
                 rows = own[(2 * w + core) * 8 : (2 * w + core + 1) * 8]
                 out_ref[core * SNAP + snap, 64 + w * 8 : 64 + w * 8 + 8, :] = rows[:, :NZ]
                 out_ref[core * SNAP + snap, 96 + w * 8 : 96 + w * 8 + 8, :] = rows[:, NZ:]
-    stores[1].start()
-    for store in stores:
-        store.wait()
+    core = lax.axis_index("core")
+    keep_ref[...] = out_ref[pl.ds(core * SNAP, SNAP)]
+    send_ref[...] = out_ref[pl.ds((1 - core) * SNAP, SNAP)]
 
 
 def finish_kernel(sums_ref, gram_ref, reduced_ref):
@@ -354,19 +360,23 @@
         WHOLE,
     )(direct_snaps)
     direct = lax.all_to_all(ready, "snap", 0, 0, tiled=True)
+    selector = (
+        term_slot[jnp.array(ORDER)][None, :] == jnp.arange(TERMS, dtype=jnp.int32)[:, None]
+    ).astype(jnp.float32)
     here = lax.axis_index("snap").astype(jnp.int32).reshape(1)
-    ready, adjoint_weight, direct_weight, coeff = call(
+    ready, adjoint_weight, direct_weight, coeff, selector = call(
         adjoint_kernel,
         (
             spread_shape,
             pltpu.HBM((R, M), jnp.bfloat16),
             pltpu.HBM((R, M), jnp.bfloat16),
             pltpu.HBM((TERMS * TILES, NZ), jnp.float32),
+            pltpu.HBM((TERMS, TERMS), jnp.float32),
         ),
         0,
         3 << 20,
         inputs={0: pltpu.SMEM},
-    )(here, adjoint_snaps, left, right, term_coeff)
+    )(here, adjoint_snaps, left, right, term_coeff, selector)
     adjoint = lax.all_to_all(ready, "snap", 0, 0, tiled=True)
     held, first, last, low, high = call(
         modes_kernel,
@@ -386,9 +396,10 @@
     after = lax.ppermute(first, SPACE, [(j, i) for i, j in slabs])
     below = lax.ppermute(high, "snap", quarters)
     above = lax.ppermute(low, "snap", [(j, i) for i, j in quarters])
-    terms = call(
+    half = shape(SNAP, 128, NZ, dtype=jnp.float32)
+    keep, send = call(
         functools.partial(products_kernel, scale),
-        pltpu.HBM((CHUNKS, 128, NZ), jnp.float32),
+        (half, half),
         1 << 30,
         6 << 20,
         (
@@ -396,18 +407,15 @@
             pltpu.VMEM((2, M, NZ), jnp.float32),
             pltpu.VMEM((COMPONENTS, 3 * R, CELLS), jnp.bfloat16),
             pltpu.VMEM((TERMS * R, CELLS), jnp.bfloat16),
-            pltpu.VMEM((CHUNKS, 128, NZ), jnp.float32),
-            pltpu.SemaphoreType.DMA((3,)),
+            pltpu.VMEM((2 * SNAP, 128, NZ), jnp.float32),
+            pltpu.SemaphoreType.DMA,
         ),
         {2: pltpu.HBM},
-        pltpu.HBM,
     )(adjoint, direct, held, before, after, below, above)
-    near = lax.all_to_all(terms, ("core", "snap"), 0, 0, tiled=True).sum(axis=0)
+    terms = keep + lax.ppermute(send, "core", [(0, 1), (1, 0)])
+    near = lax.all_to_all(terms, "snap", 0, 0, tiled=True).sum(axis=0)
     gram = near[:64]
     operators = near[64:].reshape(2, 4, 8, 8, OWN).transpose(0, 3, 1, 2, 4).reshape(TERMS, 4 * NZ)
-    selector = (
-        term_slot[jnp.array(ORDER)][None, :] == jnp.arange(TERMS, dtype=jnp.int32)[:, None]
-    ).astype(jnp.float32)
     ordered = jnp.dot(selector, operators, precision=lax.Precision.HIGHEST)
     owned = jnp.stack([gram, ordered.reshape(64, NZ)], axis=1)
     sums = lax.all_to_all(owned, ("z", "y"), 0, 0, tiled=True)

time: 100 us -> 99 us (0.990)
  blocking collectives: 32 us -> 40.8 us
  waiting for transfers between devices: 20.2 us -> 11.9 us
  starting transfers between devices: 29.3 us -> 27.7 us
    all_to_all x0 -> x1, blocking collectives: none -> 9.71 us  [shards(): near = lax.all_to_all(terms, 'snap', 0, 0, tiled=True).sum(axis=0)]
    all_to_all x1 -> x0, waiting for transfers between devices: 8.69 us -> none  [shards(): near = lax.all_to_all(terms, ('core', 'snap'), 0, 0, tiled=True).sum(axis=0)]
    all_to_all x1 -> x0, starting transfers between devices: 3.99 us -> none  [shards(): near = lax.all_to_all(terms, ('core', 'snap'), 0, 0, tiled=True).sum(axis=0)]
    ppermute x0 -> x1, starting transfers between devices: none -> 2.32 us  [shards(): terms = keep + lax.ppermute(send, 'core', [(0, 1), (1, 0)])]
    ppermute x0 -> x1, waiting for transfers between devices: none -> 1.14 us  [shards(): terms = keep + lax.ppermute(send, 'core', [(0, 1), (1, 0)])]
where the time goes in v6:
time: 99 us; the launch traced here: 98.1 us
  blocking collectives  40.8 us (41%)
  starting transfers between devices  27.7 us (28%)
  Pallas kernels  14.1 us (14%)
  waiting for transfers between devices  11.9 us (12%)
  local copies, waits for them, and re-layouts  2.28 us (2%)
    all_to_all x1, blocking collectives, shards(): sums = lax.all_to_all(owned, ('z', 'y'), 0, 0, tiled=True)  31.1 us
    pallas_call x5, Pallas kernels, run(): pl.pallas_call(kernel, out_shape=out_shape, in_specs=[pl.BlockSpec(memory...  14.1 us
    ppermute x1, starting transfers between devices, shards(): before = lax.ppermute(last, SPACE, slabs)  9.87 us
    all_to_all x1, blocking collectives, shards(): near = lax.all_to_all(terms, 'snap', 0, 0, tiled=True).sum(axis=0)  9.71 us
    all_to_all x1, waiting for transfers between devices, shards(): direct = lax.all_to_all(ready, 'snap', 0, 0, tiled=True)  7.49 us
    all_to_all x1, starting transfers between devices, shards(): direct = lax.all_to_all(ready, 'snap', 0, 0, tiled=True)  4.99 us
    all_to_all x1, starting transfers between devices, shards(): adjoint = lax.all_to_all(ready, 'snap', 0, 0, tiled=True)  3.69 us
    ppermute x1, starting transfers between devices, shards(): below = lax.ppermute(high, 'snap', quarters)  3.59 us
  transfers between devices with their start and end apart: 7, of which 3 were waited for; matrix products, arithmetic and copies ran while one was open for 1% of the time, Pallas kernels for 7%

profile of v6, /device:TPU:1, one launch (start us, length us, event | category | flops | bytes accessed | tf_op | source)
XLA Modules:
  0.0 98.1 jit_solution(14936134909230515433)
XLA Ops:
  0.6 0.0 copy-start
  0.6 3.4 %shard_map.96 = bf16[4,24,64,128]{3,2,1,0:T(8,128)(2,1)} custom-call(bf16[64,3,4,8,128]{4,3,2,1,0:T(8,128)(2,1)} %snaps_ref.3), custom_call_target="tpu_custom_call" | custom-call | bytes 3145728 | tf_op jit(solution)/shard_map/pallas_call | solution.py:324
  4.0 0.0 copy-start.11
  4.1 0.0 copy-start.10
  4.1 0.0 copy-start.7
  4.1 0.0 copy-start.8
  4.1 0.0 copy-start.2
  4.1 5.0 %all-to-all-start.1 = ((bf16[4,24,64,128]{3,2,1,0:T(8,128)(2,1)}), bf16[4,24,64,128]{3,2,1,0:T(8,128)(2,1)S(1)}, u32[]{:S(2)}, u32[]{:S(2)}) async-start(bf16[4,24,64,128]{3,2,1,0:T(8,128)(2,1)} %shard_map.96), calls=%async_computation.1 | async-start | bytes 3145728 | tf_op jit(solution)/shard_map/all_to_all | solution.py:362
  9.1 0.7 gather_fusion
  9.8 0.1 fusion.1
  9.9 5.4 %shard_map.95 = (bf16[4,24,64,128]{3,2,1,0:T(8,128)(2,1)S(1)}, bf16[64,256]{1,0:T(8,128)(2,1)}, bf16[64,256]{1,0:T(8,128)(2,1)}, f32[128,128]{1,0:T(8,128)}, f32[16,16]{1,0:T(8,128)}) custom-call(s32[1]{0:T(128)} %bitcast.snap_ref, bf16[64,3,4,8,128]{4,3,2,1,0:T(8,128)(2,1)S(1)} %copy-done.2, bf16[64,256]{1,0:T(8,128)(2,1)S(1)} %get-tuple-element.33.left_ref, ...), custom_call_target="tpu_custom_call" | custom-call | bytes 3145728 | tf_op jit(solution)/shard_map/pallas_call | solution.py:324
  15.3 1.2 %copy-done.1 = bf16[4,24,64,128]{3,2,1,0:T(8,128)(2,1)} copy-done((bf16[4,24,64,128]{3,2,1,0:T(8,128)(2,1)}, bf16[4,24,64,128]{3,2,1,0:T(8,128)(2,1)S(1)}, u32[]{:S(2)}) %copy-start.1) | copy-done | bytes 1572888
  16.5 7.5 %all-to-all-done.1.snaps_ref.direct_ref = bf16[4,24,64,128]{3,2,1,0:T(8,128)(2,1)S(1)} async-done(((bf16[4,24,64,128]{3,2,1,0:T(8,128)(2,1)}), bf16[4,24,64,128]{3,2,1,0:T(8,128)(2,1)S(1)}, u32[]{:S(2)}, u32[]{:S(2)}) %all-to-all-start.1) | async-done | bytes 1572896 | tf_op jit(solution)/shard_map/all_to_all | solution.py:362
  24.0 3.7 %all-to-all-start = ((bf16[4,24,64,128]{3,2,1,0:T(8,128)(2,1)}), bf16[4,24,64,128]{3,2,1,0:T(8,128)(2,1)S(1)}, u32[]{:S(2)}, u32[]{:S(2)}) async-start(bf16[4,24,64,128]{3,2,1,0:T(8,128)(2,1)} %copy-done.1), calls=%async_computation | async-start | bytes 3145728 | tf_op jit(solution)/shard_map/all_to_all | solution.py:380
  27.7 1.4 %shard_map.97 = (f32[28,64,128]{2,1,0:T(8,128)}, bf16[6,64,128]{2,1,0:T(8,128)(2,1)S(1)}, bf16[6,64,128]{2,1,0:T(8,128)(2,1)}, bf16[64,128]{1,0:T(8,128)(2,1)S(1)}, bf16[64,128]{1,0:T(8,128)(2,1)S(1)}) custom-call(bf16[4,24,64,128]{3,2,1,0:T(8,128)(2,1)S(1)} %all-to-all-done.1.snaps_ref.direct_ref, bf16[64,256]{1,0:T(8,128)(2,1)S(1)} %copy-done.6, ...), custom_call_target="tpu_custom_call" | custom-call | flops 100663296 | bytes 2097152 | tf_op jit(solution)/shard_map/pallas_call | solution.py:324
  29.1 9.9 %collective-permute-start = (bf16[6,64,128]{2,1,0:T(8,128)(2,1)}, bf16[6,64,128]{2,1,0:T(8,128)(2,1)S(1)}, u32[]{:S(2)}, u32[]{:S(2)}) collective-permute-start(bf16[6,64,128]{2,1,0:T(8,128)(2,1)} %get-tuple-element.21), channel_id=1, source_target_pairs={{0,4},{4,8},{8,12},{12,16},{16,20},{20,24},{24,28},{28,32},{32,36}... | collective-permute-start | bytes 294920 | tf_op jit(solution)/shard_map/ppermute | solution.py:395
  39.0 1.9 %collective-permute-start.1 = (bf16[6,64,128]{2,1,0:T(8,128)(2,1)S(1)}, bf16[6,64,128]{2,1,0:T(8,128)(2,1)S(1)}, u32[]{:S(2)}, u32[]{:S(2)}) collective-permute-start(bf16[6,64,128]{2,1,0:T(8,128)(2,1)S(1)} %get-tuple-element.22), channel_id=1, source_target_pairs={{4,0},{8,4},{12,8},{16,12},{20,16},{24,20},{28,24},{32,28},{36,32}... | collective-permute-start | bytes 294920 | tf_op jit(solution)/shard_map/ppermute | solution.py:396
  40.9 3.6 %collective-permute-start.2 = (bf16[64,128]{1,0:T(8,128)(2,1)S(1)}, bf16[64,128]{1,0:T(8,128)(2,1)S(1)}, u32[]{:S(2)}, u32[]{:S(2)}) collective-permute-start(bf16[64,128]{1,0:T(8,128)(2,1)S(1)} %get-tuple-element.23), channel_id=1, source_target_pairs={{0,1},{1,2},{2,3},{4,5},{5,6},{6,7},{8,9},{9,10},{10,11},{12,13},{... | collective-permute-start | bytes 49160 | tf_op jit(solution)/shard_map/ppermute | solution.py:397
  44.5 1.3 %collective-permute-start.3 = (bf16[64,128]{1,0:T(8,128)(2,1)S(1)}, bf16[64,128]{1,0:T(8,128)(2,1)S(1)}, u32[]{:S(2)}, u32[]{:S(2)}) collective-permute-start(bf16[64,128]{1,0:T(8,128)(2,1)S(1)} %get-tuple-element.24), channel_id=1, source_target_pairs={{1,0},{2,1},{3,2},{5,4},{6,5},{7,6},{9,8},{10,9},{11,10},{13,12},{... | collective-permute-start | bytes 49160 | tf_op jit(solution)/shard_map/ppermute | solution.py:398
  45.9 3.2 %collective-permute-done.3.above_ref = bf16[64,128]{1,0:T(8,128)(2,1)S(1)} collective-permute-done((bf16[64,128]{1,0:T(8,128)(2,1)S(1)}, bf16[64,128]{1,0:T(8,128)(2,1)S(1)}, u32[]{:S(2)}, u32[]{:S(2)}) %collective-permute-start.3) | collective-permute-done | bytes 16416 | tf_op jit(solution)/shard_map/ppermute | solution.py:398
  49.1 3.2 %shard_map.98 = (f32[4,128,128]{2,1,0:T(8,128)S(1)}, f32[4,128,128]{2,1,0:T(8,128)S(1)}) custom-call(bf16[4,24,64,128]{3,2,1,0:T(8,128)(2,1)S(1)} %all-to-all-done.adjoint_ref, bf16[4,24,64,128]{3,2,1,0:T(8,128)(2,1)S(1)} %all-to-all-done.1.snaps_ref.direct_ref, f32[28,64,128]{2,1,0:T(8,128)} %get-tuple-element.20.held_hbm, ...), custom_call_target="tpu_custom_call" | custom-call | flops 1073741824 | bytes 6291456 | tf_op jit(solution)/shard_map/pallas_call | solution.py:324
  52.3 2.3 %collective-permute-start.4 = (f32[4,128,128]{2,1,0:T(8,128)S(1)}, f32[4,128,128]{2,1,0:T(8,128)S(1)}, u32[]{:S(2)}, u32[]{:S(2)}) collective-permute-start(f32[4,128,128]{2,1,0:T(8,128)S(1)} %get-tuple-element.26), channel_id=1, source_target_pairs={{0,4},{4,0},{1,5},{5,1},{2,6},{6,2},{3,7},{7,3},{8,12},{12,8},{9,1... | collective-permute-start | bytes 786440 | tf_op jit(solution)/shard_map/ppermute | solution.py:415
  54.6 1.1 %collective-permute-done.4 = f32[4,128,128]{2,1,0:T(8,128)S(1)} collective-permute-done((f32[4,128,128]{2,1,0:T(8,128)S(1)}, f32[4,128,128]{2,1,0:T(8,128)S(1)}, u32[]{:S(2)}, u32[]{:S(2)}) %collective-permute-start.4) | collective-permute-done | bytes 262176 | tf_op jit(solution)/shard_map/ppermute | solution.py:415
  55.8 9.7 %all_to_all.20 = f32[4,128,128]{2,1,0:T(8,128)S(1)} all-to-all(f32[4,128,128]{2,1,0:T(8,128)S(1)} %add.7), channel_id=1, replica_groups=mesh['z'=8,'y'=8,'core'=2,'snap'=4] {'snap'}, dimensions={0} | all-to-all | bytes 524288 | tf_op jit(solution)/shard_map/all_to_all | solution.py:416
  65.6 0.1 reshape.16
  65.7 0.1 copy.12
  65.7 0.2 reshape.17
  65.9 0.1 fusion.4
  66.1 0.1 stack_reshape.3
  66.1 0.1 pad_maximum_fusion
  66.2 31.1 %all_to_all.21.sums_ref = f32[64,2,128]{2,1,0:T(2,128)S(1)} all-to-all(f32[64,2,128]{2,1,0:T(2,128)S(1)} %pad_maximum_fusion), channel_id=1, replica_groups=mesh['z'=8,'y'=8,'core'=2,'snap'=4] {'z','y'}, dimensions={0} | all-to-all | bytes 131072 | tf_op jit(solution)/shard_map/all_to_all | solution.py:421
  97.3 0.7 shard_map.99
  (27 shorter events, 0.1 us)
Async XLA Ops:
  0.6 8.5 %copy-start = (s32[16]{0:T(128)S(1)}, s32[16]{0:T(128)}, u32[]{:S(2)}) copy-start(s32[16]{0:T(128)} %param.14) | copy-start | bytes 196
  4.0 5.1 %copy-start.11 = (f32[64]{0:T(128)S(1)}, f32[64]{0:T(128)}, u32[]{:S(2)}) copy-start(f32[64]{0:T(128)} %param.12) | copy-start | bytes 772
  4.1 5.1 %copy-start.10 = (s32[16]{0:T(128)S(1)}, s32[16]{0:T(128)}, u32[]{:S(2)}) copy-start(s32[16]{0:T(128)} %constant.20) | copy-start | bytes 196
  4.1 5.7 %copy-start.7 = (f32[256,64]{0,1:T(8,128)S(1)}, f32[256,64]{0,1:T(8,128)}, u32[]{:S(2)}) copy-start(f32[256,64]{0,1:T(8,128)} %param.11) | copy-start | bytes 196612
  4.1 5.7 %copy-start.8 = (f32[256,64]{0,1:T(8,128)S(1)}, f32[256,64]{0,1:T(8,128)}, u32[]{:S(2)}) copy-start(f32[256,64]{0,1:T(8,128)} %param.10) | copy-start | bytes 196612
  4.1 5.8 %copy-start.2 = (bf16[64,3,4,8,128]{4,3,2,1,0:T(8,128)(2,1)S(1)}, bf16[64,3,4,8,128]{4,3,2,1,0:T(8,128)(2,1)}, u32[]{:S(2)}) copy-start(bf16[64,3,4,8,128]{4,3,2,1,0:T(8,128)(2,1)} %snaps_ref.2) | copy-start | bytes 4718596
  4.1 5.8 %copy-start.3 = (f32[16,4,8,128]{3,2,1,0:T(8,128)S(1)}, f32[16,4,8,128]{3,2,1,0:T(8,128)}, u32[]{:S(2)}) copy-start(f32[16,4,8,128]{3,2,1,0:T(8,128)} %coeff_ref.1) | copy-start | bytes 786436
  4.1 19.9 %all-to-all-start.1 = ((bf16[4,24,64,128]{3,2,1,0:T(8,128)(2,1)}), bf16[4,24,64,128]{3,2,1,0:T(8,128)(2,1)S(1)}, u32[]{:S(2)}, u32[]{:S(2)}) async-start(bf16[4,24,64,128]{3,2,1,0:T(8,128)(2,1)} %shard_map.96), calls=%async_computation.1 | async-start | bytes 3145728 | tf_op jit(solution)/shard_map/all_to_all | solution.py:362
  15.3 1.2 %copy-start.1 = (bf16[4,24,64,128]{3,2,1,0:T(8,128)(2,1)}, bf16[4,24,64,128]{3,2,1,0:T(8,128)(2,1)S(1)}, u32[]{:S(2)}) copy-start(bf16[4,24,64,128]{3,2,1,0:T(8,128)(2,1)S(1)} %get-tuple-element.16) | copy-start | bytes 4718596
  24.0 3.7 %copy-start.4 = (f32[128,128]{1,0:T(8,128)S(1)}, f32[128,128]{1,0:T(8,128)}, u32[]{:S(2)}) copy-start(f32[128,128]{1,0:T(8,128)} %get-tuple-element.19.coeff_ref) | copy-start | bytes 196612
  24.0 3.7 %copy-start.5 = (bf16[64,256]{1,0:T(8,128)(2,1)S(1)}, bf16[64,256]{1,0:T(8,128)(2,1)}, u32[]{:S(2)}) copy-start(bf16[64,256]{1,0:T(8,128)(2,1)} %get-tuple-element.18.adjoint_weight_ref) | copy-start | bytes 98308
  24.0 3.7 %copy-start.6 = (bf16[64,256]{1,0:T(8,128)(2,1)S(1)}, bf16[64,256]{1,0:T(8,128)(2,1)}, u32[]{:S(2)}) copy-start(bf16[64,256]{1,0:T(8,128)(2,1)} %get-tuple-element.17.weight_ref) | copy-start | bytes 98308
  24.0 21.9 %all-to-all-start = ((bf16[4,24,64,128]{3,2,1,0:T(8,128)(2,1)}), bf16[4,24,64,128]{3,2,1,0:T(8,128)(2,1)S(1)}, u32[]{:S(2)}, u32[]{:S(2)}) async-start(bf16[4,24,64,128]{3,2,1,0:T(8,128)(2,1)} %copy-done.1), calls=%async_computation | async-start | bytes 3145728 | tf_op jit(solution)/shard_map/all_to_all | solution.py:380
  29.1 20.0 %collective-permute-start = (bf16[6,64,128]{2,1,0:T(8,128)(2,1)}, bf16[6,64,128]{2,1,0:T(8,128)(2,1)S(1)}, u32[]{:S(2)}, u32[]{:S(2)}) collective-permute-start(bf16[6,64,128]{2,1,0:T(8,128)(2,1)} %get-tuple-element.21), channel_id=1, source_target_pairs={{0,4},{4,8},{8,12},{12,16},{16,20},{20,24},{24,28},{28,32},{32,36}... | collective-permute-start | bytes 294920 | tf_op jit(solution)/shard_map/ppermute | solution.py:395
  39.0 10.1 %collective-permute-start.1 = (bf16[6,64,128]{2,1,0:T(8,128)(2,1)S(1)}, bf16[6,64,128]{2,1,0:T(8,128)(2,1)S(1)}, u32[]{:S(2)}, u32[]{:S(2)}) collective-permute-start(bf16[6,64,128]{2,1,0:T(8,128)(2,1)S(1)} %get-tuple-element.22), channel_id=1, source_target_pairs={{4,0},{8,4},{12,8},{16,12},{20,16},{24,20},{28,24},{32,28},{36,32}... | collective-permute-start | bytes 294920 | tf_op jit(solution)/shard_map/ppermute | solution.py:396
  40.9 4.9 %collective-permute-start.2 = (bf16[64,128]{1,0:T(8,128)(2,1)S(1)}, bf16[64,128]{1,0:T(8,128)(2,1)S(1)}, u32[]{:S(2)}, u32[]{:S(2)}) collective-permute-start(bf16[64,128]{1,0:T(8,128)(2,1)S(1)} %get-tuple-element.23), channel_id=1, source_target_pairs={{0,1},{1,2},{2,3},{4,5},{5,6},{6,7},{8,9},{9,10},{10,11},{12,13},{... | collective-permute-start | bytes 49160 | tf_op jit(solution)/shard_map/ppermute | solution.py:397
  44.5 4.6 %collective-permute-start.3 = (bf16[64,128]{1,0:T(8,128)(2,1)S(1)}, bf16[64,128]{1,0:T(8,128)(2,1)S(1)}, u32[]{:S(2)}, u32[]{:S(2)}) collective-permute-start(bf16[64,128]{1,0:T(8,128)(2,1)S(1)} %get-tuple-element.24), channel_id=1, source_target_pairs={{1,0},{2,1},{3,2},{5,4},{6,5},{7,6},{9,8},{10,9},{11,10},{13,12},{... | collective-permute-start | bytes 49160 | tf_op jit(solution)/shard_map/ppermute | solution.py:398
  52.3 13.6 %copy-start.9 = (f32[16,16]{1,0:T(8,128)S(1)}, f32[16,16]{1,0:T(8,128)}, u32[]{:S(2)}) copy-start(f32[16,16]{1,0:T(8,128)} %get-tuple-element.27) | copy-start | bytes 3076
  52.3 3.5 %collective-permute-start.4 = (f32[4,128,128]{2,1,0:T(8,128)S(1)}, f32[4,128,128]{2,1,0:T(8,128)S(1)}, u32[]{:S(2)}, u32[]{:S(2)}) collective-permute-start(f32[4,128,128]{2,1,0:T(8,128)S(1)} %get-tuple-element.26), channel_id=1, source_target_pairs={{0,4},{4,0},{1,5},{5,1},{2,6},{6,2},{3,7},{7,3},{8,12},{12,8},{9,1... | collective-permute-start | bytes 786440 | tf_op jit(solution)/shard_map/ppermute | solution.py:415

commit v7 on v6

--- a/solution.py
+++ b/solution.py
@@ -83,15 +83,21 @@
     right_ref,
     coeff_ref,
     selector_ref,
-    out_ref,
+    own_ref,
+    next_ref,
+    far_ref,
+    previous_ref,
     left_out,
     right_out,
     coeff_out,
     selector_out,
+    spread,
 ):
     for comp in range(COMPONENTS):
         for x in range(4):
-            spread_rows(snaps_ref[:, comp, x], out_ref, comp * TILES + x * 2, 0)
+            spread_rows(snaps_ref[:, comp, x], spread, comp * TILES + x * 2, 0)
+    for n, ref in enumerate((own_ref, next_ref, far_ref, previous_ref)):
+        ref[...] = spread[lax.rem(snap_ref[0] + n, SNAP)]
     left_out[...] = left_ref[...]
     right_out[...] = right_ref[...]
     selector_out[...] = selector_ref[...]
@@ -106,10 +112,10 @@
                 )
 
 
-def columns(ref, comp, tiles):
+def columns(refs, comp, tiles):
     return jnp.concatenate(
         [
-            jnp.concatenate([ref[s, comp * TILES + t] for s in range(SNAP)], axis=0)
+            jnp.concatenate([ref[comp * TILES + t] for ref in refs], axis=0)
             for t in tiles
         ],
         axis=1,
@@ -132,12 +138,13 @@
         held_ref[WEIGHT_AT + n] = wide
         held_ref[COEFF_AT + n] = coeff_ref[n * R : (n + 1) * R, :]
     weight = weight_ref[...]
+    blocks = [snaps_ref.at[n] for n in range(SNAP)]
     place = lax.rem(lax.broadcasted_iota(jnp.int32, (R, NZ), 1), GROUP)
     low = jnp.zeros((R, NZ), jnp.float32)
     high = jnp.zeros((R, NZ), jnp.float32)
     for comp in range(COMPONENTS):
         for t in range(0, TILES, 2):
-            block = columns(snaps_ref, comp, (t, t + 1))
+            block = columns(blocks, comp, (t, t + 1))
             modes = jnp.dot(weight, block, preferred_element_type=jnp.float32)
             modes = modes.astype(jnp.bfloat16)
             for half in range(2):
@@ -221,7 +228,10 @@
 
 def products_kernel(
     scale,
-    adjoint_ref,
+    own_ref,
+    next_ref,
+    far_ref,
+    previous_ref,
     direct_ref,
     held_hbm,
     before_ref,
@@ -239,13 +249,16 @@
 ):
     fetch = pltpu.make_async_copy(held_hbm, held_ref, sem)
     fetch.start()
+    adjoints = (own_ref, next_ref, far_ref, previous_ref)
+    directs = [direct_ref.at[n] for n in range(SNAP)]
+    here = lax.axis_index("snap")
     transposed = (((1,), (1,)), ((), ()))
     gram = jnp.zeros((M, M), jnp.float32)
     for comp in range(COMPONENTS):
         for t in range(0, TILES, 2):
             gram = gram + lax.dot_general(
-                columns(direct_ref, comp, (t, t + 1)),
-                columns(adjoint_ref, comp, (t, t + 1)),
+                columns(directs, comp, (t, t + 1)),
+                columns(adjoints, comp, (t, t + 1)),
                 transposed,
                 preferred_element_type=jnp.float32,
             )
@@ -258,7 +271,7 @@
     weight = weight.astype(jnp.bfloat16)
     for comp in range(COMPONENTS):
         for t in range(0, TILES, 2):
-            adjoint = columns(adjoint_ref, comp, (t, t + 1))
+            adjoint = columns(adjoints, comp, (t, t + 1))
             modes = jnp.dot(weight, adjoint, preferred_element_type=jnp.float32)
             high = modes.astype(jnp.bfloat16)
             rest = modes - high.astype(jnp.float32)
@@ -277,7 +290,8 @@
                 gram_ref[half, pl.ds(2 * core + t, M // 4, stride=4), :][:, at : at + COLS]
                 for t in range(2)
             ]
-            out_ref[core * SNAP + snap, :64, :] = jnp.concatenate(halves, axis=1)
+            chunk = core * SNAP + lax.rem(here + snap, SNAP)
+            out_ref[chunk, :64, :] = jnp.concatenate(halves, axis=1)
     blocks = []
     row = 0
     for target, members in enumerate(MEMBERS):
@@ -336,7 +350,8 @@
 
 def shards(direct_snaps, adjoint_snaps, left_factor, right_factor, singular, term_coeff, term_slot):
     scale = 1.0 / math.sqrt(1572864)
-    left = mode_weight(left_factor, singular).T
+    turned = jnp.roll(left_factor, -COLS * lax.axis_index("snap"), axis=0)
+    left = mode_weight(turned, singular).T
     right = mode_weight(right_factor, singular).T
     tiles = COMPONENTS * TILES
 
@@ -364,10 +379,10 @@
         term_slot[jnp.array(ORDER)][None, :] == jnp.arange(TERMS, dtype=jnp.int32)[:, None]
     ).astype(jnp.float32)
     here = lax.axis_index("snap").astype(jnp.int32).reshape(1)
-    ready, adjoint_weight, direct_weight, coeff, selector = call(
+    own, *others, adjoint_weight, direct_weight, coeff, selector = call(
         adjoint_kernel,
         (
-            spread_shape,
+            *[shape(tiles, COLS, NZ)] * SNAP,
             pltpu.HBM((R, M), jnp.bfloat16),
             pltpu.HBM((R, M), jnp.bfloat16),
             pltpu.HBM((TERMS * TILES, NZ), jnp.float32),
@@ -375,9 +390,14 @@
         ),
         0,
         3 << 20,
-        inputs={0: pltpu.SMEM},
+        (pltpu.VMEM((SNAP, tiles, COLS, NZ), jnp.bfloat16),),
+        {0: pltpu.SMEM},
     )(here, adjoint_snaps, left, right, term_coeff, selector)
-    adjoint = lax.all_to_all(ready, "snap", 0, 0, tiled=True)
+    arrived = [
+        lax.ppermute(piece, "snap", [(i, (i + n) % SNAP) for i in range(SNAP)])
+        for n, piece in enumerate(others, 1)
+    ]
+    adjoints = (own, *arrived[::-1])
     held, first, last, low, high = call(
         modes_kernel,
         (
@@ -410,8 +430,8 @@
             pltpu.VMEM((2 * SNAP, 128, NZ), jnp.float32),
             pltpu.SemaphoreType.DMA,
         ),
-        {2: pltpu.HBM},
-    )(adjoint, direct, held, before, after, below, above)
+        {5: pltpu.HBM},
+    )(*adjoints, direct, held, before, after, below, above)
     terms = keep + lax.ppermute(send, "core", [(0, 1), (1, 0)])
     near = lax.all_to_all(terms, "snap", 0, 0, tiled=True).sum(axis=0)
     gram = near[:64]

time: 99 us -> 100 us (1.010)
  starting transfers between devices: 27.7 us -> 34.4 us
  waiting for transfers between devices: 11.9 us -> 5.75 us
  blocking collectives: 40.8 us -> 38.4 us
  local copies, waits for them, and re-layouts: 2.28 us -> 4.4 us
    ppermute x0 -> x3, starting transfers between devices: none -> 9.54 us  [shards(): lax.ppermute(piece, 'snap', [(i, (i + n) % SNAP) for i in range(SNAP)])]
    all_to_all x1, waiting for transfers between devices: 7.49 us -> 0.01 us  [shards(): direct = lax.all_to_all(ready, 'snap', 0, 0, tiled=True)]
    all_to_all x1 -> x0, starting transfers between devices: 3.69 us -> none  [shards(): adjoint = lax.all_to_all(ready, 'snap', 0, 0, tiled=True)]
    unnamed x24 -> x22, local copies, waits for them, and re-layouts: 1.22 us -> 3.34 us
    all_to_all x1, blocking collectives: 31.1 us -> 29.2 us  [shards(): sums = lax.all_to_all(owned, ('z', 'y'), 0, 0, tiled=True)]
    ppermute x1, starting transfers between devices: 3.59 us -> 5.52 us  [shards(): below = lax.ppermute(high, 'snap', quarters)]
  transfers between devices with their start and end apart: 7 -> 9, of which waited for: 3 -> 2; matrix products, arithmetic and copies ran while one was open for 1% -> 1% of each run, Pallas kernels for 7% -> 7%
where the time goes in v7:
time: 100 us; the launch traced here: 98.6 us
  blocking collectives  38.4 us (38%)
  starting transfers between devices  34.4 us (34%)
  Pallas kernels  14.3 us (14%)
  waiting for transfers between devices  5.75 us (6%)
  local copies, waits for them, and re-layouts  4.4 us (4%)
    all_to_all x1, blocking collectives, shards(): sums = lax.all_to_all(owned, ('z', 'y'), 0, 0, tiled=True)  29.2 us
    pallas_call x5, Pallas kernels, run(): pl.pallas_call(kernel, out_shape=out_shape, in_specs=[pl.BlockSpec(memory...  14.3 us
    ppermute x3, starting transfers between devices, shards(): lax.ppermute(piece, 'snap', [(i, (i + n) % SNAP) for i in range(SNAP)])  9.54 us
    ppermute x1, starting transfers between devices, shards(): before = lax.ppermute(last, SPACE, slabs)  9.23 us
    all_to_all x1, blocking collectives, shards(): near = lax.all_to_all(terms, 'snap', 0, 0, tiled=True).sum(axis=0)  9.21 us
    ppermute x1, starting transfers between devices, shards(): below = lax.ppermute(high, 'snap', quarters)  5.52 us
    all_to_all x1, starting transfers between devices, shards(): direct = lax.all_to_all(ready, 'snap', 0, 0, tiled=True)  4.99 us
    ppermute x1, waiting for transfers between devices, shards(): above = lax.ppermute(low, 'snap', [(j, i) for i, j in quarters])  4.23 us
  transfers between devices with their start and end apart: 9, of which 2 were waited for; matrix products, arithmetic and copies ran while one was open for 1% of the time, Pallas kernels for 7%

profile of v7, /device:TPU:1, one launch (start us, length us, event | category | flops | bytes accessed | tf_op | source)
XLA Modules:
  0.0 98.6 jit_solution(5793244695137820286)
XLA Ops:
  0.6 0.0 copy-start
  0.6 3.4 %shard_map.96 = bf16[4,24,64,128]{3,2,1,0:T(8,128)(2,1)} custom-call(bf16[64,3,4,8,128]{4,3,2,1,0:T(8,128)(2,1)} %snaps_ref.3), custom_call_target="tpu_custom_call" | custom-call | bytes 3145728 | tf_op jit(solution)/shard_map/pallas_call | solution.py:338
  4.0 0.0 copy-start.9
  4.1 5.0 %all-to-all-start = ((bf16[4,24,64,128]{3,2,1,0:T(8,128)(2,1)}), bf16[4,24,64,128]{3,2,1,0:T(8,128)(2,1)S(1)}, u32[]{:S(2)}, u32[]{:S(2)}) async-start(bf16[4,24,64,128]{3,2,1,0:T(8,128)(2,1)} %shard_map.96), calls=%async_computation | async-start | bytes 3145728 | tf_op jit(solution)/shard_map/all_to_all | solution.py:377
  9.1 0.7 gather_fusion
  9.8 0.1 fusion.3
  9.9 0.9 copy-done.2
  10.9 5.7 %shard_map.95 = (bf16[24,64,128]{2,1,0:T(8,128)(2,1)S(1)}, bf16[24,64,128]{2,1,0:T(8,128)(2,1)}, bf16[24,64,128]{2,1,0:T(8,128)(2,1)}, bf16[24,64,128]{2,1,0:T(8...) custom-call(s32[1]{0:T(128)} %bitcast.snap_ref, ...), custom_call_target="tpu_custom_call" | custom-call | bytes 3145728 | tf_op jit(solution)/shard_map/pallas_call | solution.py:338
  16.6 4.6 %collective-permute-start = (bf16[24,64,128]{2,1,0:T(8,128)(2,1)}, bf16[24,64,128]{2,1,0:T(8,128)(2,1)S(1)}, u32[]{:S(2)}, u32[]{:S(2)}) collective-permute-start(bf16[24,64,128]{2,1,0:T(8,128)(2,1)} %get-tuple-element.20), channel_id=1, source_target_pairs={{0,3},{1,0},{2,1},{3,2},{4,7},{5,4},{6,5},{7,6},{8,11},{9,8},{10,9... | collective-permute-start | bytes 1179656 | tf_op jit(solution)/shard_map/ppermute | solution.py:397
  21.1 2.5 %collective-permute-start.1 = (bf16[24,64,128]{2,1,0:T(8,128)(2,1)}, bf16[24,64,128]{2,1,0:T(8,128)(2,1)S(1)}, u32[]{:S(2)}, u32[]{:S(2)}) collective-permute-start(bf16[24,64,128]{2,1,0:T(8,128)(2,1)} %get-tuple-element.21), channel_id=1, source_target_pairs={{0,2},{1,3},{2,0},{3,1},{4,6},{5,7},{6,4},{7,5},{8,10},{9,11},{10,... | collective-permute-start | bytes 1179656 | tf_op jit(solution)/shard_map/ppermute | solution.py:397
  23.6 2.5 %collective-permute-start.2 = (bf16[24,64,128]{2,1,0:T(8,128)(2,1)}, bf16[24,64,128]{2,1,0:T(8,128)(2,1)S(1)}, u32[]{:S(2)}, u32[]{:S(2)}) collective-permute-start(bf16[24,64,128]{2,1,0:T(8,128)(2,1)} %get-tuple-element.22), channel_id=1, source_target_pairs={{0,1},{1,2},{2,3},{3,0},{4,5},{5,6},{6,7},{7,4},{8,9},{9,10},{10,1... | collective-permute-start | bytes 1179656 | tf_op jit(solution)/shard_map/ppermute | solution.py:397
  26.1 0.8 copy-done.3
  27.0 0.8 copy-done.4
  27.7 0.8 copy-done.5
  28.5 1.4 %shard_map.97 = (f32[28,64,128]{2,1,0:T(8,128)}, bf16[6,64,128]{2,1,0:T(8,128)(2,1)S(1)}, bf16[6,64,128]{2,1,0:T(8,128)(2,1)S(1)}, bf16[64,128]{1,0:T(8,128)(2,1)S(1)}, bf16[64,128]{1,0:T(8,128)(2,1)S(1)}) custom-call(bf16[4,24,64,128]{3,2,1,0:T(8,128)(2,1)S(1)} %all-to-all-done.snaps_ref.direct_ref, bf16[64,256]{1,0:T(8,128)(2,1)S(1)} %copy-done.5, ...), custom_call_target="tpu_custom_call" | custom-call | flops 100663296 | bytes 2097152 | tf_op jit(solution)/shard_map/pallas_call | solution.py:338
  29.9 9.2 %collective-permute-start.3 = (bf16[6,64,128]{2,1,0:T(8,128)(2,1)S(1)}, bf16[6,64,128]{2,1,0:T(8,128)(2,1)S(1)}, u32[]{:S(2)}, u32[]{:S(2)}) collective-permute-start(bf16[6,64,128]{2,1,0:T(8,128)(2,1)S(1)} %get-tuple-element.27), channel_id=1, source_target_pairs={{0,4},{4,8},{8,12},{12,16},{16,20},{20,24},{24,28},{28,32},{32,36}... | collective-permute-start | bytes 294920 | tf_op jit(solution)/shard_map/ppermute | solution.py:415
  39.1 1.9 %collective-permute-start.4 = (bf16[6,64,128]{2,1,0:T(8,128)(2,1)S(1)}, bf16[6,64,128]{2,1,0:T(8,128)(2,1)S(1)}, u32[]{:S(2)}, u32[]{:S(2)}) collective-permute-start(bf16[6,64,128]{2,1,0:T(8,128)(2,1)S(1)} %get-tuple-element.28), channel_id=1, source_target_pairs={{4,0},{8,4},{12,8},{16,12},{20,16},{24,20},{28,24},{32,28},{36,32}... | collective-permute-start | bytes 294920 | tf_op jit(solution)/shard_map/ppermute | solution.py:416
  41.0 5.5 %collective-permute-start.5 = (bf16[64,128]{1,0:T(8,128)(2,1)S(1)}, bf16[64,128]{1,0:T(8,128)(2,1)S(1)}, u32[]{:S(2)}, u32[]{:S(2)}) collective-permute-start(bf16[64,128]{1,0:T(8,128)(2,1)S(1)} %get-tuple-element.29), channel_id=1, source_target_pairs={{0,1},{1,2},{2,3},{4,5},{5,6},{6,7},{8,9},{9,10},{10,11},{12,13},{... | collective-permute-start | bytes 49160 | tf_op jit(solution)/shard_map/ppermute | solution.py:417
  46.6 1.3 %collective-permute-start.6 = (bf16[64,128]{1,0:T(8,128)(2,1)S(1)}, bf16[64,128]{1,0:T(8,128)(2,1)S(1)}, u32[]{:S(2)}, u32[]{:S(2)}) collective-permute-start(bf16[64,128]{1,0:T(8,128)(2,1)S(1)} %get-tuple-element.30), channel_id=1, source_target_pairs={{1,0},{2,1},{3,2},{5,4},{6,5},{7,6},{9,8},{10,9},{11,10},{13,12},{... | collective-permute-start | bytes 49160 | tf_op jit(solution)/shard_map/ppermute | solution.py:418
  47.9 4.2 %collective-permute-done.6.above_ref = bf16[64,128]{1,0:T(8,128)(2,1)S(1)} collective-permute-done((bf16[64,128]{1,0:T(8,128)(2,1)S(1)}, bf16[64,128]{1,0:T(8,128)(2,1)S(1)}, u32[]{:S(2)}, u32[]{:S(2)}) %collective-permute-start.6) | collective-permute-done | bytes 16416 | tf_op jit(solution)/shard_map/ppermute | solution.py:418
  52.1 3.2 %shard_map.98 = (f32[4,128,128]{2,1,0:T(8,128)S(1)}, f32[4,128,128]{2,1,0:T(8,128)S(1)}) custom-call(bf16[24,64,128]{2,1,0:T(8,128)(2,1)S(1)} %get-tuple-element.19.own_ref, bf16[24,64,128]{2,1,0:T(8,128)(2,1)S(1)} %collective-permute-done.next_ref, bf16[24,64,128]{2,1,0:T(8,128)(2,1)S(1)} %collective-permute-done.1.far_ref, ...), custom_call_target="tpu_custom_call" | custom-call | flops 1073741824 | bytes 6291456 | tf_op jit(solution)/shard_map/pallas_call | solution.py:338
  55.3 1.9 %collective-permute-start.7 = (f32[4,128,128]{2,1,0:T(8,128)S(1)}, f32[4,128,128]{2,1,0:T(8,128)S(1)}, u32[]{:S(2)}, u32[]{:S(2)}) collective-permute-start(f32[4,128,128]{2,1,0:T(8,128)S(1)} %get-tuple-element.32), channel_id=1, source_target_pairs={{0,4},{4,0},{1,5},{5,1},{2,6},{6,2},{3,7},{7,3},{8,12},{12,8},{9,1... | collective-permute-start | bytes 786440 | tf_op jit(solution)/shard_map/ppermute | solution.py:435
  57.3 1.5 %collective-permute-done.7 = f32[4,128,128]{2,1,0:T(8,128)S(1)} collective-permute-done((f32[4,128,128]{2,1,0:T(8,128)S(1)}, f32[4,128,128]{2,1,0:T(8,128)S(1)}, u32[]{:S(2)}, u32[]{:S(2)}) %collective-permute-start.7) | collective-permute-done | bytes 262176 | tf_op jit(solution)/shard_map/ppermute | solution.py:435
  58.8 9.2 %all_to_all.15 = f32[4,128,128]{2,1,0:T(8,128)S(1)} all-to-all(f32[4,128,128]{2,1,0:T(8,128)S(1)} %add.19), channel_id=1, replica_groups=mesh['z'=8,'y'=8,'core'=2,'snap'=4] {'snap'}, dimensions={0} | all-to-all | bytes 524288 | tf_op jit(solution)/shard_map/all_to_all | solution.py:436
  68.0 0.1 reshape.16
  68.2 0.1 copy.12
  68.2 0.2 reshape.17
  68.4 0.1 fusion.7
  68.5 0.1 stack_reshape.3
  68.6 0.1 pad_maximum_fusion
  68.7 29.2 %all_to_all.16.sums_ref = f32[64,2,128]{2,1,0:T(2,128)S(1)} all-to-all(f32[64,2,128]{2,1,0:T(2,128)S(1)} %pad_maximum_fusion), channel_id=1, replica_groups=mesh['z'=8,'y'=8,'core'=2,'snap'=4] {'z','y'}, dimensions={0} | all-to-all | bytes 131072 | tf_op jit(solution)/shard_map/all_to_all | solution.py:441
  97.9 0.7 shard_map.99
  (29 shorter events, 0.1 us)
Async XLA Ops:
  0.6 8.5 %copy-start = (s32[16]{0:T(128)S(1)}, s32[16]{0:T(128)}, u32[]{:S(2)}) copy-start(s32[16]{0:T(128)} %param.14) | copy-start | bytes 196
  4.0 5.0 %copy-start.10 = (f32[64]{0:T(128)S(1)}, f32[64]{0:T(128)}, u32[]{:S(2)}) copy-start(f32[64]{0:T(128)} %param.12) | copy-start | bytes 772
  4.0 5.1 %copy-start.9 = (s32[16]{0:T(128)S(1)}, s32[16]{0:T(128)}, u32[]{:S(2)}) copy-start(s32[16]{0:T(128)} %constant.43) | copy-start | bytes 196
  4.0 5.7 %copy-start.6 = (f32[256,64]{0,1:T(8,128)S(1)}, f32[256,64]{0,1:T(8,128)}, u32[]{:S(2)}) copy-start(f32[256,64]{0,1:T(8,128)} %param.11) | copy-start | bytes 196612
  4.1 5.7 %copy-start.7 = (f32[256,64]{0,1:T(8,128)S(1)}, f32[256,64]{0,1:T(8,128)}, u32[]{:S(2)}) copy-start(f32[256,64]{0,1:T(8,128)} %param.10) | copy-start | bytes 196612
  4.1 5.9 %copy-start.1 = (bf16[64,3,4,8,128]{4,3,2,1,0:T(8,128)(2,1)S(1)}, bf16[64,3,4,8,128]{4,3,2,1,0:T(8,128)(2,1)}, u32[]{:S(2)}) copy-start(bf16[64,3,4,8,128]{4,3,2,1,0:T(8,128)(2,1)} %snaps_ref.2) | copy-start | bytes 4718596
  4.1 22.1 %all-to-all-start = ((bf16[4,24,64,128]{3,2,1,0:T(8,128)(2,1)}), bf16[4,24,64,128]{3,2,1,0:T(8,128)(2,1)S(1)}, u32[]{:S(2)}, u32[]{:S(2)}) async-start(bf16[4,24,64,128]{3,2,1,0:T(8,128)(2,1)} %shard_map.96), calls=%async_computation | async-start | bytes 3145728 | tf_op jit(solution)/shard_map/all_to_all | solution.py:377
  9.9 1.0 copy-start.2
  16.6 24.5 %collective-permute-start = (bf16[24,64,128]{2,1,0:T(8,128)(2,1)}, bf16[24,64,128]{2,1,0:T(8,128)(2,1)S(1)}, u32[]{:S(2)}, u32[]{:S(2)}) collective-permute-start(bf16[24,64,128]{2,1,0:T(8,128)(2,1)} %get-tuple-element.20), channel_id=1, source_target_pairs={{0,3},{1,0},{2,1},{3,2},{4,7},{5,4},{6,5},{7,6},{8,11},{9,8},{10,9... | collective-permute-start | bytes 1179656 | tf_op jit(solution)/shard_map/ppermute | solution.py:397
  21.1 25.4 %collective-permute-start.1 = (bf16[24,64,128]{2,1,0:T(8,128)(2,1)}, bf16[24,64,128]{2,1,0:T(8,128)(2,1)S(1)}, u32[]{:S(2)}, u32[]{:S(2)}) collective-permute-start(bf16[24,64,128]{2,1,0:T(8,128)(2,1)} %get-tuple-element.21), channel_id=1, source_target_pairs={{0,2},{1,3},{2,0},{3,1},{4,6},{5,7},{6,4},{7,5},{8,10},{9,11},{10,... | collective-permute-start | bytes 1179656 | tf_op jit(solution)/shard_map/ppermute | solution.py:397
  23.6 24.3 %collective-permute-start.2 = (bf16[24,64,128]{2,1,0:T(8,128)(2,1)}, bf16[24,64,128]{2,1,0:T(8,128)(2,1)S(1)}, u32[]{:S(2)}, u32[]{:S(2)}) collective-permute-start(bf16[24,64,128]{2,1,0:T(8,128)(2,1)} %get-tuple-element.22), channel_id=1, source_target_pairs={{0,1},{1,2},{2,3},{3,0},{4,5},{5,6},{6,7},{7,4},{8,9},{9,10},{10,1... | collective-permute-start | bytes 1179656 | tf_op jit(solution)/shard_map/ppermute | solution.py:397
  26.1 0.8 copy-start.3
  27.0 0.8 copy-start.4
  27.7 0.8 copy-start.5
  29.9 22.3 %collective-permute-start.3 = (bf16[6,64,128]{2,1,0:T(8,128)(2,1)S(1)}, bf16[6,64,128]{2,1,0:T(8,128)(2,1)S(1)}, u32[]{:S(2)}, u32[]{:S(2)}) collective-permute-start(bf16[6,64,128]{2,1,0:T(8,128)(2,1)S(1)} %get-tuple-element.27), channel_id=1, source_target_pairs={{0,4},{4,8},{8,12},{12,16},{16,20},{20,24},{24,28},{28,32},{32,36}... | collective-permute-start | bytes 294920 | tf_op jit(solution)/shard_map/ppermute | solution.py:415
  39.1 13.0 %collective-permute-start.4 = (bf16[6,64,128]{2,1,0:T(8,128)(2,1)S(1)}, bf16[6,64,128]{2,1,0:T(8,128)(2,1)S(1)}, u32[]{:S(2)}, u32[]{:S(2)}) collective-permute-start(bf16[6,64,128]{2,1,0:T(8,128)(2,1)S(1)} %get-tuple-element.28), channel_id=1, source_target_pairs={{4,0},{8,4},{12,8},{16,12},{20,16},{24,20},{28,24},{32,28},{36,32}... | collective-permute-start | bytes 294920 | tf_op jit(solution)/shard_map/ppermute | solution.py:416
  41.0 6.9 %collective-permute-start.5 = (bf16[64,128]{1,0:T(8,128)(2,1)S(1)}, bf16[64,128]{1,0:T(8,128)(2,1)S(1)}, u32[]{:S(2)}, u32[]{:S(2)}) collective-permute-start(bf16[64,128]{1,0:T(8,128)(2,1)S(1)} %get-tuple-element.29), channel_id=1, source_target_pairs={{0,1},{1,2},{2,3},{4,5},{5,6},{6,7},{8,9},{9,10},{10,11},{12,13},{... | collective-permute-start | bytes 49160 | tf_op jit(solution)/shard_map/ppermute | solution.py:417
  46.6 5.6 %collective-permute-start.6 = (bf16[64,128]{1,0:T(8,128)(2,1)S(1)}, bf16[64,128]{1,0:T(8,128)(2,1)S(1)}, u32[]{:S(2)}, u32[]{:S(2)}) collective-permute-start(bf16[64,128]{1,0:T(8,128)(2,1)S(1)} %get-tuple-element.30), channel_id=1, source_target_pairs={{1,0},{2,1},{3,2},{5,4},{6,5},{7,6},{9,8},{10,9},{11,10},{13,12},{... | collective-permute-start | bytes 49160 | tf_op jit(solution)/shard_map/ppermute | solution.py:418
  55.3 13.1 %copy-start.8 = (f32[16,16]{1,0:T(8,128)S(1)}, f32[16,16]{1,0:T(8,128)}, u32[]{:S(2)}) copy-start(f32[16,16]{1,0:T(8,128)} %get-tuple-element.33) | copy-start | bytes 3076
  55.3 3.4 %collective-permute-start.7 = (f32[4,128,128]{2,1,0:T(8,128)S(1)}, f32[4,128,128]{2,1,0:T(8,128)S(1)}, u32[]{:S(2)}, u32[]{:S(2)}) collective-permute-start(f32[4,128,128]{2,1,0:T(8,128)S(1)} %get-tuple-element.32), channel_id=1, source_target_pairs={{0,4},{4,0},{1,5},{5,1},{2,6},{6,2},{3,7},{7,3},{8,12},{12,8},{9,1... | collective-permute-start | bytes 786440 | tf_op jit(solution)/shard_map/ppermute | solution.py:435

commit v8 on v7

--- a/solution.py
+++ b/solution.py
@@ -39,7 +39,9 @@
 GROUP = NZ // SNAP
 WEIGHT_AT = COMPONENTS * TILES
 COEFF_AT = WEIGHT_AT + 2
-HELD = COEFF_AT + 2
+TURNED_AT = COEFF_AT + 2
+HELD = TURNED_AT + 2
+SENT = COMPONENTS * TILES + 2
 
 
 def spread_rows(layer, out_ref, first, at):
@@ -81,14 +83,17 @@
     snaps_ref,
     left_ref,
     right_ref,
+    turned_ref,
     coeff_ref,
     selector_ref,
+    ready_ref,
     own_ref,
     next_ref,
     far_ref,
     previous_ref,
     left_out,
     right_out,
+    turned_out,
     coeff_out,
     selector_out,
     spread,
@@ -96,10 +101,30 @@
     for comp in range(COMPONENTS):
         for x in range(4):
             spread_rows(snaps_ref[:, comp, x], spread, comp * TILES + x * 2, 0)
+    place = lax.rem(lax.broadcasted_iota(jnp.int32, (COLS, NZ), 1), GROUP)
+    empty = jnp.zeros((COLS, NZ), jnp.bfloat16)
+    spread[0, SENT - 2] = empty
+    spread[SNAP - 1, SENT - 1] = empty
+    for quarter in range(SNAP):
+        low = jnp.zeros((COLS, NZ), jnp.float32)
+        high = jnp.zeros((COLS, NZ), jnp.float32)
+        for index in range(COMPONENTS * TILES):
+            wide = ready_ref[quarter, index].astype(jnp.float32)
+            if quarter > 0:
+                edge = jnp.where(place == 0, wide, 0.0)
+                low = low + (pltpu.roll(edge, index, 1) if index else edge)
+            if quarter < SNAP - 1:
+                edge = jnp.where(place == GROUP - 1, wide, 0.0)
+                high = high + pltpu.roll(edge, NZ + index - (GROUP - 1), 1)
+        if quarter > 0:
+            spread[quarter - 1, SENT - 1] = low.astype(jnp.bfloat16)
+        if quarter < SNAP - 1:
+            spread[quarter + 1, SENT - 2] = high.astype(jnp.bfloat16)
     for n, ref in enumerate((own_ref, next_ref, far_ref, previous_ref)):
         ref[...] = spread[lax.rem(snap_ref[0] + n, SNAP)]
     left_out[...] = left_ref[...]
     right_out[...] = right_ref[...]
+    turned_out[...] = turned_ref[...]
     selector_out[...] = selector_ref[...]
     shift = lax.rem(NZ - GROUP * snap_ref[0], NZ)
     for q in range(TERMS):
@@ -123,25 +148,15 @@
 
 
 def modes_kernel(
-    snaps_ref,
-    weight_ref,
-    adjoint_weight_ref,
-    coeff_ref,
-    held_ref,
-    first_ref,
-    last_ref,
-    low_ref,
-    high_ref,
+    snaps_ref, weight_ref, adjoint_weight_ref, turned_ref, coeff_ref, held_ref, first_ref, last_ref
 ):
     for n in range(2):
-        wide = adjoint_weight_ref[:, n * NZ : (n + 1) * NZ].astype(jnp.float32)
-        held_ref[WEIGHT_AT + n] = wide
+        half = slice(n * NZ, (n + 1) * NZ)
+        held_ref[WEIGHT_AT + n] = adjoint_weight_ref[:, half].astype(jnp.float32)
+        held_ref[TURNED_AT + n] = turned_ref[:, half].astype(jnp.float32)
         held_ref[COEFF_AT + n] = coeff_ref[n * R : (n + 1) * R, :]
     weight = weight_ref[...]
     blocks = [snaps_ref.at[n] for n in range(SNAP)]
-    place = lax.rem(lax.broadcasted_iota(jnp.int32, (R, NZ), 1), GROUP)
-    low = jnp.zeros((R, NZ), jnp.float32)
-    high = jnp.zeros((R, NZ), jnp.float32)
     for comp in range(COMPONENTS):
         for t in range(0, TILES, 2):
             block = columns(blocks, comp, (t, t + 1))
@@ -149,19 +164,11 @@
             modes = modes.astype(jnp.bfloat16)
             for half in range(2):
                 tile = modes[:, half * NZ : (half + 1) * NZ]
-                index = comp * TILES + t + half
-                wide = tile.astype(jnp.float32)
-                held_ref[index] = wide
+                held_ref[comp * TILES + t + half] = tile.astype(jnp.float32)
                 if t == 0:
                     first_ref[comp * 2 + half] = tile
                 if t == TILES - 2:
                     last_ref[comp * 2 + half] = tile
-                edge = jnp.where(place == 0, wide, 0.0)
-                low = low + (pltpu.roll(edge, index, 1) if index else edge)
-                edge = jnp.where(place == GROUP - 1, wide, 0.0)
-                high = high + pltpu.roll(edge, NZ + index - (GROUP - 1), 1)
-    low_ref[...] = low.astype(jnp.bfloat16)
-    high_ref[...] = high.astype(jnp.bfloat16)
 
 
 def weighted_terms(comp, held_ref, before, after, below, above, out_ref):
@@ -236,8 +243,6 @@
     held_hbm,
     before_ref,
     after_ref,
-    below_ref,
-    above_ref,
     keep_ref,
     send_ref,
     held_ref,
@@ -263,12 +268,15 @@
                 preferred_element_type=jnp.float32,
             )
     fetch.wait()
-    below = below_ref[...].astype(jnp.float32)
-    above = above_ref[...].astype(jnp.float32)
+    turned, weight = (
+        jnp.concatenate([held_ref[at], held_ref[at + 1]], axis=1).astype(jnp.bfloat16)
+        for at in (TURNED_AT, WEIGHT_AT)
+    )
+    edges = jnp.dot(turned, columns(adjoints, COMPONENTS, (0, 1)), preferred_element_type=jnp.float32)
+    edges = edges.astype(jnp.bfloat16).astype(jnp.float32)
+    below, above = edges[:, :NZ], edges[:, NZ:]
     before = [before_ref[n].astype(jnp.float32) for n in range(6)]
     after = [after_ref[n].astype(jnp.float32) for n in range(6)]
-    weight = jnp.concatenate([held_ref[WEIGHT_AT], held_ref[WEIGHT_AT + 1]], axis=1)
-    weight = weight.astype(jnp.bfloat16)
     for comp in range(COMPONENTS):
         for t in range(0, TILES, 2):
             adjoint = columns(adjoints, comp, (t, t + 1))
@@ -350,9 +358,10 @@
 
 def shards(direct_snaps, adjoint_snaps, left_factor, right_factor, singular, term_coeff, term_slot):
     scale = 1.0 / math.sqrt(1572864)
-    turned = jnp.roll(left_factor, -COLS * lax.axis_index("snap"), axis=0)
-    left = mode_weight(turned, singular).T
+    back = -COLS * lax.axis_index("snap")
+    left = mode_weight(jnp.roll(left_factor, back, axis=0), singular).T
     right = mode_weight(right_factor, singular).T
+    turned = jnp.roll(right, back, axis=1)
     tiles = COMPONENTS * TILES
 
     def shape(*dims, dtype=jnp.bfloat16):
@@ -379,10 +388,11 @@
         term_slot[jnp.array(ORDER)][None, :] == jnp.arange(TERMS, dtype=jnp.int32)[:, None]
     ).astype(jnp.float32)
     here = lax.axis_index("snap").astype(jnp.int32).reshape(1)
-    own, *others, adjoint_weight, direct_weight, coeff, selector = call(
+    own, *others, adjoint_weight, direct_weight, turned, coeff, selector = call(
         adjoint_kernel,
         (
-            *[shape(tiles, COLS, NZ)] * SNAP,
+            *[shape(SENT, COLS, NZ)] * SNAP,
+            pltpu.HBM((R, M), jnp.bfloat16),
             pltpu.HBM((R, M), jnp.bfloat16),
             pltpu.HBM((R, M), jnp.bfloat16),
             pltpu.HBM((TERMS * TILES, NZ), jnp.float32),
@@ -390,32 +400,24 @@
         ),
         0,
         3 << 20,
-        (pltpu.VMEM((SNAP, tiles, COLS, NZ), jnp.bfloat16),),
+        (pltpu.VMEM((SNAP, SENT, COLS, NZ), jnp.bfloat16),),
         {0: pltpu.SMEM},
-    )(here, adjoint_snaps, left, right, term_coeff, selector)
+    )(here, adjoint_snaps, left, right, turned, term_coeff, selector, ready)
     arrived = [
         lax.ppermute(piece, "snap", [(i, (i + n) % SNAP) for i in range(SNAP)])
         for n, piece in enumerate(others, 1)
     ]
     adjoints = (own, *arrived[::-1])
-    held, first, last, low, high = call(
+    held, first, last = call(
         modes_kernel,
-        (
-            pltpu.HBM((HELD, R, NZ), jnp.float32),
-            shape(6, R, NZ),
-            shape(6, R, NZ),
-            shape(R, NZ),
-            shape(R, NZ),
-        ),
+        (pltpu.HBM((HELD, R, NZ), jnp.float32), shape(6, R, NZ), shape(6, R, NZ)),
         2 * R * M * 3 * CELLS,
         2 << 20,
-    )(direct, direct_weight, adjoint_weight, coeff)
+    )(direct, direct_weight, adjoint_weight, turned, coeff)
     held = pltpu.with_memory_space_constraint(held, pltpu.HBM)
-    slabs, quarters = ([(i, i + 1) for i in range(n - 1)] for n in (128, SNAP))
+    slabs = [(i, i + 1) for i in range(127)]
     before = lax.ppermute(last, SPACE, slabs)
     after = lax.ppermute(first, SPACE, [(j, i) for i, j in slabs])
-    below = lax.ppermute(high, "snap", quarters)
-    above = lax.ppermute(low, "snap", [(j, i) for i, j in quarters])
     half = shape(SNAP, 128, NZ, dtype=jnp.float32)
     keep, send = call(
         functools.partial(products_kernel, scale),
@@ -431,7 +433,7 @@
             pltpu.SemaphoreType.DMA,
         ),
         {5: pltpu.HBM},
-    )(*adjoints, direct, held, before, after, below, above)
+    )(*adjoints, direct, held, before, after)
     terms = keep + lax.ppermute(send, "core", [(0, 1), (1, 0)])
     near = lax.all_to_all(terms, "snap", 0, 0, tiled=True).sum(axis=0)
     gram = near[:64]

time: 100 us -> 96.3 us (0.963)
  starting transfers between devices: 34.4 us -> 29.6 us
  local copies, waits for them, and re-layouts: 4.4 us -> 6.38 us
  waiting for transfers between devices: 5.75 us -> 4.26 us
    ppermute x2 -> x0, starting transfers between devices: 6.81 us -> none  [the longest x1 5.52 us: shards(): below = lax.ppermute(high, 'snap', quarters)]
    ppermute x2 -> x0, waiting for transfers between devices: 4.24 us -> none  [the longest x1 4.23 us: shards(): above = lax.ppermute(low, 'snap', [(j, i) for i, j in quarters])]
    ppermute x1, starting transfers between devices: 9.23 us -> 6.03 us  [shards(): before = lax.ppermute(last, SPACE, slabs)]
    ppermute x3, waiting for transfers between devices: 0.01 us -> 3.12 us  [shards(): lax.ppermute(piece, 'snap', [(i, (i + n) % SNAP) for i in range(SNAP)])]
    ppermute x1, starting transfers between devices: 1.92 us -> 5.01 us  [shards(): terms = keep + lax.ppermute(send, 'core', [(0, 1), (1, 0)])]
    unnamed x22 -> x30, local copies, waits for them, and re-layouts: 3.34 us -> 5.32 us
    ppermute x1, starting transfers between devices: 1.92 us -> 3.85 us  [shards(): after = lax.ppermute(first, SPACE, [(j, i) for i, j in slabs])]
    all_to_all x1, blocking collectives: 29.2 us -> 27.4 us  [shards(): sums = lax.all_to_all(owned, ('z', 'y'), 0, 0, tiled=True)]
  transfers between devices with their start and end apart: 9 -> 7, of which waited for: 2 -> 2; matrix products, arithmetic and copies ran while one was open for 1% -> 1% of each run, Pallas kernels for 7% -> 8%
where the time goes in v8:
time: 96.3 us; the launch traced here: 95.2 us
  blocking collectives  38.4 us (40%)
  starting transfers between devices  29.6 us (31%)
  Pallas kernels  15.1 us (16%)
  local copies, waits for them, and re-layouts  6.38 us (7%)
  waiting for transfers between devices  4.26 us (4%)
    all_to_all x1, blocking collectives, shards(): sums = lax.all_to_all(owned, ('z', 'y'), 0, 0, tiled=True)  27.4 us
    pallas_call x5, Pallas kernels, run(): pl.pallas_call(kernel, out_shape=out_shape, in_specs=[pl.BlockSpec(memory...  15.1 us
    all_to_all x1, blocking collectives, shards(): near = lax.all_to_all(terms, 'snap', 0, 0, tiled=True).sum(axis=0)  11 us
    ppermute x3, starting transfers between devices, shards(): lax.ppermute(piece, 'snap', [(i, (i + n) % SNAP) for i in range(SNAP)])  9.67 us
    ppermute x1, starting transfers between devices, shards(): before = lax.ppermute(last, SPACE, slabs)  6.03 us
    unnamed x30, local copies, waits for them, and re-layouts  5.32 us
    ppermute x1, starting transfers between devices, shards(): terms = keep + lax.ppermute(send, 'core', [(0, 1), (1, 0)])  5.01 us
    all_to_all x1, starting transfers between devices, shards(): direct = lax.all_to_all(ready, 'snap', 0, 0, tiled=True)  4.99 us
  transfers between devices with their start and end apart: 7, of which 2 were waited for; matrix products, arithmetic and copies ran while one was open for 1% of the time, Pallas kernels for 8%

profile of v8, /device:TPU:1, one launch (start us, length us, event | category | flops | bytes accessed | tf_op | source)
XLA Modules:
  0.0 95.2 jit_solution(7220905008572855660)
XLA Ops:
  0.6 0.0 copy-start
  0.6 3.4 %shard_map.95.ready_ref = bf16[4,24,64,128]{3,2,1,0:T(8,128)(2,1)} custom-call(bf16[64,3,4,8,128]{4,3,2,1,0:T(8,128)(2,1)} %snaps_ref.2), custom_call_target="tpu_custom_call" | custom-call | bytes 3145728 | tf_op jit(solution)/shard_map/pallas_call | solution.py:346
  4.1 5.0 %all-to-all-start = ((bf16[4,24,64,128]{3,2,1,0:T(8,128)(2,1)}), bf16[4,24,64,128]{3,2,1,0:T(8,128)(2,1)S(1)}, u32[]{:S(2)}, u32[]{:S(2)}) async-start(bf16[4,24,64,128]{3,2,1,0:T(8,128)(2,1)} %shard_map.95.ready_ref), calls=%async_computation | async-start | bytes 3145728 | tf_op jit(solution)/shard_map/all_to_all | solution.py:386
  9.1 0.7 gather_fusion
  9.8 0.1 fusion.4
  9.9 0.1 fusion.3.turned_ref
  10.1 1.4 %copy-done.2 = bf16[64,3,4,8,128]{4,3,2,1,0:T(8,128)(2,1)S(1)} copy-done((bf16[64,3,4,8,128]{4,3,2,1,0:T(8,128)(2,1)S(1)}, bf16[64,3,4,8,128]{4,3,2,1,0:T(8,128)(2,1)}, u32[]{:S(2)}) %copy-start.2) | copy-done | bytes 1572888
  11.5 6.4 %shard_map.96 = (bf16[26,64,128]{2,1,0:T(8,128)(2,1)S(1)}, bf16[26,64,128]{2,1,0:T(8,128)(2,1)}, bf16[26,64,128]{2,1,0:T(8,128)(2,1)}, bf16[26,64,128]{2,1,0:T(8...) custom-call(s32[1]{0:T(128)} %bitcast.snap_ref, ...), custom_call_target="tpu_custom_call" | custom-call | bytes 3145728 | tf_op jit(solution)/shard_map/pallas_call | solution.py:346
  17.9 0.8 copy-done.3
  18.7 4.7 %collective-permute-start = (bf16[26,64,128]{2,1,0:T(8,128)(2,1)}, bf16[26,64,128]{2,1,0:T(8,128)(2,1)S(1)}, u32[]{:S(2)}, u32[]{:S(2)}) collective-permute-start(bf16[26,64,128]{2,1,0:T(8,128)(2,1)} %get-tuple-element.19), channel_id=1, source_target_pairs={{0,3},{1,0},{2,1},{3,2},{4,7},{5,4},{6,5},{7,6},{8,11},{9,8},{10,9... | collective-permute-start | bytes 1277960 | tf_op jit(solution)/shard_map/ppermute | solution.py:407
  23.4 2.5 %collective-permute-start.1 = (bf16[26,64,128]{2,1,0:T(8,128)(2,1)}, bf16[26,64,128]{2,1,0:T(8,128)(2,1)S(1)}, u32[]{:S(2)}, u32[]{:S(2)}) collective-permute-start(bf16[26,64,128]{2,1,0:T(8,128)(2,1)} %get-tuple-element.20), channel_id=1, source_target_pairs={{0,2},{1,3},{2,0},{3,1},{4,6},{5,7},{6,4},{7,5},{8,10},{9,11},{10,... | collective-permute-start | bytes 1277960 | tf_op jit(solution)/shard_map/ppermute | solution.py:407
  25.9 2.5 %collective-permute-start.2 = (bf16[26,64,128]{2,1,0:T(8,128)(2,1)}, bf16[26,64,128]{2,1,0:T(8,128)(2,1)S(1)}, u32[]{:S(2)}, u32[]{:S(2)}) collective-permute-start(bf16[26,64,128]{2,1,0:T(8,128)(2,1)} %get-tuple-element.21), channel_id=1, source_target_pairs={{0,1},{1,2},{2,3},{3,0},{4,5},{5,6},{6,7},{7,4},{8,9},{9,10},{10,1... | collective-permute-start | bytes 1277960 | tf_op jit(solution)/shard_map/ppermute | solution.py:407
  28.4 0.8 copy-done.6
  29.2 0.8 copy-done.7
  30.0 0.8 copy-done.8
  30.7 0.8 copy-done.9
  31.5 1.4 %shard_map.97 = (f32[30,64,128]{2,1,0:T(8,128)}, bf16[6,64,128]{2,1,0:T(8,128)(2,1)S(1)}, bf16[6,64,128]{2,1,0:T(8,128)(2,1)S(1)}) custom-call(bf16[4,24,64,128]{3,2,1,0:T(8,128)(2,1)S(1)} %all-to-all-done.snaps_ref.direct_ref, bf16[64,256]{1,0:T(8,128)(2,1)S(1)} %copy-done.8, bf16[64,256]{1,0:T(8,128)(2,1)S(1)} %copy-done.7, bf16[64,256]{1,0:T(8,128)(2,1)S(1)} %copy-done.9, ...), custom_call_target="tpu_custom_call" | custom-call | flops 100663296 | bytes 2097152 | tf_op jit(solution)/shard_map/pallas_call | solution.py:346
  32.9 6.0 %collective-permute-start.3 = (bf16[6,64,128]{2,1,0:T(8,128)(2,1)S(1)}, bf16[6,64,128]{2,1,0:T(8,128)(2,1)S(1)}, u32[]{:S(2)}, u32[]{:S(2)}) collective-permute-start(bf16[6,64,128]{2,1,0:T(8,128)(2,1)S(1)} %get-tuple-element.27), channel_id=1, source_target_pairs={{0,4},{4,8},{8,12},{12,16},{16,20},{20,24},{24,28},{28,32},{32,36}... | collective-permute-start | bytes 294920 | tf_op jit(solution)/shard_map/ppermute | solution.py:419
  38.9 3.9 %collective-permute-start.4 = (bf16[6,64,128]{2,1,0:T(8,128)(2,1)S(1)}, bf16[6,64,128]{2,1,0:T(8,128)(2,1)S(1)}, u32[]{:S(2)}, u32[]{:S(2)}) collective-permute-start(bf16[6,64,128]{2,1,0:T(8,128)(2,1)S(1)} %get-tuple-element.28), channel_id=1, source_target_pairs={{4,0},{8,4},{12,8},{16,12},{20,16},{24,20},{28,24},{32,28},{36,32}... | collective-permute-start | bytes 294920 | tf_op jit(solution)/shard_map/ppermute | solution.py:420
  42.8 3.1 %collective-permute-done.2.previous_ref = bf16[26,64,128]{2,1,0:T(8,128)(2,1)S(1)} collective-permute-done((bf16[26,64,128]{2,1,0:T(8,128)(2,1)}, bf16[26,64,128]{2,1,0:T(8,128)(2,1)S(1)}, u32[]{:S(2)}, u32[]{:S(2)}) %collective-permute-start.2) | collective-permute-done | bytes 426016 | tf_op jit(solution)/shard_map/ppermute | solution.py:407
  45.9 3.2 %shard_map.98 = (f32[4,128,128]{2,1,0:T(8,128)S(1)}, f32[4,128,128]{2,1,0:T(8,128)S(1)}) custom-call(bf16[26,64,128]{2,1,0:T(8,128)(2,1)S(1)} %copy-done.4, bf16[26,64,128]{2,1,0:T(8,128)(2,1)S(1)} %collective-permute-done.next_ref, bf16[26,64,128]{2,1,0:T(8,128)(2,1)S(1)} %collective-permute-done.1.far_ref, ...), custom_call_target="tpu_custom_call" | custom-call | flops 1073741824 | bytes 6291456 | tf_op jit(solution)/shard_map/pallas_call | solution.py:346
  49.2 5.0 %collective-permute-start.5 = (f32[4,128,128]{2,1,0:T(8,128)S(1)}, f32[4,128,128]{2,1,0:T(8,128)S(1)}, u32[]{:S(2)}, u32[]{:S(2)}) collective-permute-start(f32[4,128,128]{2,1,0:T(8,128)S(1)} %get-tuple-element.30), channel_id=1, source_target_pairs={{0,4},{4,0},{1,5},{5,1},{2,6},{6,2},{3,7},{7,3},{8,12},{12,8},{9,1... | collective-permute-start | bytes 786440 | tf_op jit(solution)/shard_map/ppermute | solution.py:437
  54.2 1.1 %collective-permute-done.5 = f32[4,128,128]{2,1,0:T(8,128)S(1)} collective-permute-done((f32[4,128,128]{2,1,0:T(8,128)S(1)}, f32[4,128,128]{2,1,0:T(8,128)S(1)}, u32[]{:S(2)}, u32[]{:S(2)}) %collective-permute-start.5) | collective-permute-done | bytes 262176 | tf_op jit(solution)/shard_map/ppermute | solution.py:437
  55.4 11.0 %all_to_all.15 = f32[4,128,128]{2,1,0:T(8,128)S(1)} all-to-all(f32[4,128,128]{2,1,0:T(8,128)S(1)} %add.23), channel_id=1, replica_groups=mesh['z'=8,'y'=8,'core'=2,'snap'=4] {'snap'}, dimensions={0} | all-to-all | bytes 524288 | tf_op jit(solution)/shard_map/all_to_all | solution.py:438
  66.4 0.1 reshape.16
  66.5 0.1 copy.12
  66.6 0.2 reshape.17
  66.8 0.1 fusion.8
  66.9 0.1 stack_reshape.3
  67.0 0.1 pad_maximum_fusion
  67.0 27.4 %all_to_all.16.sums_ref = f32[64,2,128]{2,1,0:T(2,128)S(1)} all-to-all(f32[64,2,128]{2,1,0:T(2,128)S(1)} %pad_maximum_fusion), channel_id=1, replica_groups=mesh['z'=8,'y'=8,'core'=2,'snap'=4] {'z','y'}, dimensions={0} | all-to-all | bytes 131072 | tf_op jit(solution)/shard_map/all_to_all | solution.py:443
  94.4 0.7 shard_map.99
  (34 shorter events, 0.2 us)
Async XLA Ops:
  0.6 8.5 %copy-start = (s32[16]{0:T(128)S(1)}, s32[16]{0:T(128)}, u32[]{:S(2)}) copy-start(s32[16]{0:T(128)} %param.14) | copy-start | bytes 196
  4.0 5.1 %copy-start.14 = (f32[64]{0:T(128)S(1)}, f32[64]{0:T(128)}, u32[]{:S(2)}) copy-start(f32[64]{0:T(128)} %param.12) | copy-start | bytes 772
  4.0 5.1 %copy-start.13 = (s32[16]{0:T(128)S(1)}, s32[16]{0:T(128)}, u32[]{:S(2)}) copy-start(s32[16]{0:T(128)} %constant.53) | copy-start | bytes 196
  4.0 5.7 %copy-start.10 = (f32[256,64]{0,1:T(8,128)S(1)}, f32[256,64]{0,1:T(8,128)}, u32[]{:S(2)}) copy-start(f32[256,64]{0,1:T(8,128)} %param.11) | copy-start | bytes 196612
  4.1 5.7 %copy-start.11 = (f32[256,64]{0,1:T(8,128)S(1)}, f32[256,64]{0,1:T(8,128)}, u32[]{:S(2)}) copy-start(f32[256,64]{0,1:T(8,128)} %param.10) | copy-start | bytes 196612
  4.1 6.0 %copy-start.1 = (bf16[4,24,64,128]{3,2,1,0:T(8,128)(2,1)S(1)}, bf16[4,24,64,128]{3,2,1,0:T(8,128)(2,1)}, u32[]{:S(2)}) copy-start(bf16[4,24,64,128]{3,2,1,0:T(8,128)(2,1)} %shard_map.95.ready_ref) | copy-start | bytes 4718596
  4.1 6.0 %copy-start.5 = (f32[16,4,8,128]{3,2,1,0:T(8,128)S(1)}, f32[16,4,8,128]{3,2,1,0:T(8,128)}, u32[]{:S(2)}) copy-start(f32[16,4,8,128]{3,2,1,0:T(8,128)} %coeff_ref.1) | copy-start | bytes 786436
  4.1 24.3 %all-to-all-start = ((bf16[4,24,64,128]{3,2,1,0:T(8,128)(2,1)}), bf16[4,24,64,128]{3,2,1,0:T(8,128)(2,1)S(1)}, u32[]{:S(2)}, u32[]{:S(2)}) async-start(bf16[4,24,64,128]{3,2,1,0:T(8,128)(2,1)} %shard_map.95.ready_ref), calls=%async_computation | async-start | bytes 3145728 | tf_op jit(solution)/shard_map/all_to_all | solution.py:386
  10.1 1.4 %copy-start.2 = (bf16[64,3,4,8,128]{4,3,2,1,0:T(8,128)(2,1)S(1)}, bf16[64,3,4,8,128]{4,3,2,1,0:T(8,128)(2,1)}, u32[]{:S(2)}) copy-start(bf16[64,3,4,8,128]{4,3,2,1,0:T(8,128)(2,1)} %snaps_ref.3) | copy-start | bytes 4718596
  17.9 0.8 copy-start.3
  18.7 27.2 %copy-start.4 = (bf16[26,64,128]{2,1,0:T(8,128)(2,1)S(1)}, bf16[26,64,128]{2,1,0:T(8,128)(2,1)}, u32[]{:S(2)}) copy-start(bf16[26,64,128]{2,1,0:T(8,128)(2,1)} %copy-done.3) | copy-start | bytes 1277956
  18.7 24.1 %collective-permute-start = (bf16[26,64,128]{2,1,0:T(8,128)(2,1)}, bf16[26,64,128]{2,1,0:T(8,128)(2,1)S(1)}, u32[]{:S(2)}, u32[]{:S(2)}) collective-permute-start(bf16[26,64,128]{2,1,0:T(8,128)(2,1)} %get-tuple-element.19), channel_id=1, source_target_pairs={{0,3},{1,0},{2,1},{3,2},{4,7},{5,4},{6,5},{7,6},{8,11},{9,8},{10,9... | collective-permute-start | bytes 1277960 | tf_op jit(solution)/shard_map/ppermute | solution.py:407
  23.4 19.4 %collective-permute-start.1 = (bf16[26,64,128]{2,1,0:T(8,128)(2,1)}, bf16[26,64,128]{2,1,0:T(8,128)(2,1)S(1)}, u32[]{:S(2)}, u32[]{:S(2)}) collective-permute-start(bf16[26,64,128]{2,1,0:T(8,128)(2,1)} %get-tuple-element.20), channel_id=1, source_target_pairs={{0,2},{1,3},{2,0},{3,1},{4,6},{5,7},{6,4},{7,5},{8,10},{9,11},{10,... | collective-permute-start | bytes 1277960 | tf_op jit(solution)/shard_map/ppermute | solution.py:407
  25.9 20.0 %collective-permute-start.2 = (bf16[26,64,128]{2,1,0:T(8,128)(2,1)}, bf16[26,64,128]{2,1,0:T(8,128)(2,1)S(1)}, u32[]{:S(2)}, u32[]{:S(2)}) collective-permute-start(bf16[26,64,128]{2,1,0:T(8,128)(2,1)} %get-tuple-element.21), channel_id=1, source_target_pairs={{0,1},{1,2},{2,3},{3,0},{4,5},{5,6},{6,7},{7,4},{8,9},{9,10},{10,1... | collective-permute-start | bytes 1277960 | tf_op jit(solution)/shard_map/ppermute | solution.py:407
  28.4 0.8 copy-start.6
  29.2 0.8 copy-start.7
  30.0 0.8 copy-start.8
  30.7 0.8 copy-start.9
  32.9 13.0 %collective-permute-start.3 = (bf16[6,64,128]{2,1,0:T(8,128)(2,1)S(1)}, bf16[6,64,128]{2,1,0:T(8,128)(2,1)S(1)}, u32[]{:S(2)}, u32[]{:S(2)}) collective-permute-start(bf16[6,64,128]{2,1,0:T(8,128)(2,1)S(1)} %get-tuple-element.27), channel_id=1, source_target_pairs={{0,4},{4,8},{8,12},{12,16},{16,20},{20,24},{24,28},{28,32},{32,36}... | collective-permute-start | bytes 294920 | tf_op jit(solution)/shard_map/ppermute | solution.py:419
  38.9 7.0 %collective-permute-start.4 = (bf16[6,64,128]{2,1,0:T(8,128)(2,1)S(1)}, bf16[6,64,128]{2,1,0:T(8,128)(2,1)S(1)}, u32[]{:S(2)}, u32[]{:S(2)}) collective-permute-start(bf16[6,64,128]{2,1,0:T(8,128)(2,1)S(1)} %get-tuple-element.28), channel_id=1, source_target_pairs={{4,0},{8,4},{12,8},{16,12},{20,16},{24,20},{28,24},{32,28},{36,32}... | collective-permute-start | bytes 294920 | tf_op jit(solution)/shard_map/ppermute | solution.py:420
  49.2 17.6 %copy-start.12 = (f32[16,16]{1,0:T(8,128)S(1)}, f32[16,16]{1,0:T(8,128)}, u32[]{:S(2)}) copy-start(f32[16,16]{1,0:T(8,128)} %get-tuple-element.31) | copy-start | bytes 3076
  49.2 6.2 %collective-permute-start.5 = (f32[4,128,128]{2,1,0:T(8,128)S(1)}, f32[4,128,128]{2,1,0:T(8,128)S(1)}, u32[]{:S(2)}, u32[]{:S(2)}) collective-permute-start(f32[4,128,128]{2,1,0:T(8,128)S(1)} %get-tuple-element.30), channel_id=1, source_target_pairs={{0,4},{4,0},{1,5},{5,1},{2,6},{6,2},{3,7},{7,3},{8,12},{12,8},{9,1... | collective-permute-start | bytes 786440 | tf_op jit(solution)/shard_map/ppermute | solution.py:437

commit v9 on v8

--- a/solution.py
+++ b/solution.py
@@ -37,10 +37,10 @@
 
 TILES = 8
 GROUP = NZ // SNAP
-WEIGHT_AT = COMPONENTS * TILES
+WEIGHT_AT = 0
 COEFF_AT = WEIGHT_AT + 2
 TURNED_AT = COEFF_AT + 2
-HELD = TURNED_AT + 2
+EXTRAS = TURNED_AT + 2
 SENT = COMPONENTS * TILES + 2
 
 
@@ -81,23 +81,16 @@
 def adjoint_kernel(
     snap_ref,
     snaps_ref,
-    left_ref,
-    right_ref,
-    turned_ref,
-    coeff_ref,
-    selector_ref,
     ready_ref,
+    weight_ref,
     own_ref,
     next_ref,
     far_ref,
     previous_ref,
-    left_out,
-    right_out,
-    turned_out,
-    coeff_out,
-    selector_out,
+    weight_out,
     spread,
 ):
+    weight_out[...] = weight_ref[...]
     for comp in range(COMPONENTS):
         for x in range(4):
             spread_rows(snaps_ref[:, comp, x], spread, comp * TILES + x * 2, 0)
@@ -122,17 +115,21 @@
             spread[quarter + 1, SENT - 2] = high.astype(jnp.bfloat16)
     for n, ref in enumerate((own_ref, next_ref, far_ref, previous_ref)):
         ref[...] = spread[lax.rem(snap_ref[0] + n, SNAP)]
-    left_out[...] = left_ref[...]
-    right_out[...] = right_ref[...]
-    turned_out[...] = turned_ref[...]
+
+
+def extras_kernel(snap_ref, left_ref, turned_ref, coeff_ref, selector_ref, _, out_ref, selector_out):
     selector_out[...] = selector_ref[...]
+    for n in range(2):
+        half = slice(n * NZ, (n + 1) * NZ)
+        out_ref[WEIGHT_AT + n] = left_ref[:, half].astype(jnp.float32)
+        out_ref[TURNED_AT + n] = turned_ref[:, half].astype(jnp.float32)
     shift = lax.rem(NZ - GROUP * snap_ref[0], NZ)
     for q in range(TERMS):
         for x in range(4):
             own = pltpu.roll(coeff_ref[q, x], shift, 1)
             for half in range(2):
                 row = q * TILES + x * 2 + half
-                coeff_out[row : row + 1, :] = jnp.concatenate(
+                out_ref[COEFF_AT + row // R, row % R : row % R + 1, :] = jnp.concatenate(
                     [own[half * 4 + i : half * 4 + i + 1, :GROUP] for i in range(4)], axis=1
                 )
 
@@ -147,14 +144,7 @@
     )
 
 
-def modes_kernel(
-    snaps_ref, weight_ref, adjoint_weight_ref, turned_ref, coeff_ref, held_ref, first_ref, last_ref
-):
-    for n in range(2):
-        half = slice(n * NZ, (n + 1) * NZ)
-        held_ref[WEIGHT_AT + n] = adjoint_weight_ref[:, half].astype(jnp.float32)
-        held_ref[TURNED_AT + n] = turned_ref[:, half].astype(jnp.float32)
-        held_ref[COEFF_AT + n] = coeff_ref[n * R : (n + 1) * R, :]
+def modes_kernel(snaps_ref, weight_ref, out_ref, first_ref, last_ref):
     weight = weight_ref[...]
     blocks = [snaps_ref.at[n] for n in range(SNAP)]
     for comp in range(COMPONENTS):
@@ -164,14 +154,14 @@
             modes = modes.astype(jnp.bfloat16)
             for half in range(2):
                 tile = modes[:, half * NZ : (half + 1) * NZ]
-                held_ref[comp * TILES + t + half] = tile.astype(jnp.float32)
+                out_ref[comp * TILES + t + half] = tile.astype(jnp.float32)
                 if t == 0:
                     first_ref[comp * 2 + half] = tile
                 if t == TILES - 2:
                     last_ref[comp * 2 + half] = tile
 
 
-def weighted_terms(comp, held_ref, before, after, below, above, out_ref):
+def weighted_terms(comp, modes_ref, extras_ref, before, after, below, above, out_ref):
     lane = lax.broadcasted_iota(jnp.int32, (R, NZ), 1)
     place = lax.rem(lane, GROUP)
     base = [0]
@@ -183,13 +173,13 @@
         count = len(MEMBERS[target])
         at = MEMBERS[target].index(q)
         row = (q * TILES + t) % R
-        coeff = held_ref[COEFF_AT + q * TILES // R, row : row + 1, :]
+        coeff = extras_ref[COEFF_AT + q * TILES // R, row : row + 1, :]
         value = (value * coeff).astype(jnp.bfloat16)
         for block in range(SNAP):
             row = base[target] + (block * count + at) * OWN
             out_ref[row : row + OWN, t * NZ : (t + 1) * NZ] = value[block * OWN : (block + 1) * OWN]
 
-    field = [held_ref[comp * TILES + t] for t in range(TILES)]
+    field = [modes_ref[comp * TILES + t] for t in range(TILES)]
     down = before[comp * 2 : comp * 2 + 2] + field[:-2]
     up = field[2:] + after[comp * 2 : comp * 2 + 2]
     for x in range(4):
@@ -240,20 +230,26 @@
     far_ref,
     previous_ref,
     direct_ref,
-    held_hbm,
+    modes_hbm,
+    extras_hbm,
     before_ref,
     after_ref,
     keep_ref,
     send_ref,
-    held_ref,
+    modes_ref,
+    extras_ref,
     gram_ref,
     parts_ref,
     weighted_ref,
     out_ref,
-    sem,
+    sems,
 ):
-    fetch = pltpu.make_async_copy(held_hbm, held_ref, sem)
-    fetch.start()
+    fetches = [
+        pltpu.make_async_copy(modes_hbm, modes_ref, sems.at[0]),
+        pltpu.make_async_copy(extras_hbm, extras_ref, sems.at[1]),
+    ]
+    for fetch in fetches:
+        fetch.start()
     adjoints = (own_ref, next_ref, far_ref, previous_ref)
     directs = [direct_ref.at[n] for n in range(SNAP)]
     here = lax.axis_index("snap")
@@ -267,9 +263,10 @@
                 transposed,
                 preferred_element_type=jnp.float32,
             )
-    fetch.wait()
+    for fetch in fetches:
+        fetch.wait()
     turned, weight = (
-        jnp.concatenate([held_ref[at], held_ref[at + 1]], axis=1).astype(jnp.bfloat16)
+        jnp.concatenate([extras_ref[at], extras_ref[at + 1]], axis=1).astype(jnp.bfloat16)
         for at in (TURNED_AT, WEIGHT_AT)
     )
     edges = jnp.dot(turned, columns(adjoints, COMPONENTS, (0, 1)), preferred_element_type=jnp.float32)
@@ -287,7 +284,7 @@
             low = (rest - middle.astype(jnp.float32)).astype(jnp.bfloat16)
             for part, value in enumerate((high, middle, low)):
                 parts_ref[comp, part * R : (part + 1) * R, t * NZ : (t + 2) * NZ] = value
-        weighted_terms(comp, held_ref, before, after, below, above, weighted_ref)
+        weighted_terms(comp, modes_ref, extras_ref, before, after, below, above, weighted_ref)
     gram = gram * scale
     gram_ref[0] = gram[:, :NZ]
     gram_ref[1] = gram[:, NZ:]
@@ -388,33 +385,39 @@
         term_slot[jnp.array(ORDER)][None, :] == jnp.arange(TERMS, dtype=jnp.int32)[:, None]
     ).astype(jnp.float32)
     here = lax.axis_index("snap").astype(jnp.int32).reshape(1)
-    own, *others, adjoint_weight, direct_weight, turned, coeff, selector = call(
+    piece = (SENT, COLS, NZ)
+    own, *others, direct_weight = call(
         adjoint_kernel,
         (
-            *[shape(SENT, COLS, NZ)] * SNAP,
+            pltpu.HBM(piece, jnp.bfloat16),
+            *[shape(*piece)] * (SNAP - 1),
             pltpu.HBM((R, M), jnp.bfloat16),
-            pltpu.HBM((R, M), jnp.bfloat16),
-            pltpu.HBM((R, M), jnp.bfloat16),
-            pltpu.HBM((TERMS * TILES, NZ), jnp.float32),
-            pltpu.HBM((TERMS, TERMS), jnp.float32),
         ),
         0,
         3 << 20,
-        (pltpu.VMEM((SNAP, SENT, COLS, NZ), jnp.bfloat16),),
+        (pltpu.VMEM((SNAP, *piece), jnp.bfloat16),),
         {0: pltpu.SMEM},
-    )(here, adjoint_snaps, left, right, turned, term_coeff, selector, ready)
+    )(here, adjoint_snaps, ready, right)
     arrived = [
         lax.ppermute(piece, "snap", [(i, (i + n) % SNAP) for i in range(SNAP)])
         for n, piece in enumerate(others, 1)
     ]
     adjoints = (own, *arrived[::-1])
-    held, first, last = call(
+    modes, first, last = call(
         modes_kernel,
-        (pltpu.HBM((HELD, R, NZ), jnp.float32), shape(6, R, NZ), shape(6, R, NZ)),
+        (pltpu.HBM((tiles, R, NZ), jnp.float32), shape(6, R, NZ), shape(6, R, NZ)),
         2 * R * M * 3 * CELLS,
         2 << 20,
-    )(direct, direct_weight, adjoint_weight, turned, coeff)
-    held = pltpu.with_memory_space_constraint(held, pltpu.HBM)
+    )(direct, direct_weight)
+    modes = pltpu.with_memory_space_constraint(modes, pltpu.HBM)
+    extras, selector = call(
+        extras_kernel,
+        (pltpu.HBM((EXTRAS, R, NZ), jnp.float32), pltpu.HBM((TERMS, TERMS), jnp.float32)),
+        0,
+        1 << 20,
+        inputs={0: pltpu.SMEM, 5: pltpu.HBM},
+    )(here, left, turned, term_coeff, selector, modes)
+    extras = pltpu.with_memory_space_constraint(extras, pltpu.HBM)
     slabs = [(i, i + 1) for i in range(127)]
     before = lax.ppermute(last, SPACE, slabs)
     after = lax.ppermute(first, SPACE, [(j, i) for i, j in slabs])
@@ -425,15 +428,16 @@
         1 << 30,
         6 << 20,
         (
-            pltpu.VMEM((HELD, R, NZ), jnp.float32),
+            pltpu.VMEM(modes.shape, jnp.float32),
+            pltpu.VMEM(extras.shape, jnp.float32),
             pltpu.VMEM((2, M, NZ), jnp.float32),
             pltpu.VMEM((COMPONENTS, 3 * R, CELLS), jnp.bfloat16),
             pltpu.VMEM((TERMS * R, CELLS), jnp.bfloat16),
             pltpu.VMEM((2 * SNAP, 128, NZ), jnp.float32),
-            pltpu.SemaphoreType.DMA,
+            pltpu.SemaphoreType.DMA((2,)),
         ),
-        {5: pltpu.HBM},
-    )(*adjoints, direct, held, before, after)
+        {5: pltpu.HBM, 6: pltpu.HBM},
+    )(*adjoints, direct, modes, extras, before, after)
     terms = keep + lax.ppermute(send, "core", [(0, 1), (1, 0)])
     near = lax.all_to_all(terms, "snap", 0, 0, tiled=True).sum(axis=0)
     gram = near[:64]

time: 96.3 us -> 94.7 us (0.983)
  local copies, waits for them, and re-layouts: 6.38 us -> 3.31 us
  starting transfers between devices: 29.6 us -> 32.2 us
  blocking collectives: 38.4 us -> 36.7 us
    ppermute x1, starting transfers between devices: 6.03 us -> 11.2 us  [shards(): before = lax.ppermute(last, SPACE, slabs)]
    unnamed x30 -> x22, local copies, waits for them, and re-layouts: 5.32 us -> 2.25 us
    ppermute x1, starting transfers between devices: 5.01 us -> 2.44 us  [shards(): terms = keep + lax.ppermute(send, 'core', [(0, 1), (1, 0)])]
    all_to_all x1, blocking collectives: 11 us -> 9.36 us  [shards(): near = lax.all_to_all(terms, 'snap', 0, 0, tiled=True).sum(axis=0)]
    pallas_call x5 -> x6, Pallas kernels: 15.1 us -> 14.9 us  [run(): pl.pallas_call(kernel, out_shape=out_shape, in_specs=[pl.BlockSpec(memory...]
where the time goes in v9:
time: 94.7 us; the launch traced here: 93.5 us
  blocking collectives  36.7 us (39%)
  starting transfers between devices  32.2 us (34%)
  Pallas kernels  14.9 us (16%)
  waiting for transfers between devices  4.94 us (5%)
  local copies, waits for them, and re-layouts  3.31 us (3%)
    all_to_all x1, blocking collectives, shards(): sums = lax.all_to_all(owned, ('z', 'y'), 0, 0, tiled=True)  27.4 us
    pallas_call x6, Pallas kernels, run(): pl.pallas_call(kernel, out_shape=out_shape, in_specs=[pl.BlockSpec(memory...  14.9 us
    ppermute x1, starting transfers between devices, shards(): before = lax.ppermute(last, SPACE, slabs)  11.2 us
    ppermute x3, starting transfers between devices, shards(): lax.ppermute(piece, 'snap', [(i, (i + n) % SNAP) for i in range(SNAP)])  9.54 us
    all_to_all x1, blocking collectives, shards(): near = lax.all_to_all(terms, 'snap', 0, 0, tiled=True).sum(axis=0)  9.36 us
    all_to_all x1, starting transfers between devices, shards(): direct = lax.all_to_all(ready, 'snap', 0, 0, tiled=True)  4.99 us
    ppermute x1, starting transfers between devices, shards(): after = lax.ppermute(first, SPACE, [(j, i) for i, j in slabs])  4.03 us
    ppermute x3, waiting for transfers between devices, shards(): lax.ppermute(piece, 'snap', [(i, (i + n) % SNAP) for i in range(SNAP)])  3.79 us
  transfers between devices with their start and end apart: 7, of which 2 were waited for; matrix products, arithmetic and copies ran while one was open for 1% of the time, Pallas kernels for 8%

profile of v9, /device:TPU:1, one launch (start us, length us, event | category | flops | bytes accessed | tf_op | source)
XLA Modules:
  0.0 93.5 jit_solution(2078631652100581185)
XLA Ops:
  0.6 0.0 copy-start
  0.6 3.4 %shard_map.95.ready_ref = bf16[4,24,64,128]{3,2,1,0:T(8,128)(2,1)} custom-call(bf16[64,3,4,8,128]{4,3,2,1,0:T(8,128)(2,1)} %snaps_ref.2), custom_call_target="tpu_custom_call" | custom-call | bytes 3145728 | tf_op jit(solution)/shard_map/pallas_call | solution.py:343
  4.0 0.0 copy-start.10
  4.0 0.0 copy-start.6
  4.1 5.0 %all-to-all-start = ((bf16[4,24,64,128]{3,2,1,0:T(8,128)(2,1)}), bf16[4,24,64,128]{3,2,1,0:T(8,128)(2,1)S(1)}, u32[]{:S(2)}, u32[]{:S(2)}) async-start(bf16[4,24,64,128]{3,2,1,0:T(8,128)(2,1)} %shard_map.95.ready_ref), calls=%async_computation | async-start | bytes 3145728 | tf_op jit(solution)/shard_map/all_to_all | solution.py:383
  9.1 0.1 fusion.4
  9.2 0.0 copy-start.2
  9.2 1.4 %copy-done.2 = bf16[64,3,4,8,128]{4,3,2,1,0:T(8,128)(2,1)S(1)} copy-done((bf16[64,3,4,8,128]{4,3,2,1,0:T(8,128)(2,1)S(1)}, bf16[64,3,4,8,128]{4,3,2,1,0:T(8,128)(2,1)}, u32[]{:S(2)}) %copy-start.2) | copy-done | bytes 1572888
  10.6 3.2 %shard_map.96 = (bf16[26,64,128]{2,1,0:T(8,128)(2,1)}, bf16[26,64,128]{2,1,0:T(8,128)(2,1)}, bf16[26,64,128]{2,1,0:T(8,128)(2,1)}, bf16[26,64,128]{2,1,0:T(8,128)(2,1)}, bf16[64,256]{1,0:T(8,128)(2,1)}) custom-call(s32[1]{0:T(128)} %bitcast.snap_ref, bf16[64,3,4,8,128]{4,3,2,1,0:T(8,128)(2,1)S(1)} %copy-done.2, bf16[4,24,64,128]{3,2,1,0:T(8,128)(2,1)S(1)} %copy-done.1, ...), custom_call_target="tpu_custom_call" | custom-call | bytes 3145728 | tf_op jit(solution)/shard_map/pallas_call | solution.py:343
  13.9 4.6 %collective-permute-start = (bf16[26,64,128]{2,1,0:T(8,128)(2,1)}, bf16[26,64,128]{2,1,0:T(8,128)(2,1)S(1)}, u32[]{:S(2)}, u32[]{:S(2)}) collective-permute-start(bf16[26,64,128]{2,1,0:T(8,128)(2,1)} %get-tuple-element.17), channel_id=1, source_target_pairs={{0,3},{1,0},{2,1},{3,2},{4,7},{5,4},{6,5},{7,6},{8,11},{9,8},{10,9... | collective-permute-start | bytes 1277960 | tf_op jit(solution)/shard_map/ppermute | solution.py:402
  18.5 2.5 %collective-permute-start.1 = (bf16[26,64,128]{2,1,0:T(8,128)(2,1)}, bf16[26,64,128]{2,1,0:T(8,128)(2,1)S(1)}, u32[]{:S(2)}, u32[]{:S(2)}) collective-permute-start(bf16[26,64,128]{2,1,0:T(8,128)(2,1)} %get-tuple-element.18), channel_id=1, source_target_pairs={{0,2},{1,3},{2,0},{3,1},{4,6},{5,7},{6,4},{7,5},{8,10},{9,11},{10,... | collective-permute-start | bytes 1277960 | tf_op jit(solution)/shard_map/ppermute | solution.py:402
  21.0 2.5 %collective-permute-start.2 = (bf16[26,64,128]{2,1,0:T(8,128)(2,1)}, bf16[26,64,128]{2,1,0:T(8,128)(2,1)S(1)}, u32[]{:S(2)}, u32[]{:S(2)}) collective-permute-start(bf16[26,64,128]{2,1,0:T(8,128)(2,1)} %get-tuple-element.19), channel_id=1, source_target_pairs={{0,1},{1,2},{2,3},{3,0},{4,5},{5,6},{6,7},{7,4},{8,9},{9,10},{10,1... | collective-permute-start | bytes 1277960 | tf_op jit(solution)/shard_map/ppermute | solution.py:402
  23.5 0.7 gather_fusion
  24.2 0.8 copy-done.5
  25.0 1.3 %shard_map.97 = (f32[24,64,128]{2,1,0:T(8,128)}, bf16[6,64,128]{2,1,0:T(8,128)(2,1)S(1)}, bf16[6,64,128]{2,1,0:T(8,128)(2,1)S(1)}) custom-call(bf16[4,24,64,128]{3,2,1,0:T(8,128)(2,1)S(1)} %all-to-all-done.snaps_ref.direct_ref, bf16[64,256]{1,0:T(8,128)(2,1)S(1)} %copy-done.5), custom_call_target="tpu_custom_call" | custom-call | flops 100663296 | bytes 2097152 | tf_op jit(solution)/shard_map/pallas_call | solution.py:343
  26.3 11.2 %collective-permute-start.3 = (bf16[6,64,128]{2,1,0:T(8,128)(2,1)S(1)}, bf16[6,64,128]{2,1,0:T(8,128)(2,1)S(1)}, u32[]{:S(2)}, u32[]{:S(2)}) collective-permute-start(bf16[6,64,128]{2,1,0:T(8,128)(2,1)S(1)} %get-tuple-element.23), channel_id=1, source_target_pairs={{0,4},{4,8},{8,12},{12,16},{16,20},{20,24},{24,28},{28,32},{32,36}... | collective-permute-start | bytes 294920 | tf_op jit(solution)/shard_map/ppermute | solution.py:422
  37.5 4.0 %collective-permute-start.4 = (bf16[6,64,128]{2,1,0:T(8,128)(2,1)S(1)}, bf16[6,64,128]{2,1,0:T(8,128)(2,1)S(1)}, u32[]{:S(2)}, u32[]{:S(2)}) collective-permute-start(bf16[6,64,128]{2,1,0:T(8,128)(2,1)S(1)} %get-tuple-element.24), channel_id=1, source_target_pairs={{4,0},{8,4},{12,8},{16,12},{20,16},{24,20},{28,24},{32,28},{36,32}... | collective-permute-start | bytes 294920 | tf_op jit(solution)/shard_map/ppermute | solution.py:423
  41.5 0.1 fusion.3.turned_ref
  41.6 3.0 %shard_map.98 = (f32[6,64,128]{2,1,0:T(8,128)}, f32[16,16]{1,0:T(8,128)}) custom-call(s32[1]{0:T(128)} %bitcast.snap_ref, bf16[64,256]{1,0:T(8,128)(2,1)S(1)} %get-tuple-element.33.left_ref, bf16[64,256]{1,0:T(8,128)(2,1)S(1)} %fusion.3.turned_ref, f32[16,4,8,128]{3,2,1,0:T(8,128)S(1)} %copy-done.4, f32[16,16]{1,0:T(8,128)S(1)} %fusion.6.selector_ref, ...), custom_call_target="tpu_custom_call" | custom-call | bytes 1048576 | tf_op jit(solution)/shard_map/pallas_call | solution.py:343
  44.7 3.8 %collective-permute-done.2.previous_ref = bf16[26,64,128]{2,1,0:T(8,128)(2,1)S(1)} collective-permute-done((bf16[26,64,128]{2,1,0:T(8,128)(2,1)}, bf16[26,64,128]{2,1,0:T(8,128)(2,1)S(1)}, u32[]{:S(2)}, u32[]{:S(2)}) %collective-permute-start.2) | collective-permute-done | bytes 426016 | tf_op jit(solution)/shard_map/ppermute | solution.py:402
  48.5 3.2 %shard_map.99 = (f32[4,128,128]{2,1,0:T(8,128)S(1)}, f32[4,128,128]{2,1,0:T(8,128)S(1)}) custom-call(bf16[26,64,128]{2,1,0:T(8,128)(2,1)S(1)} %copy-done.3, bf16[26,64,128]{2,1,0:T(8,128)(2,1)S(1)} %collective-permute-done.next_ref, bf16[26,64,128]{2,1,0:T(8,128)(2,1)S(1)} %collective-permute-done.1.far_ref, ...), custom_call_target="tpu_custom_call" | custom-call | flops 1073741824 | bytes 6291456 | tf_op jit(solution)/shard_map/pallas_call | solution.py:343
  51.7 2.4 %collective-permute-start.5 = (f32[4,128,128]{2,1,0:T(8,128)S(1)}, f32[4,128,128]{2,1,0:T(8,128)S(1)}, u32[]{:S(2)}, u32[]{:S(2)}) collective-permute-start(f32[4,128,128]{2,1,0:T(8,128)S(1)} %get-tuple-element.26), channel_id=1, source_target_pairs={{0,4},{4,0},{1,5},{5,1},{2,6},{6,2},{3,7},{7,3},{8,12},{12,8},{9,1... | collective-permute-start | bytes 786440 | tf_op jit(solution)/shard_map/ppermute | solution.py:441
  54.1 1.1 %collective-permute-done.5 = f32[4,128,128]{2,1,0:T(8,128)S(1)} collective-permute-done((f32[4,128,128]{2,1,0:T(8,128)S(1)}, f32[4,128,128]{2,1,0:T(8,128)S(1)}, u32[]{:S(2)}, u32[]{:S(2)}) %collective-permute-start.5) | collective-permute-done | bytes 262176 | tf_op jit(solution)/shard_map/ppermute | solution.py:441
  55.3 9.4 %all_to_all.15 = f32[4,128,128]{2,1,0:T(8,128)S(1)} all-to-all(f32[4,128,128]{2,1,0:T(8,128)S(1)} %add.23), channel_id=1, replica_groups=mesh['z'=8,'y'=8,'core'=2,'snap'=4] {'snap'}, dimensions={0} | all-to-all | bytes 524288 | tf_op jit(solution)/shard_map/all_to_all | solution.py:442
  64.7 0.1 reshape.16
  64.8 0.1 copy.12
  64.9 0.2 reshape.17
  65.1 0.1 fusion.8
  65.2 0.1 stack_reshape.3
  65.3 0.1 pad_maximum_fusion
  65.3 27.4 %all_to_all.16.sums_ref = f32[64,2,128]{2,1,0:T(2,128)S(1)} all-to-all(f32[64,2,128]{2,1,0:T(2,128)S(1)} %pad_maximum_fusion), channel_id=1, replica_groups=mesh['z'=8,'y'=8,'core'=2,'snap'=4] {'z','y'}, dimensions={0} | all-to-all | bytes 131072 | tf_op jit(solution)/shard_map/all_to_all | solution.py:447
  92.7 0.7 shard_map.100
  (27 shorter events, 0.1 us)
Async XLA Ops:
  0.6 22.8 %copy-start = (s32[16]{0:T(128)S(1)}, s32[16]{0:T(128)}, u32[]{:S(2)}) copy-start(s32[16]{0:T(128)} %param.14) | copy-start | bytes 196
  4.0 5.0 %copy-start.10 = (f32[64]{0:T(128)S(1)}, f32[64]{0:T(128)}, u32[]{:S(2)}) copy-start(f32[64]{0:T(128)} %param.12) | copy-start | bytes 772
  4.0 5.0 %copy-start.6 = (f32[256,64]{0,1:T(8,128)S(1)}, f32[256,64]{0,1:T(8,128)}, u32[]{:S(2)}) copy-start(f32[256,64]{0,1:T(8,128)} %param.11) | copy-start | bytes 196612
  4.0 5.0 %copy-start.7 = (f32[256,64]{0,1:T(8,128)S(1)}, f32[256,64]{0,1:T(8,128)}, u32[]{:S(2)}) copy-start(f32[256,64]{0,1:T(8,128)} %param.10) | copy-start | bytes 196612
  4.1 5.2 %copy-start.1 = (bf16[4,24,64,128]{3,2,1,0:T(8,128)(2,1)S(1)}, bf16[4,24,64,128]{3,2,1,0:T(8,128)(2,1)}, u32[]{:S(2)}) copy-start(bf16[4,24,64,128]{3,2,1,0:T(8,128)(2,1)} %shard_map.95.ready_ref) | copy-start | bytes 4718596
  4.1 20.1 %all-to-all-start = ((bf16[4,24,64,128]{3,2,1,0:T(8,128)(2,1)}), bf16[4,24,64,128]{3,2,1,0:T(8,128)(2,1)S(1)}, u32[]{:S(2)}, u32[]{:S(2)}) async-start(bf16[4,24,64,128]{3,2,1,0:T(8,128)(2,1)} %shard_map.95.ready_ref), calls=%async_computation | async-start | bytes 3145728 | tf_op jit(solution)/shard_map/all_to_all | solution.py:383
  9.2 1.4 %copy-start.2 = (bf16[64,3,4,8,128]{4,3,2,1,0:T(8,128)(2,1)S(1)}, bf16[64,3,4,8,128]{4,3,2,1,0:T(8,128)(2,1)}, u32[]{:S(2)}) copy-start(bf16[64,3,4,8,128]{4,3,2,1,0:T(8,128)(2,1)} %snaps_ref.3) | copy-start | bytes 4718596
  10.6 12.8 %copy-start.9 = (s32[16]{0:T(128)S(1)}, s32[16]{0:T(128)}, u32[]{:S(2)}) copy-start(s32[16]{0:T(128)} %constant.53) | copy-start | bytes 196
  13.9 30.8 %collective-permute-start = (bf16[26,64,128]{2,1,0:T(8,128)(2,1)}, bf16[26,64,128]{2,1,0:T(8,128)(2,1)S(1)}, u32[]{:S(2)}, u32[]{:S(2)}) collective-permute-start(bf16[26,64,128]{2,1,0:T(8,128)(2,1)} %get-tuple-element.17), channel_id=1, source_target_pairs={{0,3},{1,0},{2,1},{3,2},{4,7},{5,4},{6,5},{7,6},{8,11},{9,8},{10,9... | collective-permute-start | bytes 1277960 | tf_op jit(solution)/shard_map/ppermute | solution.py:402
  18.5 26.2 %collective-permute-start.1 = (bf16[26,64,128]{2,1,0:T(8,128)(2,1)}, bf16[26,64,128]{2,1,0:T(8,128)(2,1)S(1)}, u32[]{:S(2)}, u32[]{:S(2)}) collective-permute-start(bf16[26,64,128]{2,1,0:T(8,128)(2,1)} %get-tuple-element.18), channel_id=1, source_target_pairs={{0,2},{1,3},{2,0},{3,1},{4,6},{5,7},{6,4},{7,5},{8,10},{9,11},{10,... | collective-permute-start | bytes 1277960 | tf_op jit(solution)/shard_map/ppermute | solution.py:402
  21.0 27.5 %collective-permute-start.2 = (bf16[26,64,128]{2,1,0:T(8,128)(2,1)}, bf16[26,64,128]{2,1,0:T(8,128)(2,1)S(1)}, u32[]{:S(2)}, u32[]{:S(2)}) collective-permute-start(bf16[26,64,128]{2,1,0:T(8,128)(2,1)} %get-tuple-element.19), channel_id=1, source_target_pairs={{0,1},{1,2},{2,3},{3,0},{4,5},{5,6},{6,7},{7,4},{8,9},{9,10},{10,1... | collective-permute-start | bytes 1277960 | tf_op jit(solution)/shard_map/ppermute | solution.py:402
  23.5 25.0 %copy-start.3 = (bf16[26,64,128]{2,1,0:T(8,128)(2,1)S(1)}, bf16[26,64,128]{2,1,0:T(8,128)(2,1)}, u32[]{:S(2)}) copy-start(bf16[26,64,128]{2,1,0:T(8,128)(2,1)} %get-tuple-element.16.own_ref) | copy-start | bytes 1277956
  24.2 17.4 %copy-start.4 = (f32[16,4,8,128]{3,2,1,0:T(8,128)S(1)}, f32[16,4,8,128]{3,2,1,0:T(8,128)}, u32[]{:S(2)}) copy-start(f32[16,4,8,128]{3,2,1,0:T(8,128)} %coeff_ref.1) | copy-start | bytes 786436
  24.2 0.8 copy-start.5
  26.3 22.2 %collective-permute-start.3 = (bf16[6,64,128]{2,1,0:T(8,128)(2,1)S(1)}, bf16[6,64,128]{2,1,0:T(8,128)(2,1)S(1)}, u32[]{:S(2)}, u32[]{:S(2)}) collective-permute-start(bf16[6,64,128]{2,1,0:T(8,128)(2,1)S(1)} %get-tuple-element.23), channel_id=1, source_target_pairs={{0,4},{4,8},{8,12},{12,16},{16,20},{20,24},{24,28},{28,32},{32,36}... | collective-permute-start | bytes 294920 | tf_op jit(solution)/shard_map/ppermute | solution.py:422
  37.5 11.0 %collective-permute-start.4 = (bf16[6,64,128]{2,1,0:T(8,128)(2,1)S(1)}, bf16[6,64,128]{2,1,0:T(8,128)(2,1)S(1)}, u32[]{:S(2)}, u32[]{:S(2)}) collective-permute-start(bf16[6,64,128]{2,1,0:T(8,128)(2,1)S(1)} %get-tuple-element.24), channel_id=1, source_target_pairs={{4,0},{8,4},{12,8},{16,12},{20,16},{24,20},{28,24},{32,28},{36,32}... | collective-permute-start | bytes 294920 | tf_op jit(solution)/shard_map/ppermute | solution.py:423
  51.7 13.4 %copy-start.8 = (f32[16,16]{1,0:T(8,128)S(1)}, f32[16,16]{1,0:T(8,128)}, u32[]{:S(2)}) copy-start(f32[16,16]{1,0:T(8,128)} %get-tuple-element.27) | copy-start | bytes 3076
  51.7 3.6 %collective-permute-start.5 = (f32[4,128,128]{2,1,0:T(8,128)S(1)}, f32[4,128,128]{2,1,0:T(8,128)S(1)}, u32[]{:S(2)}, u32[]{:S(2)}) collective-permute-start(f32[4,128,128]{2,1,0:T(8,128)S(1)} %get-tuple-element.26), channel_id=1, source_target_pairs={{0,4},{4,0},{1,5},{5,1},{2,6},{6,2},{3,7},{7,3},{8,12},{12,8},{9,1... | collective-permute-start | bytes 786440 | tf_op jit(solution)/shard_map/ppermute | solution.py:441

commit v10 on v9

--- a/solution.py
+++ b/solution.py
@@ -225,9 +225,9 @@
 
 def products_kernel(
     scale,
+    far_ref,
     own_ref,
     next_ref,
-    far_ref,
     previous_ref,
     direct_ref,
     modes_hbm,
@@ -402,7 +402,8 @@
         lax.ppermute(piece, "snap", [(i, (i + n) % SNAP) for i in range(SNAP)])
         for n, piece in enumerate(others, 1)
     ]
-    adjoints = (own, *arrived[::-1])
+    previous, far, following = arrived
+    adjoints = (far, own, following, previous)
     modes, first, last = call(
         modes_kernel,
         (pltpu.HBM((tiles, R, NZ), jnp.float32), shape(6, R, NZ), shape(6, R, NZ)),

time: 94.7 us -> 94.7 us (level)
  starting transfers between devices: 32.2 us -> 33.3 us
  waiting for transfers between devices: 4.94 us -> 3.85 us
    ppermute x3, waiting for transfers between devices: 3.79 us -> 2.7 us  [shards(): lax.ppermute(piece, 'snap', [(i, (i + n) % SNAP) for i in range(SNAP)])]
where the time goes in v10:
time: 94.7 us; the launch traced here: 93.5 us
  blocking collectives  36.7 us (39%)
  starting transfers between devices  33.3 us (35%)
  Pallas kernels  14.9 us (16%)
  waiting for transfers between devices  3.85 us (4%)
  local copies, waits for them, and re-layouts  3.31 us (3%)
    all_to_all x1, blocking collectives, shards(): sums = lax.all_to_all(owned, ('z', 'y'), 0, 0, tiled=True)  27.4 us
    pallas_call x6, Pallas kernels, run(): pl.pallas_call(kernel, out_shape=out_shape, in_specs=[pl.BlockSpec(memory...  14.9 us
    ppermute x1, starting transfers between devices, shards(): before = lax.ppermute(last, SPACE, slabs)  10.6 us
    ppermute x3, starting transfers between devices, shards(): lax.ppermute(piece, 'snap', [(i, (i + n) % SNAP) for i in range(SNAP)])  10.1 us
    all_to_all x1, blocking collectives, shards(): near = lax.all_to_all(terms, 'snap', 0, 0, tiled=True).sum(axis=0)  9.36 us
    all_to_all x1, starting transfers between devices, shards(): direct = lax.all_to_all(ready, 'snap', 0, 0, tiled=True)  4.99 us
    ppermute x1, starting transfers between devices, shards(): after = lax.ppermute(first, SPACE, [(j, i) for i, j in slabs])  4.64 us
    ppermute x1, starting transfers between devices, shards(): terms = keep + lax.ppermute(send, 'core', [(0, 1), (1, 0)])  2.91 us
  transfers between devices with their start and end apart: 7, of which 2 were waited for; matrix products, arithmetic and copies ran while one was open for 1% of the time, Pallas kernels for 8%

profile of v10, /device:TPU:1, one launch (start us, length us, event | category | flops | bytes accessed | tf_op | source)
XLA Modules:
  0.0 93.5 jit_solution(14656221025417964050)
XLA Ops:
  0.6 0.0 copy-start
  0.6 3.4 %shard_map.95.ready_ref = bf16[4,24,64,128]{3,2,1,0:T(8,128)(2,1)} custom-call(bf16[64,3,4,8,128]{4,3,2,1,0:T(8,128)(2,1)} %snaps_ref.2), custom_call_target="tpu_custom_call" | custom-call | bytes 3145728 | tf_op jit(solution)/shard_map/pallas_call | solution.py:343
  4.0 0.0 copy-start.10
  4.0 0.0 copy-start.6
  4.1 5.0 %all-to-all-start = ((bf16[4,24,64,128]{3,2,1,0:T(8,128)(2,1)}), bf16[4,24,64,128]{3,2,1,0:T(8,128)(2,1)S(1)}, u32[]{:S(2)}, u32[]{:S(2)}) async-start(bf16[4,24,64,128]{3,2,1,0:T(8,128)(2,1)} %shard_map.95.ready_ref), calls=%async_computation | async-start | bytes 3145728 | tf_op jit(solution)/shard_map/all_to_all | solution.py:383
  9.1 0.1 fusion.4
  9.2 0.0 copy-start.2
  9.2 1.4 %copy-done.2 = bf16[64,3,4,8,128]{4,3,2,1,0:T(8,128)(2,1)S(1)} copy-done((bf16[64,3,4,8,128]{4,3,2,1,0:T(8,128)(2,1)S(1)}, bf16[64,3,4,8,128]{4,3,2,1,0:T(8,128)(2,1)}, u32[]{:S(2)}) %copy-start.2) | copy-done | bytes 1572888
  10.6 3.2 %shard_map.96 = (bf16[26,64,128]{2,1,0:T(8,128)(2,1)}, bf16[26,64,128]{2,1,0:T(8,128)(2,1)}, bf16[26,64,128]{2,1,0:T(8,128)(2,1)}, bf16[26,64,128]{2,1,0:T(8,128)(2,1)}, bf16[64,256]{1,0:T(8,128)(2,1)}) custom-call(s32[1]{0:T(128)} %bitcast.snap_ref, bf16[64,3,4,8,128]{4,3,2,1,0:T(8,128)(2,1)S(1)} %copy-done.2, bf16[4,24,64,128]{3,2,1,0:T(8,128)(2,1)S(1)} %copy-done.1, ...), custom_call_target="tpu_custom_call" | custom-call | bytes 3145728 | tf_op jit(solution)/shard_map/pallas_call | solution.py:343
  13.9 4.9 %collective-permute-start = (bf16[26,64,128]{2,1,0:T(8,128)(2,1)}, bf16[26,64,128]{2,1,0:T(8,128)(2,1)S(1)}, u32[]{:S(2)}, u32[]{:S(2)}) collective-permute-start(bf16[26,64,128]{2,1,0:T(8,128)(2,1)} %get-tuple-element.16), channel_id=1, source_target_pairs={{0,2},{1,3},{2,0},{3,1},{4,6},{5,7},{6,4},{7,5},{8,10},{9,11},{10,... | collective-permute-start | bytes 1277960 | tf_op jit(solution)/shard_map/ppermute | solution.py:402
  18.8 2.8 %collective-permute-start.1 = (bf16[26,64,128]{2,1,0:T(8,128)(2,1)}, bf16[26,64,128]{2,1,0:T(8,128)(2,1)S(1)}, u32[]{:S(2)}, u32[]{:S(2)}) collective-permute-start(bf16[26,64,128]{2,1,0:T(8,128)(2,1)} %get-tuple-element.18), channel_id=1, source_target_pairs={{0,3},{1,0},{2,1},{3,2},{4,7},{5,4},{6,5},{7,6},{8,11},{9,8},{10,9... | collective-permute-start | bytes 1277960 | tf_op jit(solution)/shard_map/ppermute | solution.py:402
  21.6 2.5 %collective-permute-start.2 = (bf16[26,64,128]{2,1,0:T(8,128)(2,1)}, bf16[26,64,128]{2,1,0:T(8,128)(2,1)S(1)}, u32[]{:S(2)}, u32[]{:S(2)}) collective-permute-start(bf16[26,64,128]{2,1,0:T(8,128)(2,1)} %get-tuple-element.19), channel_id=1, source_target_pairs={{0,1},{1,2},{2,3},{3,0},{4,5},{5,6},{6,7},{7,4},{8,9},{9,10},{10,1... | collective-permute-start | bytes 1277960 | tf_op jit(solution)/shard_map/ppermute | solution.py:402
  24.1 0.7 gather_fusion
  24.8 0.8 copy-done.5
  25.6 1.3 %shard_map.97 = (f32[24,64,128]{2,1,0:T(8,128)}, bf16[6,64,128]{2,1,0:T(8,128)(2,1)S(1)}, bf16[6,64,128]{2,1,0:T(8,128)(2,1)S(1)}) custom-call(bf16[4,24,64,128]{3,2,1,0:T(8,128)(2,1)S(1)} %all-to-all-done.snaps_ref.direct_ref, bf16[64,256]{1,0:T(8,128)(2,1)S(1)} %copy-done.5), custom_call_target="tpu_custom_call" | custom-call | flops 100663296 | bytes 2097152 | tf_op jit(solution)/shard_map/pallas_call | solution.py:343
  26.9 10.6 %collective-permute-start.3 = (bf16[6,64,128]{2,1,0:T(8,128)(2,1)S(1)}, bf16[6,64,128]{2,1,0:T(8,128)(2,1)S(1)}, u32[]{:S(2)}, u32[]{:S(2)}) collective-permute-start(bf16[6,64,128]{2,1,0:T(8,128)(2,1)S(1)} %get-tuple-element.23), channel_id=1, source_target_pairs={{0,4},{4,8},{8,12},{12,16},{16,20},{20,24},{24,28},{28,32},{32,36}... | collective-permute-start | bytes 294920 | tf_op jit(solution)/shard_map/ppermute | solution.py:423
  37.5 4.6 %collective-permute-start.4 = (bf16[6,64,128]{2,1,0:T(8,128)(2,1)S(1)}, bf16[6,64,128]{2,1,0:T(8,128)(2,1)S(1)}, u32[]{:S(2)}, u32[]{:S(2)}) collective-permute-start(bf16[6,64,128]{2,1,0:T(8,128)(2,1)S(1)} %get-tuple-element.24), channel_id=1, source_target_pairs={{4,0},{8,4},{12,8},{16,12},{20,16},{24,20},{28,24},{32,28},{36,32}... | collective-permute-start | bytes 294920 | tf_op jit(solution)/shard_map/ppermute | solution.py:424
  42.1 0.1 fusion.3.turned_ref
  42.2 3.0 %shard_map.98 = (f32[6,64,128]{2,1,0:T(8,128)}, f32[16,16]{1,0:T(8,128)}) custom-call(s32[1]{0:T(128)} %bitcast.snap_ref, bf16[64,256]{1,0:T(8,128)(2,1)S(1)} %get-tuple-element.33.left_ref, bf16[64,256]{1,0:T(8,128)(2,1)S(1)} %fusion.3.turned_ref, f32[16,4,8,128]{3,2,1,0:T(8,128)S(1)} %copy-done.4, f32[16,16]{1,0:T(8,128)S(1)} %fusion.6.selector_ref, ...), custom_call_target="tpu_custom_call" | custom-call | bytes 1048576 | tf_op jit(solution)/shard_map/pallas_call | solution.py:343
  45.3 2.7 %collective-permute-done.2.previous_ref = bf16[26,64,128]{2,1,0:T(8,128)(2,1)S(1)} collective-permute-done((bf16[26,64,128]{2,1,0:T(8,128)(2,1)}, bf16[26,64,128]{2,1,0:T(8,128)(2,1)S(1)}, u32[]{:S(2)}, u32[]{:S(2)}) %collective-permute-start.2) | collective-permute-done | bytes 426016 | tf_op jit(solution)/shard_map/ppermute | solution.py:402
  48.0 3.2 %shard_map.99 = (f32[4,128,128]{2,1,0:T(8,128)S(1)}, f32[4,128,128]{2,1,0:T(8,128)S(1)}) custom-call(bf16[26,64,128]{2,1,0:T(8,128)(2,1)S(1)} %collective-permute-done.far_ref, bf16[26,64,128]{2,1,0:T(8,128)(2,1)S(1)} %copy-done.3, bf16[26,64,128]{2,1,0:T(8,128)(2,1)S(1)} %collective-permute-done.1.next_ref, ...), custom_call_target="tpu_custom_call" | custom-call | flops 1073741824 | bytes 6291456 | tf_op jit(solution)/shard_map/pallas_call | solution.py:343
  51.2 2.9 %collective-permute-start.5 = (f32[4,128,128]{2,1,0:T(8,128)S(1)}, f32[4,128,128]{2,1,0:T(8,128)S(1)}, u32[]{:S(2)}, u32[]{:S(2)}) collective-permute-start(f32[4,128,128]{2,1,0:T(8,128)S(1)} %get-tuple-element.26), channel_id=1, source_target_pairs={{0,4},{4,0},{1,5},{5,1},{2,6},{6,2},{3,7},{7,3},{8,12},{12,8},{9,1... | collective-permute-start | bytes 786440 | tf_op jit(solution)/shard_map/ppermute | solution.py:442
  54.1 1.1 %collective-permute-done.5 = f32[4,128,128]{2,1,0:T(8,128)S(1)} collective-permute-done((f32[4,128,128]{2,1,0:T(8,128)S(1)}, f32[4,128,128]{2,1,0:T(8,128)S(1)}, u32[]{:S(2)}, u32[]{:S(2)}) %collective-permute-start.5) | collective-permute-done | bytes 262176 | tf_op jit(solution)/shard_map/ppermute | solution.py:442
  55.3 9.4 %all_to_all.15 = f32[4,128,128]{2,1,0:T(8,128)S(1)} all-to-all(f32[4,128,128]{2,1,0:T(8,128)S(1)} %add.23), channel_id=1, replica_groups=mesh['z'=8,'y'=8,'core'=2,'snap'=4] {'snap'}, dimensions={0} | all-to-all | bytes 524288 | tf_op jit(solution)/shard_map/all_to_all | solution.py:443
  64.7 0.1 reshape.16
  64.8 0.1 copy.12
  64.9 0.2 reshape.17
  65.1 0.1 fusion.8
  65.2 0.1 stack_reshape.3
  65.3 0.1 pad_maximum_fusion
  65.3 27.4 %all_to_all.16.sums_ref = f32[64,2,128]{2,1,0:T(2,128)S(1)} all-to-all(f32[64,2,128]{2,1,0:T(2,128)S(1)} %pad_maximum_fusion), channel_id=1, replica_groups=mesh['z'=8,'y'=8,'core'=2,'snap'=4] {'z','y'}, dimensions={0} | all-to-all | bytes 131072 | tf_op jit(solution)/shard_map/all_to_all | solution.py:448
  92.7 0.7 shard_map.100
  (27 shorter events, 0.1 us)
Async XLA Ops:
  0.6 23.4 %copy-start = (s32[16]{0:T(128)S(1)}, s32[16]{0:T(128)}, u32[]{:S(2)}) copy-start(s32[16]{0:T(128)} %param.14) | copy-start | bytes 196
  4.0 5.0 %copy-start.10 = (f32[64]{0:T(128)S(1)}, f32[64]{0:T(128)}, u32[]{:S(2)}) copy-start(f32[64]{0:T(128)} %param.12) | copy-start | bytes 772
  4.0 5.0 %copy-start.6 = (f32[256,64]{0,1:T(8,128)S(1)}, f32[256,64]{0,1:T(8,128)}, u32[]{:S(2)}) copy-start(f32[256,64]{0,1:T(8,128)} %param.11) | copy-start | bytes 196612
  4.0 5.0 %copy-start.7 = (f32[256,64]{0,1:T(8,128)S(1)}, f32[256,64]{0,1:T(8,128)}, u32[]{:S(2)}) copy-start(f32[256,64]{0,1:T(8,128)} %param.10) | copy-start | bytes 196612
  4.1 5.2 %copy-start.1 = (bf16[4,24,64,128]{3,2,1,0:T(8,128)(2,1)S(1)}, bf16[4,24,64,128]{3,2,1,0:T(8,128)(2,1)}, u32[]{:S(2)}) copy-start(bf16[4,24,64,128]{3,2,1,0:T(8,128)(2,1)} %shard_map.95.ready_ref) | copy-start | bytes 4718596
  4.1 20.7 %all-to-all-start = ((bf16[4,24,64,128]{3,2,1,0:T(8,128)(2,1)}), bf16[4,24,64,128]{3,2,1,0:T(8,128)(2,1)S(1)}, u32[]{:S(2)}, u32[]{:S(2)}) async-start(bf16[4,24,64,128]{3,2,1,0:T(8,128)(2,1)} %shard_map.95.ready_ref), calls=%async_computation | async-start | bytes 3145728 | tf_op jit(solution)/shard_map/all_to_all | solution.py:383
  9.2 1.4 %copy-start.2 = (bf16[64,3,4,8,128]{4,3,2,1,0:T(8,128)(2,1)S(1)}, bf16[64,3,4,8,128]{4,3,2,1,0:T(8,128)(2,1)}, u32[]{:S(2)}) copy-start(bf16[64,3,4,8,128]{4,3,2,1,0:T(8,128)(2,1)} %snaps_ref.3) | copy-start | bytes 4718596
  10.6 13.4 %copy-start.9 = (s32[16]{0:T(128)S(1)}, s32[16]{0:T(128)}, u32[]{:S(2)}) copy-start(s32[16]{0:T(128)} %constant.53) | copy-start | bytes 196
  13.9 31.4 %collective-permute-start = (bf16[26,64,128]{2,1,0:T(8,128)(2,1)}, bf16[26,64,128]{2,1,0:T(8,128)(2,1)S(1)}, u32[]{:S(2)}, u32[]{:S(2)}) collective-permute-start(bf16[26,64,128]{2,1,0:T(8,128)(2,1)} %get-tuple-element.16), channel_id=1, source_target_pairs={{0,2},{1,3},{2,0},{3,1},{4,6},{5,7},{6,4},{7,5},{8,10},{9,11},{10,... | collective-permute-start | bytes 1277960 | tf_op jit(solution)/shard_map/ppermute | solution.py:402
  18.8 26.5 %collective-permute-start.1 = (bf16[26,64,128]{2,1,0:T(8,128)(2,1)}, bf16[26,64,128]{2,1,0:T(8,128)(2,1)S(1)}, u32[]{:S(2)}, u32[]{:S(2)}) collective-permute-start(bf16[26,64,128]{2,1,0:T(8,128)(2,1)} %get-tuple-element.18), channel_id=1, source_target_pairs={{0,3},{1,0},{2,1},{3,2},{4,7},{5,4},{6,5},{7,6},{8,11},{9,8},{10,9... | collective-permute-start | bytes 1277960 | tf_op jit(solution)/shard_map/ppermute | solution.py:402
  21.6 26.4 %collective-permute-start.2 = (bf16[26,64,128]{2,1,0:T(8,128)(2,1)}, bf16[26,64,128]{2,1,0:T(8,128)(2,1)S(1)}, u32[]{:S(2)}, u32[]{:S(2)}) collective-permute-start(bf16[26,64,128]{2,1,0:T(8,128)(2,1)} %get-tuple-element.19), channel_id=1, source_target_pairs={{0,1},{1,2},{2,3},{3,0},{4,5},{5,6},{6,7},{7,4},{8,9},{9,10},{10,1... | collective-permute-start | bytes 1277960 | tf_op jit(solution)/shard_map/ppermute | solution.py:402
  24.1 23.9 %copy-start.3 = (bf16[26,64,128]{2,1,0:T(8,128)(2,1)S(1)}, bf16[26,64,128]{2,1,0:T(8,128)(2,1)}, u32[]{:S(2)}) copy-start(bf16[26,64,128]{2,1,0:T(8,128)(2,1)} %get-tuple-element.17.own_ref) | copy-start | bytes 1277956
  24.8 17.5 %copy-start.4 = (f32[16,4,8,128]{3,2,1,0:T(8,128)S(1)}, f32[16,4,8,128]{3,2,1,0:T(8,128)}, u32[]{:S(2)}) copy-start(f32[16,4,8,128]{3,2,1,0:T(8,128)} %coeff_ref.1) | copy-start | bytes 786436
  24.8 0.8 copy-start.5
  26.9 21.1 %collective-permute-start.3 = (bf16[6,64,128]{2,1,0:T(8,128)(2,1)S(1)}, bf16[6,64,128]{2,1,0:T(8,128)(2,1)S(1)}, u32[]{:S(2)}, u32[]{:S(2)}) collective-permute-start(bf16[6,64,128]{2,1,0:T(8,128)(2,1)S(1)} %get-tuple-element.23), channel_id=1, source_target_pairs={{0,4},{4,8},{8,12},{12,16},{16,20},{20,24},{24,28},{28,32},{32,36}... | collective-permute-start | bytes 294920 | tf_op jit(solution)/shard_map/ppermute | solution.py:423
  37.5 10.5 %collective-permute-start.4 = (bf16[6,64,128]{2,1,0:T(8,128)(2,1)S(1)}, bf16[6,64,128]{2,1,0:T(8,128)(2,1)S(1)}, u32[]{:S(2)}, u32[]{:S(2)}) collective-permute-start(bf16[6,64,128]{2,1,0:T(8,128)(2,1)S(1)} %get-tuple-element.24), channel_id=1, source_target_pairs={{4,0},{8,4},{12,8},{16,12},{20,16},{24,20},{28,24},{32,28},{36,32}... | collective-permute-start | bytes 294920 | tf_op jit(solution)/shard_map/ppermute | solution.py:424
  51.2 13.8 %copy-start.8 = (f32[16,16]{1,0:T(8,128)S(1)}, f32[16,16]{1,0:T(8,128)}, u32[]{:S(2)}) copy-start(f32[16,16]{1,0:T(8,128)} %get-tuple-element.27) | copy-start | bytes 3076
  51.2 4.1 %collective-permute-start.5 = (f32[4,128,128]{2,1,0:T(8,128)S(1)}, f32[4,128,128]{2,1,0:T(8,128)S(1)}, u32[]{:S(2)}, u32[]{:S(2)}) collective-permute-start(f32[4,128,128]{2,1,0:T(8,128)S(1)} %get-tuple-element.26), channel_id=1, source_target_pairs={{0,4},{4,0},{1,5},{5,1},{2,6},{6,2},{3,7},{7,3},{8,12},{12,8},{9,1... | collective-permute-start | bytes 786440 | tf_op jit(solution)/shard_map/ppermute | solution.py:442
